TPU v7x, 32 devices: a whole 2x2x4 slice. The times are simulated.
32 devices in a mesh: dp: 16 (over z, y, core), seq: 2 (over x).
Axes of the slice: x: 2, y: 2, z: 4, core: 2. Of those that a mesh axis runs over, the one named last changes fastest.
Arguments:
- short_tokens: bfloat16 [128, 128, 768], P(('dp', 'seq')), may hold values from -6 to 6
- long_tokens: bfloat16 [32, 512, 768], P('dp', 'seq'), may hold values from -6 to 6
- short_len: int32 [128], P(('dp', 'seq')), may hold values from 1 to 128, as said below
- long_len: int32 [32], P('dp'), may hold values from 129 to 512, as said below
- short_pool: int32 [128, 128], P(('dp', 'seq')), may hold values 0 or 1
- long_pool: int32 [32, 512], P('dp', 'seq'), may hold values 0 or 1
- short_cot: bfloat16 [128, 128, 768], P(('dp', 'seq')), may hold values from -6 to 6
- long_cot: bfloat16 [32, 512, 768], P('dp', 'seq'), may hold values from -6 to 6
- short_pool_cot: float32 [128, 768], P(('dp', 'seq')), may hold values from -6 to 6
- long_pool_cot: float32 [32, 768], P('dp'), may hold values from -6 to 6
- w_qkv: bfloat16 [768, 2304], P(('dp', 'seq')), may hold values from -0.21875 to 0.21875
- w_out: bfloat16 [768, 768], P(('dp', 'seq')), may hold values from -0.625 to 0.625
- w_up: bfloat16 [768, 3072], P(('dp', 'seq')), may hold values from -0.21875 to 0.21875
- w_down: bfloat16 [3072, 768], P(('dp', 'seq')), may hold values from -0.109375 to 0.109375
- qv_bias: bfloat16 [768, 2], P(('dp', 'seq')), may hold values from -3 to 3
- out_bias: bfloat16 [768, 2], P(('dp', 'seq')), may hold values from -3 to 3
- up_bias: bfloat16 [3072], P(('dp', 'seq')), may hold values from -3 to 3
- norm_gain: bfloat16 [768, 2], P(('dp', 'seq')), may hold values from 0.25 to 1.75
- norm_shift: bfloat16 [768, 2], P(('dp', 'seq')), may hold values from -3 to 3
Outputs:
- short_out: bfloat16 [128, 128, 768], P(('dp', 'seq'))
- long_out: bfloat16 [32, 512, 768], P('dp', 'seq')
- short_pooled: float32 [128, 768], P(('dp', 'seq'))
- long_pooled: float32 [32, 768], P('dp')
- short_grad_in: float32 [128, 128, 768], P(('dp', 'seq'))
- long_grad_in: float32 [32, 512, 768], P('dp', 'seq')
- grad_w_qkv: float32 [768, 2304], P(('dp', 'seq'))
- grad_w_out: float32 [768, 768], P(('dp', 'seq'))
- grad_w_up: float32 [768, 3072], P(('dp', 'seq'))
- grad_w_down: float32 [3072, 768], P(('dp', 'seq'))
- grad_qv_bias: float32 [768, 2], P(('dp', 'seq'))
- grad_out_bias: float32 [768, 2], P(('dp', 'seq'))
- grad_up_bias: float32 [3072], P(('dp', 'seq'))
- grad_norm_gain: float32 [768, 2], P(('dp', 'seq'))
- grad_norm_shift: float32 [768, 2], P(('dp', 'seq'))
Inputs may be any that keep to these rules, and one draw needn't show every extreme that they name: `short_len`: among the 4 short sequences of each device, one has length exactly 128. `long_len`: among the 2 passages of each dp index, one has length exactly 512.
All inputs are finite; a program needn't handle non-finite values. No bound on the sum of `short_pool` or of `long_pool` on one device may be relied on, other than what follows from the above.
Results may differ from a plain program's by a relative error of at most 0.013.
Values may be sent and summed in bfloat16 or wider, within the bound.
A program may use at most 256 MiB of HBM per device.

v0:
```python
import math

import jax
import jax.numpy as jnp
from jax import lax
from jax.sharding import PartitionSpec as P

HEADS = 12


EPS = 1e-12


def layer_norm(row_data, gain_vec, shift_vec):
    center = row_data - jnp.mean(row_data, axis=-1, keepdims=True)
    spread = jnp.mean(center * center, axis=-1, keepdims=True)
    return center * lax.rsqrt(spread + EPS) * gain_vec + shift_vec


def exact_gelu(inner_act):
    return jax.nn.gelu(inner_act, approximate=False)


def outer_sum(left_rows, right_rows):
    return lax.dot_general(
        left_rows, right_rows, (((0,), (0,)), ((), ())), preferred_element_type=jnp.float32
    )


def times_transposed(left_rows, matrix):
    return lax.dot_general(
        left_rows, matrix, (((1,), (1,)), ((), ())), preferred_element_type=jnp.float32
    )


def masked_scores(queries, keys_all, key_live, score_scale):
    scores = (
        jnp.einsum("bqhe,bkhe->bhqk", queries, keys_all, preferred_element_type=jnp.float32)
        * score_scale
    )
    return jnp.where(key_live[:, None, None, :], scores, -1e30)


def attend_forward(pieces, score_scale):
    queries, keys_all, values, key_live = pieces
    scores = masked_scores(queries, keys_all, key_live, score_scale)
    highest = jnp.max(scores, axis=-1, keepdims=True)
    exponent = jnp.exp(scores - highest)
    totals = jnp.sum(exponent, axis=-1, keepdims=True)
    soft_probs = (exponent / totals).astype(jnp.bfloat16)
    mixed_heads = jnp.einsum(
        "bhqk,bkhe->bqhe", soft_probs, values, preferred_element_type=jnp.float32
    )
    return (mixed_heads.astype(jnp.bfloat16), (highest + jnp.log(totals))[..., 0])


def attend_backward(pieces, score_scale):
    queries, keys_all, values, key_live, grad_mixed, log_total = pieces
    scores = masked_scores(queries, keys_all, key_live, score_scale)
    soft_probs = jnp.exp(scores - log_total[..., None])
    grad_probs = jnp.einsum(
        "bqhe,bkhe->bhqk", grad_mixed, values, preferred_element_type=jnp.float32
    )
    grad_values = jnp.einsum(
        "bhqk,bqhe->bkhe",
        soft_probs.astype(jnp.bfloat16),
        grad_mixed,
        preferred_element_type=jnp.float32,
    )
    center = jnp.sum(soft_probs * grad_probs, axis=-1, keepdims=True)
    grad_scores = (soft_probs * (grad_probs - center)).astype(jnp.bfloat16)
    grad_queries = (
        jnp.einsum("bhqk,bkhe->bqhe", grad_scores, keys_all, preferred_element_type=jnp.float32)
        * score_scale
    )
    grad_keys = (
        jnp.einsum("bhqk,bqhe->bkhe", grad_scores, queries, preferred_element_type=jnp.float32)
        * score_scale
    )
    return (grad_queries, grad_keys, grad_values)


def by_blocks(function, per_block, arrays):
    blocks = arrays[0].shape[0] // per_block
    stacked = tuple((member.reshape((blocks, per_block) + member.shape[1:]) for member in arrays))
    results = lax.map(function, stacked)
    return jax.tree.map(
        lambda member: member.reshape((blocks * per_block,) + member.shape[2:]), results
    )


def shards(
    short_tokens,
    long_tokens,
    short_len,
    long_len,
    short_pool,
    long_pool,
    short_cot,
    long_cot,
    short_pool_cot,
    long_pool_cot,
    w_qkv,
    w_out,
    w_up,
    w_down,
    qv_bias,
    out_bias,
    up_bias,
    norm_gain,
    norm_shift,
):
    gathered = (
        lax.all_gather(w_qkv, ("dp", "seq"), axis=0, tiled=True),
        lax.all_gather(w_out, ("dp", "seq"), axis=0, tiled=True),
        lax.all_gather(w_up, ("dp", "seq"), axis=0, tiled=True),
        lax.all_gather(w_down, ("dp", "seq"), axis=0, tiled=True),
        lax.all_gather(qv_bias, ("dp", "seq"), axis=0, tiled=True),
        lax.all_gather(out_bias, ("dp", "seq"), axis=0, tiled=True),
        lax.all_gather(up_bias, ("dp", "seq"), axis=0, tiled=True),
        lax.all_gather(norm_gain, ("dp", "seq"), axis=0, tiled=True),
        lax.all_gather(norm_shift, ("dp", "seq"), axis=0, tiled=True),
    )
    qkv_matrix, out_matrix, up_matrix, down_matrix, qv_vec, out_vec, up_vec, gains, shifts = (
        gathered
    )
    gains = gains.astype(jnp.float32)
    shifts = shifts.astype(jnp.float32)
    short_count, short_cap, model_width = short_tokens.shape
    long_count, long_half = (long_tokens.shape[0], long_tokens.shape[1])
    head_count = HEADS
    head_dim = model_width // head_count
    score_scale = 1.0 / math.sqrt(head_dim)
    short_rows = short_count * short_cap
    long_rows = long_count * long_half
    short_place = jnp.arange(short_cap, dtype=jnp.int32)
    short_live = short_place[None, :] < short_len[:, None]
    long_place = lax.axis_index("seq") * long_half + jnp.arange(long_half, dtype=jnp.int32)
    long_live = long_place[None, :] < long_len[:, None]
    short_weight = (short_live & ((short_pool > 0) | (short_place[None, :] == 0))).astype(
        jnp.float32
    )
    long_weight = (long_live & ((long_pool > 0) | (long_place[None, :] == 0))).astype(jnp.float32)
    row_live = jnp.concatenate([short_live.reshape(-1), long_live.reshape(-1)]).astype(jnp.float32)
    inputs = jnp.concatenate(
        [
            short_tokens.reshape(short_rows, model_width),
            long_tokens.reshape(long_rows, model_width),
        ],
        axis=0,
    )
    joined = jnp.dot(inputs, qkv_matrix, preferred_element_type=jnp.float32)
    queries = (joined[:, :model_width] + qv_vec[:, 0]).astype(jnp.bfloat16)
    keys_all = joined[:, model_width : 2 * model_width].astype(jnp.bfloat16)
    values = (joined[:, 2 * model_width :] + qv_vec[:, 1]).astype(jnp.bfloat16)
    short_shape = (short_count, short_cap, head_count, head_dim)
    long_shape = (long_count, long_half, head_count, head_dim)
    short_q = queries[:short_rows].reshape(short_shape)
    short_k = keys_all[:short_rows].reshape(short_shape)
    short_v = values[:short_rows].reshape(short_shape)
    long_q = queries[short_rows:].reshape(long_shape)
    long_k = keys_all[short_rows:].reshape(long_count, long_half, model_width)
    long_v = values[short_rows:].reshape(long_count, long_half, model_width)
    short_block = math.gcd(short_count, max(1, 512 // short_cap))
    long_block = math.gcd(long_count, max(1, 512 // long_half))

    def forward_blocks(pieces):
        return attend_forward(pieces, score_scale)

    def backward_blocks(pieces):
        return attend_backward(pieces, score_scale)

    short_mixed, short_logsum = by_blocks(
        forward_blocks, short_block, (short_q, short_k, short_v, short_live)
    )
    gathered_k, gathered_v = (
        lax.all_gather(long_k, "seq", axis=1, tiled=True),
        lax.all_gather(long_v, "seq", axis=1, tiled=True),
    )
    full_len = gathered_k.shape[1]
    full_shape = (long_count, full_len, head_count, head_dim)
    long_key_live = jnp.arange(full_len, dtype=jnp.int32)[None, :] < long_len[:, None]
    long_mixed, long_logsum = by_blocks(
        forward_blocks,
        long_block,
        (long_q, gathered_k.reshape(full_shape), gathered_v.reshape(full_shape), long_key_live),
    )
    mixed_heads = jnp.concatenate(
        [short_mixed.reshape(short_rows, model_width), long_mixed.reshape(long_rows, model_width)],
        axis=0,
    )
    attn_out = jnp.dot(mixed_heads, out_matrix, preferred_element_type=jnp.float32) + out_vec[:, 0]
    first_in = inputs.astype(jnp.float32) + attn_out
    first_norm = layer_norm(first_in, gains[:, 0], shifts[:, 0])
    first_low = first_norm.astype(jnp.bfloat16)
    inner_act = jnp.dot(first_low, up_matrix, preferred_element_type=jnp.float32) + up_vec
    activated = exact_gelu(inner_act).astype(jnp.bfloat16)
    branch = jnp.dot(activated, down_matrix, preferred_element_type=jnp.float32) + out_vec[:, 1]
    second_in = first_norm + branch
    final_norm = layer_norm(second_in, gains[:, 1], shifts[:, 1]) * row_live[:, None]
    short_final = final_norm[:short_rows].reshape(short_count, short_cap, model_width)
    long_final = final_norm[short_rows:].reshape(long_count, long_half, model_width)
    short_total = jnp.sum(short_weight, axis=1)
    short_pooled = jnp.sum(short_final * short_weight[..., None], axis=1) / short_total[:, None]
    long_partial = jnp.sum(long_final * long_weight[..., None], axis=1)
    long_sum, long_total = lax.psum((long_partial, jnp.sum(long_weight, axis=1)), "seq")
    long_pooled = long_sum / long_total[:, None]
    grad_short = (
        short_cot.astype(jnp.float32) * short_live[..., None]
        + short_weight[..., None] * short_pool_cot[:, None, :] / short_total[:, None, None]
    )
    grad_long = (
        long_cot.astype(jnp.float32) * long_live[..., None]
        + long_weight[..., None] * long_pool_cot[:, None, :] / long_total[:, None, None]
    )
    grad_top = jnp.concatenate(
        [grad_short.reshape(short_rows, model_width), grad_long.reshape(long_rows, model_width)],
        axis=0,
    )
    _, second_back = jax.vjp(layer_norm, second_in, gains[:, 1], shifts[:, 1])
    grad_second, grad_gain_two, grad_shift_two = second_back(grad_top)
    grad_branch = grad_second.astype(jnp.bfloat16)
    grad_down = outer_sum(activated, grad_branch)
    grad_bias_two = jnp.sum(grad_branch.astype(jnp.float32), axis=0)
    grad_acted = times_transposed(grad_branch, down_matrix)
    _, gelu_back = jax.vjp(exact_gelu, inner_act)
    grad_inner = gelu_back(grad_acted)[0].astype(jnp.bfloat16)
    grad_up = outer_sum(first_low, grad_inner)
    grad_up_bias = jnp.sum(grad_inner.astype(jnp.float32), axis=0)
    grad_first = grad_second + times_transposed(grad_inner, up_matrix)
    _, first_back = jax.vjp(layer_norm, first_in, gains[:, 0], shifts[:, 0])
    grad_first_in, grad_gain_one, grad_shift_one = first_back(grad_first)
    grad_attn = grad_first_in.astype(jnp.bfloat16)
    grad_out = outer_sum(mixed_heads, grad_attn)
    grad_bias_one = jnp.sum(grad_attn.astype(jnp.float32), axis=0)
    grad_mixed = times_transposed(grad_attn, out_matrix).astype(jnp.bfloat16)
    short_dq, short_dk, short_dv = by_blocks(
        backward_blocks,
        short_block,
        (
            short_q,
            short_k,
            short_v,
            short_live,
            grad_mixed[:short_rows].reshape(short_shape),
            short_logsum,
        ),
    )
    again_k, again_v = (gathered_k, gathered_v)
    long_dq, long_dk, long_dv = by_blocks(
        backward_blocks,
        long_block,
        (
            long_q,
            again_k.reshape(full_shape),
            again_v.reshape(full_shape),
            long_key_live,
            grad_mixed[short_rows:].reshape(long_shape),
            long_logsum,
        ),
    )
    own_dk, own_dv = (
        lax.psum_scatter(
            long_dk.reshape(long_count, full_len, model_width).astype(jnp.bfloat16),
            "seq",
            scatter_dimension=1,
            tiled=True,
        ).astype(jnp.float32),
        lax.psum_scatter(
            long_dv.reshape(long_count, full_len, model_width).astype(jnp.bfloat16),
            "seq",
            scatter_dimension=1,
            tiled=True,
        ).astype(jnp.float32),
    )
    grad_queries = jnp.concatenate(
        [short_dq.reshape(short_rows, model_width), long_dq.reshape(long_rows, model_width)], axis=0
    ).astype(jnp.bfloat16)
    grad_keys = jnp.concatenate(
        [short_dk.reshape(short_rows, model_width), own_dk.reshape(long_rows, model_width)], axis=0
    ).astype(jnp.bfloat16)
    grad_values = jnp.concatenate(
        [short_dv.reshape(short_rows, model_width), own_dv.reshape(long_rows, model_width)], axis=0
    ).astype(jnp.bfloat16)
    grad_joined = jnp.concatenate([grad_queries, grad_keys, grad_values], axis=1)
    grad_qkv = outer_sum(inputs, grad_joined)
    grad_qv = jnp.stack(
        [
            jnp.sum(grad_queries.astype(jnp.float32), axis=0),
            jnp.sum(grad_values.astype(jnp.float32), axis=0),
        ],
        axis=1,
    )
    grad_inputs = grad_first_in + times_transposed(grad_joined, qkv_matrix)
    grad_out_vec = jnp.stack([grad_bias_one, grad_bias_two], axis=1)
    grad_gains = jnp.stack([grad_gain_one, grad_gain_two], axis=1)
    grad_shifts = jnp.stack([grad_shift_one, grad_shift_two], axis=1)
    shard_grads = (
        lax.psum_scatter(grad_qkv, ("dp", "seq"), scatter_dimension=0, tiled=True),
        lax.psum_scatter(grad_out, ("dp", "seq"), scatter_dimension=0, tiled=True),
        lax.psum_scatter(grad_up, ("dp", "seq"), scatter_dimension=0, tiled=True),
        lax.psum_scatter(grad_down, ("dp", "seq"), scatter_dimension=0, tiled=True),
        lax.psum_scatter(grad_qv, ("dp", "seq"), scatter_dimension=0, tiled=True),
        lax.psum_scatter(grad_out_vec, ("dp", "seq"), scatter_dimension=0, tiled=True),
        lax.psum_scatter(grad_up_bias, ("dp", "seq"), scatter_dimension=0, tiled=True),
        lax.psum_scatter(grad_gains, ("dp", "seq"), scatter_dimension=0, tiled=True),
        lax.psum_scatter(grad_shifts, ("dp", "seq"), scatter_dimension=0, tiled=True),
    )
    short_out = short_final.astype(jnp.bfloat16)
    long_out = long_final.astype(jnp.bfloat16)
    short_grad_in = grad_inputs[:short_rows].reshape(short_count, short_cap, model_width)
    long_grad_in = grad_inputs[short_rows:].reshape(long_count, long_half, model_width)
    return (
        short_out,
        long_out,
        short_pooled,
        long_pooled,
        short_grad_in,
        long_grad_in,
        shard_grads[0],
        shard_grads[1],
        shard_grads[2],
        shard_grads[3],
        shard_grads[4],
        shard_grads[5],
        shard_grads[6],
        shard_grads[7],
        shard_grads[8],
    )


def solution(mesh):
    in_specs = (
        P(("dp", "seq"), None, None),
        P("dp", "seq", None),
        P(("dp", "seq")),
        P("dp"),
        P(("dp", "seq"), None),
        P("dp", "seq"),
        P(("dp", "seq"), None, None),
        P("dp", "seq", None),
        P(("dp", "seq"), None),
        P("dp", None),
        P(("dp", "seq"), None),
        P(("dp", "seq"), None),
        P(("dp", "seq"), None),
        P(("dp", "seq"), None),
        P(("dp", "seq"), None),
        P(("dp", "seq"), None),
        P(("dp", "seq")),
        P(("dp", "seq"), None),
        P(("dp", "seq"), None),
    )
    out_specs = (
        P(("dp", "seq"), None, None),
        P("dp", "seq", None),
        P(("dp", "seq"), None),
        P("dp", None),
        P(("dp", "seq"), None, None),
        P("dp", "seq", None),
        P(("dp", "seq"), None),
        P(("dp", "seq"), None),
        P(("dp", "seq"), None),
        P(("dp", "seq"), None),
        P(("dp", "seq"), None),
        P(("dp", "seq"), None),
        P(("dp", "seq")),
        P(("dp", "seq"), None),
        P(("dp", "seq"), None),
    )
    return jax.shard_map(shards, mesh=mesh, in_specs=in_specs, out_specs=out_specs, check_vma=False)
```

profile of v0, /device:TPU:0, one launch (start us, length us, event | category | flops | bytes accessed | tf_op | source)
XLA Modules:
  0.0 1115.1 jit_solution(3266507481454749521)
XLA Ops:
  8.0 65.9 %all-gather.11.cloned.1.call-done = bf16[768,2304]{1,0:T(8,128)(2,1)} async-done(((bf16[24,2304]{1,0:T(8,128)(2,1)}), bf16[768,2304]{1,0:T(8,128)(2,1)}) %all-gather.11.cloned.1.call-update) | async-done | bytes 3538960 | tf_op jit(solution)/shard_map/all_gather | solution.py:114
  73.8 9.9 fusion.87
  85.1 65.8 %all-gather = bf16[32,24,2]{1,2,0:T(2,128)(2,1)S(1)} all-gather(bf16[1,24,2]{1,2,0:T(2,128)(2,1)S(1)} %bitcast.163), channel_id=1, replica_groups=mesh['dp'=16,'seq'=2] {'dp','seq'}, dimensions={0}, use_global_device_ids=true | all-gather | bytes 3168 | tf_op jit(solution)/shard_map/all_gather | solution.py:118
  151.0 3.4 fusion.14
  158.0 37.3 %all-reduce = bf16[3072]{0:T(1024)(128)(2,1)S(1)} all-reduce(bf16[3072]{0:T(1024)(128)(2,1)S(1)} %dynamic-update-slice), channel_id=1, replica_groups=mesh['dp'=16,'seq'=2] {'dp','seq'}, use_global_device_ids=true, to_apply=%add | all-reduce | flops 3072 | bytes 12288
  195.2 65.5 %all-gather.1 = bf16[32,24,2]{1,2,0:T(2,128)(2,1)S(1)} all-gather(bf16[1,24,2]{1,2,0:T(2,128)(2,1)S(1)} %bitcast.164), channel_id=1, replica_groups=mesh['dp'=16,'seq'=2] {'dp','seq'}, dimensions={0}, use_global_device_ids=true | all-gather | bytes 3168 | tf_op jit(solution)/shard_map/all_gather | solution.py:119
  260.8 63.2 %all-gather.2 = bf16[32,24,2]{1,2,0:T(2,128)(2,1)S(1)} all-gather(bf16[1,24,2]{1,2,0:T(2,128)(2,1)S(1)} %bitcast.165), channel_id=1, replica_groups=mesh['dp'=16,'seq'=2] {'dp','seq'}, dimensions={0}, use_global_device_ids=true | all-gather | bytes 3168 | tf_op jit(solution)/shard_map/all_gather | solution.py:121
  324.1 65.3 %all-gather.3 = bf16[32,24,2]{1,2,0:T(2,128)(2,1)S(1)} all-gather(bf16[1,24,2]{1,2,0:T(2,128)(2,1)S(1)} %bitcast.166), channel_id=1, replica_groups=mesh['dp'=16,'seq'=2] {'dp','seq'}, dimensions={0}, use_global_device_ids=true | all-gather | bytes 3168 | tf_op jit(solution)/shard_map/all_gather | solution.py:122
  405.3 4.6 copy-done
  409.9 3.2 fusion.6
  414.9 7.4 fusion.37
  424.3 3.8 fusion.89
  430.2 36.2 %multiply_convert_fusion.1 = (bf16[1024,3072]{1,0:T(8,128)(2,1)}, f32[1024,3072]{1,0:T(8,128)}, f32[1024,3072]{1,0:T(8,128)}) fusion(f32[3072]{0:T(1024)S(1)} %convert_element_type.212, bf16[768,3072]{1,0:T(8,128)(2,1)} %all-gather.19.cloned.1.call-done, f32[1024,768]{1,0:T(8,128)S(1)} %get-tuple-element.182, f32[768]{0:T(1024)S(1)} %get-tuple-element.105, ...), kind=kOutput, calls=%fused_computation.7 | convolution fusion | flops 5043388416 | bytes 39348224 | tf_op jit(solution)/shard_map/dot_general | solution.py:196
  466.4 9.3 fusion.90
  478.7 5.0 all-reduce.7
  492.9 18.4 %convert_reduce_fusion = (f32[3072]{0:T(1024)S(1)}, bf16[1024,3072]{1,0:T(8,128)(2,1)}) fusion(f32[1024,3072]{1,0:T(8,128)} %get-tuple-element.156, bf16[1024,768]{1,0:T(8,128)(2,1)} %get-tuple-element.144, bf16[3072,768]{1,0:T(8,128)(2,1)} %all-gather.21.cloned.1.call-done, f32[1024,3072]{1,0:T(8,128)} %get-tuple-element.183, ...), kind=kOutput, calls=%fused_computation.2 | convolution fusion | flops 4885312512 | bytes 37773312 | tf_op jit(solution)/shard_map/dot_general | solution.py:31
  511.3 9.6 multiply_reduce_fusion.2
  529.6 3.1 squeeze.78
  532.7 8.7 fusion.18
  544.0 8.7 multiply_reduce_fusion
  552.8 7.0 multiply_convert_fusion
  559.8 2.9 multiply_convert_fusion.2
  565.6 4.7 fusion.91
  570.4 11.1 fusion.69
  582.9 10.2 fusion.92
  617.5 15.6 %fusion.53 = f32[768,2304]{1,0:T(8,128)} fusion(bf16[512,768]{1,0:T(8,128)(2,1)} %bitcast.169, bf16[512,768]{1,0:T(8,128)(2,1)} %bitcast.172, bf16[512,768]{0,1:T(8,128)(2,1)S(1)} %copy.167, bf16[512,768]{0,1:T(8,128)(2,1)S(1)} %bitcast.143, bf16[512,768]{0,1:T(8,128)(2,1)} %copy.161, bf16[512,768]{0,1:T(8,128)(2,1)} %bitcast.158, ...), kind=kOutput, calls=%fused_computation.107 | convolution fusion | flops 3650617344 | bytes 13369344 | tf_op jit(solution)/shard_map/dot_general | solution.py:25
  638.2 38.2 %all-reduce.6 = (f32[768,2]{0,1:T(2,128)S(1)}, f32[768,2]{0,1:T(2,128)S(1)}, f32[3072]{0:T(1024)S(1)}, f32[768,2]{0,1:T(2,128)S(1)}, f32[768,2]{0,1:T(2,128)S(1)}) all-reduce(f32[768,2]{0,1:T(2,128)S(1)} %pad_maximum_fusion.4, f32[768,2]{0,1:T(2,128)S(1)} %pad_maximum_fusion.5, ...), channel_id=8, replica_groups=mesh['dp'=16,'seq'=2] {'dp','seq'}, use_global_device_ids=true, to_apply=%region_28.29.clone | all-reduce | flops 9216 | bytes 73728
  679.5 8.5 add_add_fusion.4
  689.9 10.0 reduce-scatter.17.cloned.1.call-done
  699.8 142.0 %reduce-scatter.19.cloned.1.call-done = f32[24,3072]{1,0:T(8,128)} async-done(((f32[768,3072]{1,0:T(8,128)}), f32[24,3072]{1,0:T(8,128)}) %reduce-scatter.19.cloned.1.call-update) | async-done | bytes 294928 | tf_op jit(solution)/shard_map/reduce_scatter | solution.py:301
  841.8 141.1 %reduce-scatter.21.cloned.1.call-done = f32[96,768]{1,0:T(8,128)} async-done(((f32[3072,768]{1,0:T(8,128)}), f32[96,768]{1,0:T(8,128)}) %reduce-scatter.21.cloned.1.call-update) | async-done | bytes 294928 | tf_op jit(solution)/shard_map/reduce_scatter | solution.py:302
  982.9 125.2 %reduce-scatter.15.cloned.1.call-done = f32[24,2304]{1,0:T(8,128)} async-done(((f32[768,2304]{1,0:T(8,128)}), f32[24,2304]{1,0:T(8,128)}) %reduce-scatter.15.cloned.1.call-update) | async-done | bytes 221200 | tf_op jit(solution)/shard_map/reduce_scatter | solution.py:299
  (247 shorter events, 89.2 us)
Async XLA Ops:
  7.2 66.7 %all-gather.11.cloned.1.call-start = ((), (), s32[]{:S(2)}) async-start(), calls=%async_computation.6 | async-start | bytes 3649536 | tf_op jit(solution)/shard_map/all_gather | solution.py:114
  7.9 393.2 %all-gather.15.cloned.1.call-start = ((), (), s32[]{:S(2)}) async-start(), calls=%async_computation.8 | async-start | bytes 2359296 | tf_op jit(solution)/shard_map/all_gather | solution.py:177
  85.0 328.1 %all-gather.13.cloned.1.call-start = ((), (), s32[]{:S(2)}) async-start(), calls=%async_computation.7 | async-start | bytes 2359296 | tf_op jit(solution)/shard_map/all_gather | solution.py:178
  154.5 40.8 %copy-start.43 = (bf16[24,2]{0,1:T(2,128)(2,1)S(1)}, bf16[24,2]{0,1:T(2,128)(2,1)}, u32[]{:S(2)}) copy-start(bf16[24,2]{0,1:T(2,128)(2,1)} %param.34) | copy-start | bytes 292
  154.5 106.4 %copy-start.44 = (bf16[24,2]{0,1:T(2,128)(2,1)S(1)}, bf16[24,2]{0,1:T(2,128)(2,1)}, u32[]{:S(2)}) copy-start(bf16[24,2]{0,1:T(2,128)(2,1)} %param.36) | copy-start | bytes 292
  154.5 169.6 %copy-start.45 = (bf16[24,2]{0,1:T(2,128)(2,1)S(1)}, bf16[24,2]{0,1:T(2,128)(2,1)}, u32[]{:S(2)}) copy-start(bf16[24,2]{0,1:T(2,128)(2,1)} %param.37) | copy-start | bytes 292
  154.5 235.4 %copy-start.40 = (s32[4,128]{1,0:T(4,128)S(1)}, s32[4,128]{1,0:T(4,128)}, u32[]{:S(2)}) copy-start(s32[4,128]{1,0:T(4,128)} %param.23) | copy-start | bytes 6148
  154.5 235.6 %copy-start.38 = (s32[2,256]{1,0:T(2,128)S(1)}, s32[2,256]{1,0:T(2,128)}, u32[]{:S(2)}) copy-start(s32[2,256]{1,0:T(2,128)} %param.24) | copy-start | bytes 6148
  155.6 268.7 %all-gather.17.cloned.1.call-start = ((), (), s32[]{:S(2)}) async-start(), calls=%async_computation.9 | async-start | bytes 1216512 | tf_op jit(solution)/shard_map/all_gather | solution.py:115
  156.2 274.0 %all-gather.19.cloned.1.call-start = ((), (), s32[]{:S(2)}) async-start(), calls=%async_computation.10 | async-start | bytes 4866048 | tf_op jit(solution)/shard_map/all_gather | solution.py:116
  156.8 309.6 %all-gather.21.cloned.1.call-start = ((), (), s32[]{:S(2)}) async-start(), calls=%async_computation.11 | async-start | bytes 4866048 | tf_op jit(solution)/shard_map/all_gather | solution.py:117
  157.4 455.6 %reduce-scatter.13.cloned.1.call-start = ((), (), s32[]{:S(2)}) async-start(), calls=%async_computation.13 | async-start | bytes 2359296 | tf_op jit(solution)/shard_map/reduce_scatter | solution.py:269
  157.6 257.4 %copy-start.32 = (pred[2,512]{1,0:T(4,128)(4,1)}, pred[2,512]{1,0:T(4,128)(4,1)S(1)}, u32[]{:S(2)}) copy-start(pred[2,512]{1,0:T(4,128)(4,1)S(1)} %iota_compare_fusion) | copy-start | bytes 3076
  393.2 9.8 copy-start.11
  414.9 7.5 copy-start.14
  428.1 38.3 %copy-start.4 = (f32[1024,768]{1,0:T(8,128)}, f32[1024,768]{1,0:T(8,128)S(1)}, u32[]{:S(2)}) copy-start(f32[1024,768]{1,0:T(8,128)S(1)} %get-tuple-element.182) | copy-start | bytes 9437188
  476.2 7.5 copy-start.37
  476.9 8.4 copy-start.36
  492.9 18.4 %copy-start.5 = (f32[1024,768]{1,0:T(8,128)S(1)}, f32[1024,768]{1,0:T(8,128)}, u32[]{:S(2)}) copy-start(f32[1024,768]{1,0:T(8,128)} %copy-done.4) | copy-start | bytes 9437188
  511.3 9.6 copy-start.35
  525.9 6.7 copy-start.27
  526.0 6.7 copy-start.33
  543.9 71.0 %reduce-scatter.11.cloned.1.call-start = ((), (), s32[]{:S(2)}) async-start(), calls=%async_computation.12 | async-start | bytes 2359296 | tf_op jit(solution)/shard_map/reduce_scatter | solution.py:263
  552.7 7.1 copy-start.12
  565.6 134.3 %reduce-scatter.17.cloned.1.call-start = ((), (), s32[]{:S(2)}) async-start(), calls=%async_computation.15 | async-start | bytes 2433024 | tf_op jit(solution)/shard_map/reduce_scatter | solution.py:300
  570.4 271.4 %reduce-scatter.19.cloned.1.call-start = ((), (), s32[]{:S(2)}) async-start(), calls=%async_computation.16 | async-start | bytes 9732096 | tf_op jit(solution)/shard_map/reduce_scatter | solution.py:301
  581.5 401.4 %reduce-scatter.21.cloned.1.call-start = ((), (), s32[]{:S(2)}) async-start(), calls=%async_computation.17 | async-start | bytes 9732096 | tf_op jit(solution)/shard_map/reduce_scatter | solution.py:302
  593.1 5.7 copy-start.3
  593.1 514.9 %reduce-scatter.15.cloned.1.call-start = ((), (), s32[]{:S(2)}) async-start(), calls=%async_computation.14 | async-start | bytes 7299072 | tf_op jit(solution)/shard_map/reduce_scatter | solution.py:299
  604.1 5.5 slice-start
  612.9 20.2 %copy-start.15 = (bf16[1024,768]{0,1:T(8,128)(2,1)}, bf16[1024,768]{0,1:T(8,128)(2,1)S(1)}, u32[]{:S(2)}) copy-start(bf16[1024,768]{0,1:T(8,128)(2,1)S(1)} %constant_dynamic-update-slice_fusion.1) | copy-start | bytes 4718596
  614.9 18.2 %copy-start.18 = (bf16[512,768]{0,1:T(8,128)(2,1)}, bf16[512,768]{0,1:T(8,128)(2,1)S(1)}, u32[]{:S(2)}) copy-start(bf16[512,768]{0,1:T(8,128)(2,1)S(1)} %copy.167) | copy-start | bytes 2359300
  (30 other events, 80.2 us)
Sparse Core Ops, SparseCore 0:
  10.9 62.8 all-gather.10
  85.2 26.0 all-gather.14
  155.7 23.7 all-gather.12
  182.3 53.7 all-gather.16
  238.8 62.5 all-gather.18
  304.2 62.4 all-gather.20
  544.1 21.9 reduce-scatter.12
  568.4 26.0 reduce-scatter.10
  600.4 99.3 reduce-scatter.16
  707.1 134.5 reduce-scatter.18
  848.3 134.6 reduce-scatter.20
  990.0 118.0 reduce-scatter.14
where the time goes:
time: 1120 us
  waiting for transfers between devices  487 us (43%)
  blocking collectives  340 us (30%)
  matrix products  179 us (16%)
  local copies, waits for them, and re-layouts  60.9 us (5%)
  other arithmetic  32.8 us (3%)
  between operations  15.5 us (1%)
    reduce_scatter x1, waiting for transfers between devices, shards(): lax.psum_scatter(grad_up, ('dp', 'seq'), scatter_dimension=0, tiled=True)  142 us
    reduce_scatter x1, waiting for transfers between devices, shards(): lax.psum_scatter(grad_down, ('dp', 'seq'), scatter_dimension=0, tiled=True)  141 us
    reduce_scatter x1, waiting for transfers between devices, shards(): lax.psum_scatter(grad_qkv, ('dp', 'seq'), scatter_dimension=0, tiled=True)  125 us
    unnamed x2, blocking collectives  75.4 us
    all_gather x1, waiting for transfers between devices, shards(): lax.all_gather(w_qkv, ('dp', 'seq'), axis=0, tiled=True)  65.9 us
    all_gather x1, blocking collectives, shards(): lax.all_gather(qv_bias, ('dp', 'seq'), axis=0, tiled=True)  65.8 us
    all_gather x1, blocking collectives, shards(): lax.all_gather(out_bias, ('dp', 'seq'), axis=0, tiled=True)  65.5 us
    all_gather x1, blocking collectives, shards(): lax.all_gather(norm_shift, ('dp', 'seq'), axis=0, tiled=True)  65.3 us
  transfers between devices with their start and end apart: 12, of which 5 were waited for; matrix products, arithmetic and copies ran while one was open for 16% of the time, Pallas kernels for 0%

commit v1 on v0

--- a/solution.py
+++ b/solution.py
@@ -1,14 +1,431 @@
+import functools
 import math
 
 import jax
 import jax.numpy as jnp
 from jax import lax
+from jax.experimental import pallas as pl
+from jax.experimental.pallas import tpu as pltpu
 from jax.sharding import PartitionSpec as P
 
 HEADS = 12
-
-
 EPS = 1e-12
+MESH = pl.DeviceIdType.MESH
+
+CHUNKS = ((0, 48, 32), (80, 64, 64), (208, 48, 48))
+SLAB = 304
+
+
+class Place:
+    def __init__(self):
+        dp = lax.axis_index("dp")
+        self.x = lax.axis_index("seq")
+        self.groups = lax.axis_size("dp") // 4
+        self.z = lax.div(dp, 4)
+        self.y = lax.rem(lax.div(dp, 2), 2)
+        self.c = lax.rem(dp, 2)
+        self.dp = dp
+
+    def at_z(self, step):
+        z = lax.rem(self.z + step, self.groups)
+        return (z * 4 + self.y * 2 + self.c, self.x)
+
+    def at_x(self):
+        return (self.dp, 1 - self.x)
+
+    def at_y(self):
+        return (self.z * 4 + (1 - self.y) * 2 + self.c, self.x)
+
+    def at_core(self):
+        return (self.z * 4 + self.y * 2 + 1 - self.c, self.x)
+
+    def slot(self, flip_y=0, flip_c=0, flip_x=0):
+        y = 1 - self.y if flip_y else self.y
+        c = 1 - self.c if flip_c else self.c
+        x = 1 - self.x if flip_x else self.x
+        return y * 4 + c * 2 + x
+
+    def z_back(self, step):
+        return lax.rem(self.z + self.groups - step, self.groups)
+
+    def partners(self):
+        return [self.at_z(step) for step in range(1, self.groups)] + [
+            self.at_x(),
+            self.at_y(),
+            self.at_core(),
+        ]
+
+    def greet(self):
+        barrier = pltpu.get_barrier_semaphore()
+        partners = self.partners()
+        for partner in partners:
+            pl.semaphore_signal(barrier, inc=1, device_id=partner, device_id_type=MESH)
+        pl.semaphore_wait(barrier, len(partners))
+
+
+class Wires:
+    def __init__(self, send, recv):
+        self.send, self.recv, self.sent = send, recv, []
+
+    def put(self, src, dst, to):
+        number = len(self.sent)
+        copy = pltpu.make_async_remote_copy(
+            src_ref=src,
+            dst_ref=dst,
+            send_sem=self.send.at[number],
+            recv_sem=self.recv.at[number],
+            device_id=to,
+            device_id_type=MESH,
+        )
+        copy.start()
+        self.sent.append(copy)
+        return (number, to)
+
+    def landed(self, ticket, ref):
+        number, to = ticket
+        pltpu.make_async_remote_copy(
+            src_ref=ref,
+            dst_ref=ref,
+            send_sem=self.send.at[number],
+            recv_sem=self.recv.at[number],
+            device_id=to,
+            device_id_type=MESH,
+        ).wait_recv()
+
+    def close(self):
+        for copy in self.sent:
+            copy.wait_send()
+
+
+class Gather:
+    def __init__(self, wires, place, slab, whole):
+        self.wires, self.place, self.slab, self.whole = wires, place, slab, whole
+        self.steps = place.groups
+        self.own, self.along_z, self.along_x, self.along_y = {}, {}, {}, {}
+        self.by_x, self.by_y, self.core = {}, {}, {}
+
+    def start(self, k):
+        first, some, more = CHUNKS[k]
+        rows = pl.ds(first, some + more)
+        place, wires = self.place, self.wires
+        src = self.slab.at[rows]
+        dst = self.whole.at[place.z, place.slot(), rows]
+        for step in range(1, self.steps):
+            self.along_z[k, step] = wires.put(src, dst, place.at_z(step))
+        self.along_x[k, 0] = wires.put(src, dst, place.at_x())
+        self.along_y[k, 0] = wires.put(src, dst, place.at_y())
+        self.core[k, 0, 0] = wires.put(src, dst, place.at_core())
+
+    def relay_z(self, k):
+        first, some, more = CHUNKS[k]
+        rows = pl.ds(first, some + more)
+        place, wires = self.place, self.wires
+        for step in range(1, self.steps):
+            ref = self.whole.at[place.z_back(step), place.slot(), rows]
+            wires.landed(self.along_z[k, step], ref)
+            self.along_x[k, step] = wires.put(ref, ref, place.at_x())
+            self.along_y[k, step] = wires.put(ref, ref, place.at_y())
+            self.core[k, 0, step] = wires.put(ref, ref, place.at_core())
+
+    def relay_plane(self, k):
+        first, some, more = CHUNKS[k]
+        rows, upper, lower = pl.ds(first, some + more), pl.ds(first, some), pl.ds(first + some, more)
+        place, wires = self.place, self.wires
+        for step in range(self.steps):
+            z = place.z_back(step)
+            slot = place.slot(flip_x=1)
+            ref = self.whole.at[z, slot, rows]
+            wires.landed(self.along_x[k, step], ref)
+            half = self.whole.at[z, slot, upper]
+            self.by_y[k, step] = wires.put(half, half, place.at_y())
+            self.core[k, 1, step] = wires.put(ref, ref, place.at_core())
+            slot = place.slot(flip_y=1)
+            ref = self.whole.at[z, slot, rows]
+            wires.landed(self.along_y[k, step], ref)
+            half = self.whole.at[z, slot, lower]
+            self.by_x[k, step] = wires.put(half, half, place.at_x())
+            self.core[k, 2, step] = wires.put(ref, ref, place.at_core())
+
+    def relay_corner(self, k):
+        first, some, more = CHUNKS[k]
+        rows, upper, lower = pl.ds(first, some + more), pl.ds(first, some), pl.ds(first + some, more)
+        place, wires = self.place, self.wires
+        for step in range(self.steps):
+            z = place.z_back(step)
+            slot = place.slot(flip_x=1, flip_y=1)
+            wires.landed(self.by_y[k, step], self.whole.at[z, slot, upper])
+            wires.landed(self.by_x[k, step], self.whole.at[z, slot, lower])
+            ref = self.whole.at[z, slot, rows]
+            self.core[k, 3, step] = wires.put(ref, ref, place.at_core())
+
+    def finish(self, k):
+        first, some, more = CHUNKS[k]
+        rows = pl.ds(first, some + more)
+        place = self.place
+        flips = ((0, 0), (0, 1), (1, 0), (1, 1))
+        for part, (flip_y, flip_x) in enumerate(flips):
+            slot = place.slot(flip_y=flip_y, flip_c=1, flip_x=flip_x)
+            for step in range(self.steps):
+                self.wires.landed(
+                    self.core[k, part, step], self.whole.at[place.z_back(step), slot, rows]
+                )
+
+
+def gather_kernel(
+    slab, short_tok, long_tok, short_cot, long_cot, pool,
+    whole, rows_in, rows_cot, pool_out,
+    send, recv, here,
+):
+    place = Place()
+    short_rows, half = short_tok.shape[0], long_tok.shape[1]
+    x, other = place.x, 1 - place.x
+    mine = pl.ds(pl.multiple_of(short_rows + x * half, half), half)
+    local = [
+        (short_tok, rows_in.at[pl.ds(0, short_rows)]),
+        (long_tok.at[x], rows_in.at[mine]),
+        (short_cot, rows_cot.at[pl.ds(0, short_rows)]),
+        (long_cot.at[x], rows_cot.at[mine]),
+        (pool.at[x], pool_out.at[x]),
+        (slab, whole.at[place.z, place.slot()]),
+    ]
+    copies = [pltpu.make_async_copy(src, dst, here.at[i]) for i, (src, dst) in enumerate(local)]
+    for copy in copies:
+        copy.start()
+    place.greet()
+    wires = Wires(send, recv)
+    net = Gather(wires, place, slab, whole)
+    net.start(0)
+    theirs = pl.ds(pl.multiple_of(short_rows + other * half, half), half)
+    tok = wires.put(long_tok.at[other], rows_in.at[mine], place.at_x())
+    pooled = wires.put(pool.at[other], pool_out.at[x], place.at_x())
+    last = len(CHUNKS) - 1
+    for k in range(last + 1):
+        if k < last:
+            net.start(k + 1)
+        net.relay_z(k)
+        net.relay_plane(k)
+        net.relay_corner(k)
+        if k == 0:
+            cot = wires.put(long_cot.at[other], rows_cot.at[mine], place.at_x())
+    for k in range(last + 1):
+        net.finish(k)
+    wires.landed(tok, rows_in.at[theirs])
+    wires.landed(cot, rows_cot.at[theirs])
+    wires.landed(pooled, pool_out.at[other])
+    wires.close()
+    for copy in copies:
+        copy.wait()
+
+
+def gather_all(slab, short_tok, long_tok, short_cot, long_cot, pool, groups):
+    short_rows, width = short_tok.shape
+    rows = short_rows + 2 * long_tok.shape[1]
+    copies = len(CHUNKS) * ((groups - 1) + 4 * groups + 4 * groups) + 3
+    anywhere = pl.BlockSpec(memory_space=pl.ANY)
+    return pl.pallas_call(
+        gather_kernel,
+        name="gather_parameters",
+        out_shape=(
+            jax.ShapeDtypeStruct((groups, 8) + slab.shape, slab.dtype),
+            jax.ShapeDtypeStruct((rows, width), short_tok.dtype),
+            jax.ShapeDtypeStruct((rows, width), short_cot.dtype),
+            jax.ShapeDtypeStruct(pool.shape, pool.dtype),
+        ),
+        in_specs=[anywhere] * 6,
+        out_specs=[anywhere] * 4,
+        scratch_shapes=[
+            pltpu.SemaphoreType.DMA((copies,)),
+            pltpu.SemaphoreType.DMA((copies,)),
+            pltpu.SemaphoreType.DMA((6,)),
+        ],
+        compiler_params=pltpu.CompilerParams(collective_id=0, has_side_effects=True),
+    )(slab, short_tok, long_tok, short_cot, long_cot, pool)
+
+
+class Scatter:
+    def __init__(self, wires, place, sums, from_core, from_x, from_y, last_x, last_y, from_z, out):
+        self.wires, self.place = wires, place
+        self.sums, self.from_core, self.from_x, self.from_y = sums, from_core, from_x, from_y
+        self.last_x, self.last_y, self.from_z, self.out = last_x, last_y, from_z, out
+        self.steps = place.groups
+        self.core, self.first, self.second, self.third = {}, {}, {}, {}
+
+    def send_core(self, k, grads):
+        first, some, more = CHUNKS[k]
+        rows = pl.ds(first, some + more)
+        place = self.place
+        for part, (flip_y, flip_x) in enumerate(((0, 0), (0, 1), (1, 0), (1, 1))):
+            slot = place.slot(flip_y=flip_y, flip_c=1, flip_x=flip_x)
+            self.core[k, part] = self.wires.put(
+                grads.at[:, slot, rows], self.from_core.at[part, :, rows], place.at_core()
+            )
+
+    def add(self, into, other):
+        for z in range(self.steps):
+            total = into[z].astype(jnp.float32) + other[z].astype(jnp.float32)
+            into[z] = total.astype(into.dtype)
+
+    def after_core(self, k):
+        first, some, more = CHUNKS[k]
+        rows, upper, lower = pl.ds(first, some + more), pl.ds(first, some), pl.ds(first + some, more)
+        wires, place = self.wires, self.place
+        for part in (3, 1, 2, 0):
+            wires.landed(self.core[k, part], self.from_core.at[part, :, rows])
+            self.add(self.sums.at[part, :, rows], self.from_core.at[part, :, rows])
+            if part == 3:
+                self.first[k, "x", 1] = wires.put(
+                    self.sums.at[3, :, upper], self.from_x.at[1, :, upper], place.at_x()
+                )
+                self.first[k, "y", 1] = wires.put(
+                    self.sums.at[3, :, lower], self.from_y.at[1, :, lower], place.at_y()
+                )
+            elif part == 1:
+                self.first[k, "x", 0] = wires.put(
+                    self.sums.at[1, :, upper], self.from_x.at[0, :, upper], place.at_x()
+                )
+            elif part == 2:
+                self.first[k, "y", 0] = wires.put(
+                    self.sums.at[2, :, lower], self.from_y.at[0, :, lower], place.at_y()
+                )
+
+    def after_first(self, k):
+        first, some, more = CHUNKS[k]
+        upper, lower = pl.ds(first, some), pl.ds(first + some, more)
+        wires, place = self.wires, self.place
+        wires.landed(self.first[k, "x", 1], self.from_x.at[1, :, upper])
+        self.add(self.sums.at[2, :, upper], self.from_x.at[1, :, upper])
+        self.second[k, "y"] = wires.put(
+            self.sums.at[2, :, upper], self.last_y.at[:, upper], place.at_y()
+        )
+        wires.landed(self.first[k, "y", 1], self.from_y.at[1, :, lower])
+        self.add(self.sums.at[1, :, lower], self.from_y.at[1, :, lower])
+        self.second[k, "x"] = wires.put(
+            self.sums.at[1, :, lower], self.last_x.at[:, lower], place.at_x()
+        )
+        wires.landed(self.first[k, "x", 0], self.from_x.at[0, :, upper])
+        self.add(self.sums.at[0, :, upper], self.from_x.at[0, :, upper])
+        wires.landed(self.first[k, "y", 0], self.from_y.at[0, :, lower])
+        self.add(self.sums.at[0, :, lower], self.from_y.at[0, :, lower])
+
+    def after_second(self, k):
+        first, some, more = CHUNKS[k]
+        rows, upper, lower = pl.ds(first, some + more), pl.ds(first, some), pl.ds(first + some, more)
+        wires, place = self.wires, self.place
+        wires.landed(self.second[k, "y"], self.last_y.at[:, upper])
+        self.add(self.sums.at[0, :, upper], self.last_y.at[:, upper])
+        wires.landed(self.second[k, "x"], self.last_x.at[:, lower])
+        self.add(self.sums.at[0, :, lower], self.last_x.at[:, lower])
+        for step in range(1, self.steps):
+            z = lax.rem(place.z + step, self.steps)
+            self.third[k, step] = wires.put(
+                self.sums.at[0, z, rows], self.from_z.at[step - 1, rows], place.at_z(step)
+            )
+
+    def finish(self, k):
+        first, some, more = CHUNKS[k]
+        rows = pl.ds(first, some + more)
+        total = self.sums[0, self.place.z, rows].astype(jnp.float32)
+        for step in range(1, self.steps):
+            self.wires.landed(self.third[k, step], self.from_z.at[step - 1, rows])
+            total = total + self.from_z[step - 1, rows].astype(jnp.float32)
+        self.out[rows] = total
+
+
+def scatter_kernel(
+    grads, long_out, long_grad, pooled,
+    out, both_out, both_grad, both_pooled,
+    sums, from_core, from_x, from_y, last_x, last_y, from_z,
+    send, recv, load, here,
+):
+    place = Place()
+    x, other = place.x, 1 - place.x
+    half = both_out.shape[1]
+    own_rows = pl.ds(pl.multiple_of(x * half, half), half)
+    their_rows = pl.ds(pl.multiple_of(other * half, half), half)
+    loads = {}
+    order = (2, 1, 0)
+    for k in order:
+        first, some, more = CHUNKS[k]
+        rows = pl.ds(first, some + more)
+        for part, (flip_y, flip_x) in enumerate(((0, 0), (0, 1), (1, 0), (1, 1))):
+            slot = place.slot(flip_y=flip_y, flip_x=flip_x)
+            loads[k, part] = pltpu.make_async_copy(
+                grads.at[:, slot, rows], sums.at[part, :, rows], load.at[k * 4 + part]
+            )
+            loads[k, part].start()
+    copies = [
+        pltpu.make_async_copy(long_out.at[own_rows], both_out.at[x], here.at[0]),
+        pltpu.make_async_copy(long_grad.at[own_rows], both_grad.at[x], here.at[1]),
+        pltpu.make_async_copy(pooled, both_pooled.at[x], here.at[2]),
+    ]
+    for copy in copies:
+        copy.start()
+    place.greet()
+    wires = Wires(send, recv)
+    net = Scatter(wires, place, sums, from_core, from_x, from_y, last_x, last_y, from_z, out)
+    for k in order:
+        net.send_core(k, grads)
+    swaps = [
+        (wires.put(long_out.at[their_rows], both_out.at[x], place.at_x()), both_out),
+        (wires.put(long_grad.at[their_rows], both_grad.at[x], place.at_x()), both_grad),
+        (wires.put(pooled, both_pooled.at[x], place.at_x()), both_pooled),
+    ]
+    todo = []
+    for k in order:
+        for part in range(4):
+            loads[k, part].wait()
+        net.after_core(k)
+        if len(todo) >= 1:
+            net.after_first(todo[-1])
+        if len(todo) >= 2:
+            net.after_second(todo[-2])
+        todo.append(k)
+    net.after_first(todo[-1])
+    net.after_second(todo[-2])
+    net.after_second(todo[-1])
+    for k in order:
+        net.finish(k)
+    for ticket, ref in swaps:
+        wires.landed(ticket, ref.at[other])
+    wires.close()
+    for copy in copies:
+        copy.wait()
+
+
+def scatter_all(grads, long_out, long_grad, pooled, groups):
+    width = grads.shape[-1]
+    half = long_out.shape[0] // 2
+    copies = len(CHUNKS) * (4 + 6 + (groups - 1)) + 3
+    anywhere = pl.BlockSpec(memory_space=pl.ANY)
+    low = jnp.bfloat16
+    return pl.pallas_call(
+        scatter_kernel,
+        name="scatter_gradients",
+        out_shape=(
+            jax.ShapeDtypeStruct((SLAB, width), jnp.float32),
+            jax.ShapeDtypeStruct((2, half, width), long_out.dtype),
+            jax.ShapeDtypeStruct((2, half, width), long_grad.dtype),
+            jax.ShapeDtypeStruct((2,) + pooled.shape, pooled.dtype),
+        ),
+        in_specs=[anywhere] * 4,
+        out_specs=[pl.BlockSpec(memory_space=pltpu.VMEM)] + [anywhere] * 3,
+        scratch_shapes=[
+            pltpu.VMEM((4, groups, SLAB, width), low),
+            pltpu.VMEM((4, groups, SLAB, width), low),
+            pltpu.VMEM((2, groups, SLAB, width), low),
+            pltpu.VMEM((2, groups, SLAB, width), low),
+            pltpu.VMEM((groups, SLAB, width), low),
+            pltpu.VMEM((groups, SLAB, width), low),
+            pltpu.VMEM((groups - 1, SLAB, width), low),
+            pltpu.SemaphoreType.DMA((copies,)),
+            pltpu.SemaphoreType.DMA((copies,)),
+            pltpu.SemaphoreType.DMA((4 * len(CHUNKS),)),
+            pltpu.SemaphoreType.DMA((3,)),
+        ],
+        compiler_params=pltpu.CompilerParams(
+            collective_id=1, has_side_effects=True, vmem_limit_bytes=48 * 1024 * 1024
+        ),
+    )(grads, long_out, long_grad, pooled)
 
 
 def layer_norm(row_data, gain_vec, shift_vec):
@@ -89,7 +506,7 @@
     )
 
 
-def shards(
+def general_shards(
     short_tokens,
     long_tokens,
     short_len,
@@ -329,43 +746,220 @@
     )
 
 
+def pack_slab(w_qkv, w_out, w_up, w_down, qv_bias, out_bias, up_bias, norm_gain, norm_shift):
+    rows, width = w_out.shape
+    pairs = [member.T for member in (qv_bias, out_bias, norm_gain, norm_shift)]
+    vectors = jnp.concatenate([jnp.concatenate(pairs, axis=0).reshape(-1), up_bias])
+    vectors = jnp.pad(vectors, (0, 8 * width - vectors.shape[0])).reshape(8, width)
+    blocks = [w_qkv[:, i * width : (i + 1) * width] for i in range(3)]
+    blocks += [vectors, w_out, jnp.zeros((8, width), w_out.dtype)]
+    blocks += [w_up[:, i * width : (i + 1) * width] for i in range(4)]
+    return jnp.concatenate(blocks + [w_down], axis=0)
+
+
+def by_columns(slabs, first, rows, blocks):
+    part = slabs[:, first : first + blocks * rows]
+    width = part.shape[-1]
+    part = part.reshape(slabs.shape[0], blocks, rows, width).transpose(0, 2, 1, 3)
+    return part.reshape(slabs.shape[0] * rows, blocks * width)
+
+
+def to_columns(grad, devices, blocks):
+    rows, width = grad.shape[0] // devices, grad.shape[1] // blocks
+    grad = grad.reshape(devices, rows, blocks, width).transpose(0, 2, 1, 3)
+    return grad.reshape(devices, blocks * rows, width)
+
+
+def fast_shards(
+    short_tokens, long_tokens, short_len, long_len, short_pool, long_pool, short_cot, long_cot,
+    short_pool_cot, long_pool_cot, w_qkv, w_out, w_up, w_down, qv_bias, out_bias, up_bias,
+    norm_gain, norm_shift,
+):
+    groups = lax.axis_size("dp") // 4
+    devices = groups * 8
+    rows, width = w_out.shape
+    x = lax.axis_index("seq")
+    short_count, short_cap, _ = short_tokens.shape
+    half = long_tokens.shape[1]
+    short_rows, long_rows = short_count * short_cap, 2 * half
+    slab = pack_slab(w_qkv, w_out, w_up, w_down, qv_bias, out_bias, up_bias, norm_gain, norm_shift)
+    pool = jnp.broadcast_to(long_pool[:, None, :], (2, 8, half))
+    whole, inputs, cot, pool = gather_all(
+        slab,
+        short_tokens.reshape(short_rows, width),
+        long_tokens,
+        short_cot.reshape(short_rows, width),
+        long_cot,
+        pool,
+        groups,
+    )
+    slabs = whole.reshape(devices, SLAB, width)
+    qkv_matrix = by_columns(slabs, 0, rows, 3)
+    out_matrix = slabs[:, 80 : 80 + rows].reshape(width, width)
+    up_matrix = by_columns(slabs, 112, rows, 4)
+    down_matrix = slabs[:, 208:304].reshape(4 * width, width)
+    vectors = slabs[:, 72].astype(jnp.float32)
+    pairs = vectors[:, : 8 * rows].reshape(devices, 8, rows).transpose(1, 0, 2).reshape(8, width)
+    up_vec = vectors[:, 8 * rows : 12 * rows].reshape(4 * width)
+    long_pool = pool[:, 0].reshape(1, long_rows)
+    long_len = lax.dynamic_slice_in_dim(long_len, x, 1)
+    long_pool_cot = lax.dynamic_slice_in_dim(long_pool_cot, x, 1)
+
+    score_scale = 1.0 / math.sqrt(width // HEADS)
+    short_place = jnp.arange(short_cap, dtype=jnp.int32)
+    short_live = short_place[None, :] < short_len[:, None]
+    long_place = jnp.arange(long_rows, dtype=jnp.int32)
+    long_live = long_place[None, :] < long_len[:, None]
+    short_weight = (short_live & ((short_pool > 0) | (short_place[None, :] == 0))).astype(jnp.float32)
+    long_weight = (long_live & ((long_pool > 0) | (long_place[None, :] == 0))).astype(jnp.float32)
+    row_live = jnp.concatenate([short_live.reshape(-1), long_live.reshape(-1)]).astype(jnp.float32)
+    joined = jnp.dot(inputs, qkv_matrix, preferred_element_type=jnp.float32)
+    queries = (joined[:, :width] + pairs[0]).astype(jnp.bfloat16)
+    keys_all = joined[:, width : 2 * width].astype(jnp.bfloat16)
+    values = (joined[:, 2 * width :] + pairs[1]).astype(jnp.bfloat16)
+    short_shape = (short_count, short_cap, HEADS, width // HEADS)
+    long_shape = (1, long_rows, HEADS, width // HEADS)
+    short_qkv = [m[:short_rows].reshape(short_shape) for m in (queries, keys_all, values)]
+    long_qkv = [m[short_rows:].reshape(long_shape) for m in (queries, keys_all, values)]
+    short_mixed, short_logsum = attend_forward((*short_qkv, short_live), score_scale)
+    long_mixed, long_logsum = attend_forward((*long_qkv, long_live), score_scale)
+    mixed_heads = jnp.concatenate(
+        [short_mixed.reshape(short_rows, width), long_mixed.reshape(long_rows, width)], axis=0
+    )
+    attn_out = jnp.dot(mixed_heads, out_matrix, preferred_element_type=jnp.float32) + pairs[2]
+    first_in = inputs.astype(jnp.float32) + attn_out
+    first_norm = layer_norm(first_in, pairs[4], pairs[6])
+    first_low = first_norm.astype(jnp.bfloat16)
+    inner_act = jnp.dot(first_low, up_matrix, preferred_element_type=jnp.float32) + up_vec
+    activated = exact_gelu(inner_act).astype(jnp.bfloat16)
+    branch = jnp.dot(activated, down_matrix, preferred_element_type=jnp.float32) + pairs[3]
+    second_in = first_norm + branch
+    final_norm = layer_norm(second_in, pairs[5], pairs[7]) * row_live[:, None]
+    short_final = final_norm[:short_rows].reshape(short_count, short_cap, width)
+    long_final = final_norm[short_rows:].reshape(1, long_rows, width)
+    short_total = jnp.sum(short_weight, axis=1)
+    long_total = jnp.sum(long_weight, axis=1)
+    short_pooled = jnp.sum(short_final * short_weight[..., None], axis=1) / short_total[:, None]
+    long_pooled = jnp.sum(long_final * long_weight[..., None], axis=1) / long_total[:, None]
+    weight = jnp.concatenate([short_weight.reshape(-1), long_weight.reshape(-1)])
+    spread_cot = jnp.concatenate(
+        [
+            jnp.repeat(short_pool_cot / short_total[:, None], short_cap, axis=0),
+            jnp.repeat(long_pool_cot / long_total[:, None], long_rows, axis=0),
+        ],
+        axis=0,
+    )
+    grad_top = cot.astype(jnp.float32) * row_live[:, None] + weight[:, None] * spread_cot
+    _, second_back = jax.vjp(layer_norm, second_in, pairs[5], pairs[7])
+    grad_second, grad_gain_two, grad_shift_two = second_back(grad_top)
+    grad_branch = grad_second.astype(jnp.bfloat16)
+    grad_down = outer_sum(activated, grad_branch)
+    grad_bias_two = jnp.sum(grad_branch.astype(jnp.float32), axis=0)
+    grad_acted = times_transposed(grad_branch, down_matrix)
+    _, gelu_back = jax.vjp(exact_gelu, inner_act)
+    grad_inner = gelu_back(grad_acted)[0].astype(jnp.bfloat16)
+    grad_up = outer_sum(first_low, grad_inner)
+    grad_up_bias = jnp.sum(grad_inner.astype(jnp.float32), axis=0)
+    grad_first = grad_second + times_transposed(grad_inner, up_matrix)
+    _, first_back = jax.vjp(layer_norm, first_in, pairs[4], pairs[6])
+    grad_first_in, grad_gain_one, grad_shift_one = first_back(grad_first)
+    grad_attn = grad_first_in.astype(jnp.bfloat16)
+    grad_out = outer_sum(mixed_heads, grad_attn)
+    grad_bias_one = jnp.sum(grad_attn.astype(jnp.float32), axis=0)
+    grad_mixed = times_transposed(grad_attn, out_matrix).astype(jnp.bfloat16)
+    short_back = attend_backward(
+        (*short_qkv, short_live, grad_mixed[:short_rows].reshape(short_shape), short_logsum), score_scale
+    )
+    long_back = attend_backward(
+        (*long_qkv, long_live, grad_mixed[short_rows:].reshape(long_shape), long_logsum), score_scale
+    )
+    grad_joined = jnp.concatenate(
+        [
+            jnp.concatenate([a.reshape(short_rows, width), b.reshape(long_rows, width)], axis=0)
+            for a, b in zip(short_back, long_back)
+        ],
+        axis=1,
+    ).astype(jnp.bfloat16)
+    grad_qkv = outer_sum(inputs, grad_joined)
+    grad_bias = jnp.sum(grad_joined.astype(jnp.float32), axis=0)
+    grad_inputs = grad_first_in + times_transposed(grad_joined, qkv_matrix)
+
+    grad_pairs = jnp.stack(
+        [
+            grad_bias[:width], grad_bias[2 * width :], grad_bias_one, grad_bias_two,
+            grad_gain_one, grad_gain_two, grad_shift_one, grad_shift_two,
+        ]
+    )
+    grad_vectors = jnp.concatenate(
+        [
+            grad_pairs.reshape(8, devices, rows).transpose(1, 0, 2).reshape(devices, 8 * rows),
+            grad_up_bias.reshape(devices, 4 * rows),
+        ],
+        axis=1,
+    )
+    grad_vectors = jnp.pad(grad_vectors, ((0, 0), (0, 8 * width - 12 * rows)))
+    grads = jnp.concatenate(
+        [
+            to_columns(grad_qkv, devices, 3),
+            grad_vectors.reshape(devices, 8, width),
+            grad_out.reshape(devices, rows, width),
+            jnp.zeros((devices, 8, width), jnp.float32),
+            to_columns(grad_up, devices, 4),
+            grad_down.reshape(devices, 4 * rows, width),
+        ],
+        axis=1,
+    ).astype(jnp.bfloat16)
+    pooled = jnp.broadcast_to(long_pooled, (8, width))
+    out, long_out, long_grad, both_pooled = scatter_all(
+        grads.reshape(groups, 8, SLAB, width),
+        final_norm[short_rows:].astype(jnp.bfloat16),
+        grad_inputs[short_rows:].astype(jnp.bfloat16),
+        pooled,
+        groups,
+    )
+
+    def widen(first, blocks):
+        part = out[first : first + blocks * rows].reshape(blocks, rows, width)
+        return part.transpose(1, 0, 2).reshape(rows, blocks * width)
+
+    small = out[72, : 8 * rows].reshape(8, rows)
+    return (
+        short_final.astype(jnp.bfloat16),
+        long_out,
+        short_pooled,
+        both_pooled[:, 0],
+        grad_inputs[:short_rows].reshape(short_count, short_cap, width),
+        long_grad.astype(jnp.float32),
+        widen(0, 3),
+        out[80 : 80 + rows],
+        widen(112, 4),
+        out[208:304],
+        small[0:2].T,
+        small[2:4].T,
+        out[72, 8 * rows : 12 * rows],
+        small[4:6].T,
+        small[6:8].T,
+    )
+
+
 def solution(mesh):
+    short_spec, long_spec, spread = P(("dp", "seq"), None, None), P("dp", "seq", None), P(("dp", "seq"), None)
+    vector, parameters = P(("dp", "seq")), [P(("dp", "seq"), None)] * 6
     in_specs = (
-        P(("dp", "seq"), None, None),
-        P("dp", "seq", None),
-        P(("dp", "seq")),
-        P("dp"),
-        P(("dp", "seq"), None),
-        P("dp", "seq"),
-        P(("dp", "seq"), None, None),
-        P("dp", "seq", None),
-        P(("dp", "seq"), None),
-        P("dp", None),
-        P(("dp", "seq"), None),
-        P(("dp", "seq"), None),
-        P(("dp", "seq"), None),
-        P(("dp", "seq"), None),
-        P(("dp", "seq"), None),
-        P(("dp", "seq"), None),
-        P(("dp", "seq")),
-        P(("dp", "seq"), None),
-        P(("dp", "seq"), None),
+        short_spec, long_spec, vector, P("dp"), spread, P("dp", "seq"), short_spec, long_spec,
+        spread, P("dp", None), *parameters, vector, spread, spread,
     )
     out_specs = (
-        P(("dp", "seq"), None, None),
-        P("dp", "seq", None),
-        P(("dp", "seq"), None),
-        P("dp", None),
-        P(("dp", "seq"), None, None),
-        P("dp", "seq", None),
-        P(("dp", "seq"), None),
-        P(("dp", "seq"), None),
-        P(("dp", "seq"), None),
-        P(("dp", "seq"), None),
-        P(("dp", "seq"), None),
-        P(("dp", "seq"), None),
-        P(("dp", "seq")),
-        P(("dp", "seq"), None),
-        P(("dp", "seq"), None),
-    )
-    return jax.shard_map(shards, mesh=mesh, in_specs=in_specs, out_specs=out_specs, check_vma=False)
+        short_spec, long_spec, spread, P("dp", None), short_spec, long_spec, *parameters, vector,
+        spread, spread,
+    )
+    dp, seq = mesh.shape["dp"], mesh.shape["seq"]
+
+    def run(*arrays):
+        width = arrays[11].shape[1]
+        passages = arrays[1].shape[0] // dp
+        regular = dp % 4 == 0 and seq == 2 and passages == 2 and width == 24 * dp * seq
+        body = fast_shards if regular else general_shards
+        return jax.shard_map(body, mesh=mesh, in_specs=in_specs, out_specs=out_specs, check_vma=False)(*arrays)
+
+    return run

time: 1120 us -> 554 us (0.49)
  waiting for transfers between devices: 487 us -> 0 us
  blocking collectives: 340 us -> 0 us
  Pallas kernels: 0 us -> 198 us
  local copies, waits for them, and re-layouts: 60.9 us -> 113 us
  other arithmetic: 32.8 us -> 64.3 us
  between operations: 15.5 us -> 2 us
    reduce_scatter x6 -> x0, waiting for transfers between devices: 418 us -> none  [the longest x1 142 us: shards(): lax.psum_scatter(grad_up, ('dp', 'seq'), scatter_dimension=0, tiled=True)]
    all_gather x4 -> x0, blocking collectives: 260 us -> none  [the longest x1 65.8 us: shards(): lax.all_gather(qv_bias, ('dp', 'seq'), axis=0, tiled=True)]
    pallas_call x0 -> x2, Pallas kernels: none -> 198 us  [the longest x1 109 us: scatter_all(): pl.pallas_call(scatter_kernel, name='scatter_gradients', out_shape=(jax.S...]
    unnamed x2 -> x0, blocking collectives: 75.4 us -> none
    all_gather x6 -> x0, waiting for transfers between devices: 65.9 us -> none  [the longest x1 65.9 us: shards(): lax.all_gather(w_qkv, ('dp', 'seq'), axis=0, tiled=True)]
    reshape x2 -> x15, local copies, waits for them, and re-layouts: 4.55 us -> 30.4 us  [the longest x3 24.1 us: to_columns(): grad = grad.reshape(devices, rows, blocks, width).transpose(0, 2, 1, 3)]
    reduce_sum x7, other arithmetic: 4.43 us -> 28.7 us  [the longest x1 22.9 us: fast_shards(): grad_bias = jnp.sum(grad_joined.astype(jnp.float32), axis=0)]
    slice x12 -> x28, local copies, waits for them, and re-layouts: 13.9 us -> 28.7 us  [the longest x1 6.54 us: fast_shards(): down_matrix = slabs[:, 208:304].reshape(4 * width, width)]
  transfers between devices with their start and end apart: 12 -> 0, of which waited for: 5 -> 0; matrix products, arithmetic and copies ran while one was open for 16% -> 0% of each run, Pallas kernels for 0% -> 0%
where the time goes in v1:
time: 554 us; the launch traced here: 549 us
  Pallas kernels  198 us (36%)
  matrix products  171 us (31%)
  local copies, waits for them, and re-layouts  113 us (20%)
  other arithmetic  64.3 us (12%)
    pallas_call x1, Pallas kernels, scatter_all(): pl.pallas_call(scatter_kernel, name='scatter_gradients', out_shape=(jax.S...  109 us
    pallas_call x1, Pallas kernels, gather_all(): pl.pallas_call(gather_kernel, name='gather_parameters', out_shape=(jax.Sh...  89.3 us
    dot_general x4, matrix products, outer_sum(): lax.dot_general(left_rows, right_rows, (((0,), (0,)), ((), ())), preferre...  50.4 us
    dot_general x1, matrix products, fast_shards(): jnp.dot(first_low, up_matrix, preferred_element_type=jnp.float32) + up_vec  35 us
    dot_general x4, matrix products, times_transposed(): lax.dot_general(left_rows, matrix, (((1,), (1,)), ((), ())), preferred_el...  33.6 us
    unnamed x162, local copies, waits for them, and re-layouts  32.8 us
    reshape x3, local copies, waits for them, and re-layouts, to_columns(): grad = grad.reshape(devices, rows, blocks, width).transpose(0, 2, 1, 3)  24.1 us
    reduce_sum x1, other arithmetic, fast_shards(): grad_bias = jnp.sum(grad_joined.astype(jnp.float32), axis=0)  22.9 us

profile of v1, /device:TPU:0, one launch (start us, length us, event | category | flops | bytes accessed | tf_op | source)
XLA Modules:
  0.0 549.0 jit_solution(17310923994089232440)
XLA Ops:
  15.6 89.3 %gather_parameters.1 = (bf16[4,8,304,768]{3,2,1,0:T(8,128)(2,1)}, bf16[1024,768]{1,0:T(8,128)(2,1)}, bf16[1024,768]{1,0:T(8,128)(2,1)}, s32[2,8,256]{2,1,0:T(8,128)}) custom-call(bf16[304,768]{1,0:T(8,128)(2,1)} %copy-done.31, bf16[512,768]{1,0:T(8,128)(2,1)} %bitcast.229, bf16[2,256,768]{2,1,0:T(8,128)(2,1)} %long_tok.1, bf16[512,768]{1,0:T(8,128)(2,1)} %bitcast.230, ...), custom_call_target="tpu_custom_call" | custom-call | tf_op jit(solution)/shard_map/gather_parameters/pallas_call | solution.py:225
  120.2 6.5 %fusion.71 = (bf16[32,96,768]{2,1,0:T(8,128)(2,1)}, bf16[32,96,768]{2,1,0:T(8,128)(2,1)S(1)}) fusion(bf16[32,304,768]{2,1,0:T(8,128)(2,1)} %bitcast.177), kind=kLoop, calls=%fused_computation.188 | loop fusion | bytes 18874368 | tf_op jit(solution)/shard_map/slice | solution.py:800
  129.1 3.3 copy.138
  136.2 6.4 %fusion.79 = (bf16[1024,2304]{1,0:T(8,128)(2,1)S(1)}, f32[1024,2304]{1,0:T(8,128)}) fusion(bf16[1024,768]{1,0:T(8,128)(2,1)S(1)} %copy-done.48, bf16[768,2304]{1,0:T(8,128)(2,1)S(1)} %bitcast.198), kind=kOutput, calls=%fused_computation.196 | convolution fusion | flops 3626237952 | bytes 19267584 | tf_op jit(solution)/shard_map/dot_general | solution.py:816
  144.4 3.6 fusion.12
  162.2 3.0 fusion.80
  167.8 3.2 copy-done.2
  171.0 12.5 %fusion.29 = bf16[12,64,512]{2,1,0:T(8,128)(2,1)S(1)} fusion(bf16[512,12,64]{0,2,1:T(8,128)(2,1)} %bitcast.200, f32[12,512,512]{1,2,0:T(8,128)S(1)} %get-tuple-element.85, f32[12,512]{1,0:T(8,128)S(1)} %fusion.6, f32[12,512]{1,0:T(8,128)S(1)} %get-tuple-element.84), kind=kOutput, calls=%fused_computation.80 | convolution fusion | flops 412483584 | bytes 14204928 | tf_op jit(solution)/shard_map/bhqk,bkhe->bqhe/dot_general | solution.py:468
  185.8 35.0 %multiply_convert_fusion.1 = (bf16[1024,3072]{1,0:T(8,128)(2,1)S(1)}, f32[1024,3072]{1,0:T(8,128)}, f32[1024,3072]{1,0:T(8,128)}) fusion(f32[3072]{0:T(1024)S(1)} %add.159, bf16[768,3072]{1,0:T(8,128)(2,1)S(1)} %bitcast.193, f32[1024,768]{1,0:T(8,128)S(1)} %get-tuple-element.89, f32[768]{0:T(1024)S(1)} %add.156, f32[768]{0:T(1024)S(1)} %mul.249, ...), kind=kOutput, calls=%fused_computation.6 | convolution fusion | flops 5043388416 | bytes 39348224 | tf_op jit(solution)/shard_map/dot_general | solution.py:833
  220.9 5.5 fusion.83
  228.3 2.8 multiply_reduce_fusion.1
  231.1 3.6 fusion.68
  236.6 3.1 fusion.73
  240.7 16.7 %fusion.84 = (bf16[3072]{0:T(1024)(128)(2,1)S(1)}, bf16[1024,3072]{1,0:T(8,128)(2,1)}) fusion(f32[1024,3072]{1,0:T(8,128)} %get-tuple-element.60, bf16[1024,768]{1,0:T(8,128)(2,1)S(1)} %get-tuple-element.50, bf16[3072,768]{1,0:T(8,128)(2,1)} %bitcast.194, f32[1024,3072]{1,0:T(8,128)} %get-tuple-element.90, f32[3072]{0:T(1024)S(1)} %add.159), kind=kOutput, calls=%fused_computation.201 | convolution fusion | flops 4882166784 | bytes 37767168 | tf_op jit(solution)/shard_map/dot_general | solution.py:448
  257.4 10.0 %convolution_convert_fusion = bf16[3072,768]{1,0:T(8,128)(2,1)} fusion(bf16[1024,3072]{1,0:T(8,128)(2,1)} %copy-done.53, bf16[1024,768]{1,0:T(8,128)(2,1)S(1)} %get-tuple-element.50), kind=kOutput, calls=%fused_computation.28 | convolution fusion | flops 4834197504 | bytes 12582912 | tf_op jit(solution)/shard_map/dot_general | solution.py:442
  267.4 8.5 %multiply_reduce_fusion.2 = (bf16[768]{0:T(1024)(128)(2,1)S(1)}, f32[1024]{0:T(1024)S(1)}, bf16[768]{0:T(1024)(128)(2,1)S(1)}, f32[1024,768]{1,0:T(8,128)S(1)}) fusion(f32[1024,768]{1,0:T(8,128)S(1)} %copy-done.10, f32[1024]{0:T(1024)S(1)} %fusion.51, f32[1024]{0:T(1024)S(1)} %broadcast_multiply_fusion.1, f32[768]{0:T(1024)S(1)} %mul.249, ...), kind=kOutput, calls=%fused_computation.41 | convolution fusion | flops 4839699456 | bytes 20469760 | tf_op jit(solution)/shard_map/dot_general | solution.py:448
  275.9 2.7 fusion.67
  278.5 8.0 %convolution_convert_fusion.1 = bf16[768,3072]{1,0:T(8,128)(2,1)} fusion(bf16[1024,3072]{1,0:T(8,128)(2,1)S(1)} %copy-done.52, f32[1024,768]{1,0:T(8,128)S(1)} %copy-done.10, f32[768]{0:T(1024)S(1)} %add.156, f32[768]{0:T(1024)S(1)} %mul.249, f32[1024]{0:T(1024)S(1)} %fusion.51, f32[1024]{0:T(1024)S(1)} %broadcast_multiply_fusion.1), kind=kOutput, calls=%fused_computation.29 | convolution fusion | flops 4838129664 | bytes 14170112 | tf_op jit(solution)/shard_map/dot_general | solution.py:442
  286.5 9.7 %reshape.553 = bf16[32,24,4,768]{3,2,1,0:T(4,128)(2,1)} reshape(bf16[768,3072]{1,0:T(8,128)(2,1)} %convolution_convert_fusion.1) | data formatting | bytes 9437184 | tf_op jit(solution)/shard_map/reshape | solution.py:769
  296.3 5.4 copy.122
  304.3 3.5 convolution_convert_fusion.4
  308.0 2.7 convolution_convert_fusion.3
  311.4 6.8 %fusion.26 = bf16[12,64,512]{2,1,0:T(8,128)(2,1)S(1)} fusion(bf16[512,12,64]{0,2,1:T(8,128)(2,1)S(1)} %bitcast.180, f32[12,512,512]{1,2,0:T(8,128)} %copy-done.2, f32[12,512]{1,0:T(8,128)S(1)} %copy-done.33), kind=kOutput, calls=%fused_computation.79 | convolution fusion | flops 409337856 | bytes 14180352 | tf_op jit(solution)/shard_map/bhqk,bqhe->bkhe/dot_general | solution.py:481
  327.7 6.3 %multiply_reduce_fusion = (f32[12,512]{1,0:T(8,128)S(1)}, f32[12,512,512]{1,2,0:T(8,128)}) fusion(f32[12,512,512]{1,2,0:T(8,128)S(1)} %bitcast.162, f32[12,512]{1,0:T(8,128)S(1)} %copy-done.33, bf16[512,12,64]{0,2,1:T(8,128)(2,1)S(1)} %bitcast.181, bf16[512,12,64]{0,2,1:T(8,128)(2,1)S(1)} %bitcast.201), kind=kOutput, calls=%fused_computation.3 | convolution fusion | flops 412084224 | bytes 26787840 | tf_op jit(solution)/shard_map/bqhe,bkhe->bhqk/dot_general | solution.py:478
  334.0 6.9 %multiply_convert_fusion = bf16[12,512,512]{1,2,0:T(8,128)(2,1)S(1)} fusion(f32[12,512,512]{1,2,0:T(8,128)} %get-tuple-element.95, f32[12,512,512]{1,2,0:T(8,128)S(1)} %bitcast.162, f32[12,512]{1,0:T(8,128)S(1)} %get-tuple-element.94, f32[12,512]{1,0:T(8,128)S(1)} %copy-done.33), kind=kLoop, calls=%fused_computation.2 | loop fusion | flops 12582912 | bytes 31506432 | tf_op jit(solution)/shard_map/convert_element_type | solution.py:488
  346.2 5.8 %add_add_fusion.4 = f32[1024,768]{1,0:T(8,128)} fusion(f32[1024,768]{1,0:T(8,128)S(1)} %copy-done.11, bf16[768,2304]{1,0:T(8,128)(2,1)S(1)} %bitcast.199, f32[1024]{0:T(1024)S(1)} %negate_multiply_fusion.1, bf16[512,768]{0,1:T(8,128)(2,1)S(1)} %bitcast.202, bf16[512,768]{0,1:T(8,128)(2,1)S(1)} %bitcast.205, bf16[512,768]{0,1:T(8,128)(2,1)S(1)} %bitcast.218, ...), kind=kOutput, calls=%fused_computation.56 | convolution fusion | flops 3653763072 | bytes 14553088 | tf_op jit(solution)/shard_map/dot_general | solution.py:448
  352.0 22.9 %fusion.64 = bf16[2304]{0:T(1024)(128)(2,1)S(1)} fusion(bf16[512,768]{0,1:T(8,128)(2,1)S(1)} %bitcast.203, bf16[512,768]{0,1:T(8,128)(2,1)S(1)} %bitcast.206, bf16[512,768]{0,1:T(8,128)(2,1)S(1)} %bitcast.219, bf16[512,768]{0,1:T(8,128)(2,1)S(1)} %bitcast.212, bf16[512,768]{0,1:T(8,128)(2,1)S(1)} %bitcast.185, bf16[512,768]{0,1:T(8,128)(2,1)S(1)} %bitcast.209), kind=kLoop, calls=%fused_computation.182 | loop fusion | flops 30668544 | bytes 4723200 | tf_op jit(solution)/shard_map/reduce_sum | solution.py:884
  374.9 28.9 %convolution_convert_fusion.2 = bf16[768,2304]{1,0:T(8,128)(2,1)} fusion(bf16[1024,768]{1,0:T(8,128)(2,1)S(1)} %copy-done.50, bf16[512,768]{0,1:T(8,128)(2,1)S(1)} %bitcast.204, bf16[512,768]{0,1:T(8,128)(2,1)S(1)} %bitcast.207, bf16[512,768]{0,1:T(8,128)(2,1)S(1)} %bitcast.220, bf16[512,768]{0,1:T(8,128)(2,1)S(1)} %bitcast.213, ...), kind=kOutput, calls=%fused_computation.30 | convolution fusion | flops 3653959680 | bytes 9830400 | tf_op jit(solution)/shard_map/dot_general | solution.py:442
  405.8 2.7 slice.277
  408.5 8.9 %reshape.550 = bf16[32,24,3,768]{3,2,1,0:T(4,128)(2,1)} reshape(bf16[768,2304]{1,0:T(8,128)(2,1)} %convolution_convert_fusion.2) | data formatting | bytes 7077888 | tf_op jit(solution)/shard_map/reshape | solution.py:769
  417.4 3.0 copy.120
  430.2 108.7 %scatter_gradients.1 = (f32[304,768]{1,0:T(8,128)S(1)}, bf16[2,256,768]{2,1,0:T(8,128)(2,1)S(1)}, bf16[2,256,768]{2,1,0:T(8,128)(2,1)S(1)}, f32[2,8,768]{2,1,0:T(8,128)S(1)}) custom-call(bf16[4,8,304,768]{3,2,1,0:T(8,128)(2,1)} %constant_dynamic-update-slice_fusion.19.grads, bf16[512,768]{1,0:T(8,128)(2,1)S(1)} %get-tuple-element.68.long_out, ...), custom_call_target="tpu_custom_call" | custom-call | tf_op jit(solution)/shard_map/scatter_gradients/pallas_call | solution.py:401
  (280 shorter events, 101.1 us)
Async XLA Ops:
  0.6 108.3 %copy-start.47 = (f32[2,768]{1,0:T(2,128)S(1)}, f32[2,768]{1,0:T(2,128)}, u32[]{:S(2)}) copy-start(f32[2,768]{1,0:T(2,128)} %param.28) | copy-start | bytes 18436
  4.3 107.6 %copy-start.41 = (f32[4,128]{1,0:T(4,128)}, f32[4,128]{1,0:T(4,128)S(1)}, u32[]{:S(2)}) copy-start(f32[4,128]{1,0:T(4,128)S(1)} %get-tuple-element.58) | copy-start | bytes 6148
  135.5 7.1 %copy-start.17 = (bf16[96,8,3,768]{3,1,2,0:T(8,128)(2,1)}, bf16[96,8,3,768]{3,1,2,0:T(8,128)(2,1)S(1)}, u32[]{:S(2)}) copy-start(bf16[96,8,3,768]{3,1,2,0:T(8,128)(2,1)S(1)} %copy.136) | copy-start | bytes 10616836
  144.3 17.9 %copy-start.12 = (bf16[512,768]{0,1:T(8,128)(2,1)}, bf16[512,768]{0,1:T(8,128)(2,1)S(1)}, u32[]{:S(2)}) copy-start(bf16[512,768]{0,1:T(8,128)(2,1)S(1)} %copy.103) | copy-start | bytes 2359300
  155.3 7.0 %copy-start.14 = (bf16[512,768]{0,1:T(8,128)(2,1)}, bf16[512,768]{0,1:T(8,128)(2,1)S(1)}, u32[]{:S(2)}) copy-start(bf16[512,768]{0,1:T(8,128)(2,1)S(1)} %copy.102) | copy-start | bytes 2359300
  165.3 5.7 %copy-start.2 = (f32[12,512,512]{1,2,0:T(8,128)}, f32[12,512,512]{1,2,0:T(8,128)S(1)}, u32[]{:S(2)}) copy-start(f32[12,512,512]{1,2,0:T(8,128)S(1)} %get-tuple-element.85) | copy-start | bytes 37748740
  165.3 20.5 %slice-start.7 = ((s8[4718592]{0:T(1024)(128)(4,1)}), s8[4194304]{0:T(1024)(128)(4,1)S(1)}, s32[]{:S(2)}) async-start(s8[4718592]{0:T(1024)(128)(4,1)} %bitcast.191), calls=%async_computation.7 | async-start | bytes 8388608
  171.0 12.5 %copy-start.27 = (bf16[32,24,768]{2,1,0:T(8,128)(2,1)S(1)}, bf16[32,24,768]{2,1,0:T(8,128)(2,1)}, u32[]{:S(2)}) copy-start(bf16[32,24,768]{2,1,0:T(8,128)(2,1)} %slice.260) | copy-start | bytes 3538948
  171.0 12.5 %copy-start.29 = (bf16[96,8,4,128]{3,1,2,0:T(8,128)(2,1)S(1)}, bf16[96,8,4,128]{3,1,2,0:T(8,128)(2,1)}, u32[]{:S(2)}) copy-start(bf16[96,8,4,128]{3,1,2,0:T(8,128)(2,1)} %copy.178) | copy-start | bytes 2359300
  171.0 12.6 %copy-start.49 = (bf16[1024,768]{1,0:T(8,128)(2,1)S(1)}, bf16[1024,768]{1,0:T(8,128)(2,1)}, u32[]{:S(2)}) copy-start(bf16[1024,768]{1,0:T(8,128)(2,1)} %get-tuple-element.23) | copy-start | bytes 4718596
  171.0 14.8 %slice-start.8 = ((s8[4718592]{0:T(1024)(128)(4,1)}), s8[524288]{0:T(1024)(128)(4,1)S(1)}, s32[]{:S(2)}) async-start(s8[4718592]{0:T(1024)(128)(4,1)} %bitcast.191), calls=%async_computation.8 | async-start | bytes 1048576
  183.5 37.3 %slice-start.9 = ((s8[4718592]{0:T(1024)(128)(4,1)}), s8[4194304]{0:T(1024)(128)(4,1)S(1)}, s32[]{:S(2)}) async-start(s8[4718592]{0:T(1024)(128)(4,1)} %bitcast.195), calls=%async_computation.9 | async-start | bytes 8388608
  185.2 35.6 %copy-start.9 = (f32[1024,768]{1,0:T(8,128)}, f32[1024,768]{1,0:T(8,128)S(1)}, u32[]{:S(2)}) copy-start(f32[1024,768]{1,0:T(8,128)S(1)} %get-tuple-element.89) | copy-start | bytes 9437188
  185.8 35.1 %copy-start.37 = (f32[1024]{0:T(1024)}, f32[1024]{0:T(1024)S(1)}, u32[]{:S(2)}) copy-start(f32[1024]{0:T(1024)S(1)} %multiply_reduce_fusion.7) | copy-start | bytes 12292
  185.8 35.0 %slice-start.10 = ((s8[4718592]{0:T(1024)(128)(4,1)}), s8[524288]{0:T(1024)(128)(4,1)S(1)}, s32[]{:S(2)}) async-start(s8[4718592]{0:T(1024)(128)(4,1)} %bitcast.195), calls=%async_computation.10 | async-start | bytes 1048576
  185.8 35.0 %copy-start.46 = (f32[768]{0:T(1024)S(1)}, f32[768]{0:T(1024)}, u32[]{:S(2)}) copy-start(f32[768]{0:T(1024)} %add.162) | copy-start | bytes 9220
  220.9 6.1 %copy-start.16 = (bf16[1024,768]{1,0:T(8,128)(2,1)S(1)}, bf16[1024,768]{1,0:T(8,128)(2,1)}, u32[]{:S(2)}) copy-start(bf16[1024,768]{1,0:T(8,128)(2,1)} %get-tuple-element.25) | copy-start | bytes 4718596
  220.9 6.1 %copy-start.34 = (f32[1024]{0:T(1024)S(1)}, f32[1024]{0:T(1024)}, u32[]{:S(2)}) copy-start(f32[1024]{0:T(1024)} %add_convert_fusion.3) | copy-start | bytes 12292
  220.9 6.1 %copy-start.35 = (f32[768]{0:T(1024)S(1)}, f32[768]{0:T(1024)}, u32[]{:S(2)}) copy-start(f32[768]{0:T(1024)} %mul.258) | copy-start | bytes 9220
  220.9 6.1 %copy-start.36 = (f32[1024]{0:T(1024)S(1)}, f32[1024]{0:T(1024)}, u32[]{:S(2)}) copy-start(f32[1024]{0:T(1024)} %pad_maximum_fusion.3) | copy-start | bytes 12292
  257.4 10.0 %copy-start.10 = (f32[1024,768]{1,0:T(8,128)S(1)}, f32[1024,768]{1,0:T(8,128)}, u32[]{:S(2)}) copy-start(f32[1024,768]{1,0:T(8,128)} %copy-done.9) | copy-start | bytes 9437188
  257.4 10.0 %copy-start.52 = (bf16[1024,3072]{1,0:T(8,128)(2,1)S(1)}, bf16[1024,3072]{1,0:T(8,128)(2,1)}, u32[]{:S(2)}) copy-start(bf16[1024,3072]{1,0:T(8,128)(2,1)} %get-tuple-element.99) | copy-start | bytes 18874372
  267.4 8.5 %copy-start.38 = (f32[1024]{0:T(1024)S(1)}, f32[1024]{0:T(1024)}, u32[]{:S(2)}) copy-start(f32[1024]{0:T(1024)} %copy-done.37) | copy-start | bytes 12292
  311.4 6.8 %copy-start.4 = (f32[4,12,128,128]{2,3,1,0:T(8,128)S(1)}, f32[4,12,128,128]{2,3,1,0:T(8,128)}, u32[]{:S(2)}) copy-start(f32[4,12,128,128]{2,3,1,0:T(8,128)} %copy-done.3) | copy-start | bytes 9437188
  311.4 6.8 %copy-start.32 = (f32[4,12,128]{2,1,0:T(8,128)S(1)}, f32[4,12,128]{2,1,0:T(8,128)}, u32[]{:S(2)}) copy-start(f32[4,12,128]{2,1,0:T(8,128)} %log_add_fusion.1) | copy-start | bytes 73732
  321.1 6.6 %slice-start = ((s8[12582912]{0:T(1024)(128)(4,1)}), s8[4194304]{0:T(1024)(128)(4,1)S(1)}, s32[]{:S(2)}) async-start(s8[12582912]{0:T(1024)(128)(4,1)} %bitcast.161), calls=%async_computation | async-start | bytes 8388608
  322.1 5.6 %slice-start.1 = ((s8[12582912]{0:T(1024)(128)(4,1)}), s8[4194304]{0:T(1024)(128)(4,1)S(1)}, s32[]{:S(2)}) async-start(s8[12582912]{0:T(1024)(128)(4,1)} %bitcast.161), calls=%async_computation.1 | async-start | bytes 8388608
  334.0 6.9 %copy-start.15 = (bf16[512,768]{0,1:T(8,128)(2,1)S(1)}, bf16[512,768]{0,1:T(8,128)(2,1)}, u32[]{:S(2)}) copy-start(bf16[512,768]{0,1:T(8,128)(2,1)} %copy-done.14) | copy-start | bytes 2359300
  352.0 22.9 %copy-start.50 = (bf16[1024,768]{1,0:T(8,128)(2,1)S(1)}, bf16[1024,768]{1,0:T(8,128)(2,1)}, u32[]{:S(2)}) copy-start(bf16[1024,768]{1,0:T(8,128)(2,1)} %get-tuple-element.23) | copy-start | bytes 4718596
  417.4 6.0 %copy-start.28 = (bf16[768,768]{1,0:T(8,128)(2,1)S(1)}, bf16[768,768]{1,0:T(8,128)(2,1)}, u32[]{:S(2)}) copy-start(bf16[768,768]{1,0:T(8,128)(2,1)} %convolution_convert_fusion.4) | copy-start | bytes 3538948
  420.5 7.3 %slice-start.5 = ((s8[4718592]{0:T(1024)(128)(4,1)}), s8[4194304]{0:T(1024)(128)(4,1)S(1)}, s32[]{:S(2)}) async-start(s8[4718592]{0:T(1024)(128)(4,1)} %bitcast.187), calls=%async_computation.5 | async-start | bytes 8388608
  539.8 6.8 %copy-start.1 = (bf16[2,256,768]{2,1,0:T(8,128)(2,1)S(1)}, bf16[2,256,768]{2,1,0:T(8,128)(2,1)}, u32[]{:S(2)}) copy-start(bf16[2,256,768]{2,1,0:T(8,128)(2,1)} %copy-done) | copy-start | bytes 2359300
  (33 other events, 93.1 us)

commit v2 on v0

--- a/solution.py
+++ b/solution.py
@@ -1,14 +1,1007 @@
+import functools
 import math
 
 import jax
 import jax.numpy as jnp
 from jax import lax
+from jax.experimental import pallas as pl
+from jax.experimental.pallas import tpu as pltpu
 from jax.sharding import PartitionSpec as P
 
 HEADS = 12
-
-
 EPS = 1e-12
+MESH = pl.DeviceIdType.MESH
+
+SIZES = (80, 32, 96, 96)
+GATHER_X = (48, 16, 64, 64)
+SCATTER_X = (32, 16, 32, 32)
+
+
+FLIPS = ((0, 0), (0, 1), (1, 0), (1, 1))
+
+
+class Place:
+    def __init__(self):
+        dp = lax.axis_index("dp")
+        self.x = lax.axis_index("seq")
+        self.groups = lax.axis_size("dp") // 4
+        self.z = lax.div(dp, 4)
+        self.y = lax.rem(lax.div(dp, 2), 2)
+        self.c = lax.rem(dp, 2)
+        self.dp = dp
+
+    def at_z(self, step):
+        z = lax.rem(self.z + step, self.groups)
+        return (z * 4 + self.y * 2 + self.c, self.x)
+
+    def at_x(self):
+        return (self.dp, 1 - self.x)
+
+    def at_y(self):
+        return (self.z * 4 + (1 - self.y) * 2 + self.c, self.x)
+
+    def at_core(self):
+        return (self.z * 4 + self.y * 2 + 1 - self.c, self.x)
+
+    def slot(self, flip_y=0, flip_c=0, flip_x=0):
+        y = 1 - self.y if flip_y else self.y
+        c = 1 - self.c if flip_c else self.c
+        x = 1 - self.x if flip_x else self.x
+        return y * 4 + c * 2 + x
+
+    def z_back(self, step):
+        return lax.rem(self.z + self.groups - step, self.groups)
+
+    def partners(self):
+        return [self.at_z(step) for step in range(1, self.groups)] + [
+            self.at_x(),
+            self.at_y(),
+            self.at_core(),
+        ]
+
+    def greet(self):
+        barrier = pltpu.get_barrier_semaphore()
+        partners = self.partners()
+        for partner in partners:
+            pl.semaphore_signal(barrier, inc=1, device_id=partner, device_id_type=MESH)
+        pl.semaphore_wait(barrier, len(partners))
+
+
+class Wires:
+    def __init__(self, send, recv):
+        self.send, self.recv, self.sent, self.left = send, recv, [], set()
+
+    def put(self, src, dst, to):
+        number = len(self.sent)
+        copy = pltpu.make_async_remote_copy(
+            src_ref=src,
+            dst_ref=dst,
+            send_sem=self.send.at[number],
+            recv_sem=self.recv.at[number],
+            device_id=to,
+            device_id_type=MESH,
+        )
+        copy.start()
+        self.sent.append(copy)
+        return (number, to)
+
+    def landed(self, ticket, ref):
+        number, to = ticket
+        pltpu.make_async_remote_copy(
+            src_ref=ref,
+            dst_ref=ref,
+            send_sem=self.send.at[number],
+            recv_sem=self.recv.at[number],
+            device_id=to,
+            device_id_type=MESH,
+        ).wait_recv()
+
+    def has_left(self, ticket):
+        self.sent[ticket[0]].wait_send()
+        self.left.add(ticket[0])
+
+    def close(self):
+        for number, copy in enumerate(self.sent):
+            if number not in self.left:
+                copy.wait_send()
+
+
+class Gather:
+    def __init__(self, wires, place, slabs, wholes):
+        self.wires, self.place, self.slabs, self.wholes = wires, place, slabs, wholes
+        self.steps = place.groups
+        self.along_z, self.along_x, self.along_y = {}, {}, {}
+        self.by_x, self.by_y, self.core = {}, {}, {}
+
+    def halves(self, k):
+        some = GATHER_X[k]
+        return pl.ds(0, some), pl.ds(some, SIZES[k] - some)
+
+    def start(self, k):
+        place, wires = self.place, self.wires
+        src = self.slabs[k]
+        dst = self.wholes[k].at[place.z, place.slot()]
+        for step in range(1, self.steps):
+            self.along_z[k, step] = wires.put(src, dst, place.at_z(step))
+        self.along_x[k, 0] = wires.put(src, dst, place.at_x())
+        self.along_y[k, 0] = wires.put(src, dst, place.at_y())
+        self.core[k, 0, 0] = wires.put(src, dst, place.at_core())
+
+    def relay_z(self, k):
+        place, wires = self.place, self.wires
+        for step in range(1, self.steps):
+            ref = self.wholes[k].at[place.z_back(step), place.slot()]
+            wires.landed(self.along_z[k, step], ref)
+            self.along_x[k, step] = wires.put(ref, ref, place.at_x())
+            self.along_y[k, step] = wires.put(ref, ref, place.at_y())
+            self.core[k, 0, step] = wires.put(ref, ref, place.at_core())
+
+    def relay_plane(self, k):
+        upper, lower = self.halves(k)
+        place, wires, whole = self.place, self.wires, self.wholes[k]
+        for step in range(self.steps):
+            z = place.z_back(step)
+            slot = place.slot(flip_x=1)
+            ref = whole.at[z, slot]
+            wires.landed(self.along_x[k, step], ref)
+            half = whole.at[z, slot, upper]
+            self.by_y[k, step] = wires.put(half, half, place.at_y())
+            self.core[k, 1, step] = wires.put(ref, ref, place.at_core())
+            slot = place.slot(flip_y=1)
+            ref = whole.at[z, slot]
+            wires.landed(self.along_y[k, step], ref)
+            half = whole.at[z, slot, lower]
+            self.by_x[k, step] = wires.put(half, half, place.at_x())
+            self.core[k, 2, step] = wires.put(ref, ref, place.at_core())
+
+    def relay_corner(self, k):
+        upper, lower = self.halves(k)
+        place, wires, whole = self.place, self.wires, self.wholes[k]
+        slot = place.slot(flip_x=1, flip_y=1)
+        for step in range(self.steps):
+            z = place.z_back(step)
+            wires.landed(self.by_y[k, step], whole.at[z, slot, upper])
+            wires.landed(self.by_x[k, step], whole.at[z, slot, lower])
+            ref = whole.at[z, slot]
+            self.core[k, 3, step] = wires.put(ref, ref, place.at_core())
+
+    def finish(self, k):
+        place = self.place
+        for part, (flip_y, flip_x) in enumerate(FLIPS):
+            slot = place.slot(flip_y=flip_y, flip_c=1, flip_x=flip_x)
+            for step in range(self.steps):
+                ref = self.wholes[k].at[place.z_back(step), slot]
+                self.wires.landed(self.core[k, part, step], ref)
+
+
+class Scatter:
+    def __init__(self, wires, place, grads, from_core, from_x, from_y, last_x, last_y, from_z):
+        self.wires, self.place, self.grads = wires, place, grads
+        self.from_core, self.from_x, self.from_y = from_core, from_x, from_y
+        self.last_x, self.last_y, self.from_z = last_x, last_y, from_z
+        self.steps = place.groups
+        self.core, self.first, self.second, self.third = {}, {}, {}, {}
+
+    def halves(self, k):
+        some = SCATTER_X[k]
+        return pl.ds(0, some), pl.ds(some, SIZES[k] - some)
+
+    def own(self, k, part, rows):
+        flip_y, flip_x = FLIPS[part]
+        return self.grads[k].at[:, self.place.slot(flip_y=flip_y, flip_x=flip_x), rows]
+
+    def send_core(self, k):
+        place = self.place
+        for part in (3, 1, 2, 0):
+            flip_y, flip_x = FLIPS[part]
+            slot = place.slot(flip_y=flip_y, flip_c=1, flip_x=flip_x)
+            self.core[k, part] = self.wires.put(
+                self.grads[k].at[:, slot], self.from_core[k].at[part], place.at_core()
+            )
+
+    def add(self, into, other):
+        def one(z, carry):
+            total = into[z].astype(jnp.float32) + other[z].astype(jnp.float32)
+            into[z] = total.astype(into.dtype)
+            return carry
+
+        lax.fori_loop(0, self.steps, one, 0)
+
+    def after_core(self, k):
+        upper, lower = self.halves(k)
+        whole = pl.ds(0, SIZES[k])
+        wires, place = self.wires, self.place
+        for part in (3, 1, 2, 0):
+            wires.landed(self.core[k, part], self.from_core[k].at[part])
+            self.add(self.own(k, part, whole), self.from_core[k].at[part])
+            if part == 3:
+                self.first[k, "x", 1] = wires.put(
+                    self.own(k, 3, upper), self.from_x[k].at[1], place.at_x()
+                )
+                self.first[k, "y", 1] = wires.put(
+                    self.own(k, 3, lower), self.from_y[k].at[1], place.at_y()
+                )
+            elif part == 1:
+                self.first[k, "x", 0] = wires.put(
+                    self.own(k, 1, upper), self.from_x[k].at[0], place.at_x()
+                )
+            elif part == 2:
+                self.first[k, "y", 0] = wires.put(
+                    self.own(k, 2, lower), self.from_y[k].at[0], place.at_y()
+                )
+
+    def after_first(self, k):
+        upper, lower = self.halves(k)
+        wires, place = self.wires, self.place
+        wires.landed(self.first[k, "x", 1], self.from_x[k].at[1])
+        self.add(self.own(k, 2, upper), self.from_x[k].at[1])
+        self.second[k, "y"] = wires.put(self.own(k, 2, upper), self.last_y[k], place.at_y())
+        wires.landed(self.first[k, "y", 1], self.from_y[k].at[1])
+        self.add(self.own(k, 1, lower), self.from_y[k].at[1])
+        self.second[k, "x"] = wires.put(self.own(k, 1, lower), self.last_x[k], place.at_x())
+        wires.landed(self.first[k, "x", 0], self.from_x[k].at[0])
+        self.add(self.own(k, 0, upper), self.from_x[k].at[0])
+        wires.landed(self.first[k, "y", 0], self.from_y[k].at[0])
+        self.add(self.own(k, 0, lower), self.from_y[k].at[0])
+
+    def after_second(self, k):
+        upper, lower = self.halves(k)
+        wires, place = self.wires, self.place
+        wires.landed(self.second[k, "y"], self.last_y[k])
+        self.add(self.own(k, 0, upper), self.last_y[k])
+        wires.landed(self.second[k, "x"], self.last_x[k])
+        self.add(self.own(k, 0, lower), self.last_x[k])
+        for step in range(1, self.steps):
+            z = lax.rem(place.z + step, self.steps)
+            self.third[k, step] = wires.put(
+                self.grads[k].at[z, place.slot()], self.from_z[k].at[step - 1], place.at_z(step)
+            )
+
+    def finish(self, k):
+        place = self.place
+        total = self.grads[k][place.z, place.slot()].astype(jnp.float32)
+        for step in range(1, self.steps):
+            self.wires.landed(self.third[k, step], self.from_z[k].at[step - 1])
+            total = total + self.from_z[k][step - 1].astype(jnp.float32)
+        return total
+
+
+def times(a, b):
+    return lax.dot_general(a, b, (((1,), (0,)), ((), ())), preferred_element_type=jnp.float32)
+
+
+def times_turned(a, b):
+    return lax.dot_general(a, b, (((1,), (1,)), ((), ())), preferred_element_type=jnp.float32)
+
+
+def turned_times(a, b):
+    return lax.dot_general(a, b, (((0,), (0,)), ((), ())), preferred_element_type=jnp.float32)
+
+
+def aligned(index, size):
+    return pl.ds(pl.multiple_of(index * size, size), size)
+
+
+def head_masks(lanes, head_dim):
+    lane = lax.broadcasted_iota(jnp.int32, (1, lanes), 1)
+    return [
+        jnp.where((lane >= h * head_dim) & (lane < (h + 1) * head_dim), 1.0, 0.0).astype(jnp.bfloat16)
+        for h in range(lanes // head_dim)
+    ]
+
+
+def gelu_and_slope(u):
+    near = 1.0 / (1.0 + (0.3275911 * math.sqrt(0.5)) * jnp.abs(u))
+    bell = jnp.exp(-0.5 * (u * u))
+    series = near * (
+        0.127414796
+        + near * (-0.142248368 + near * (0.7107068705 + near * (-0.7265760135 + near * 0.5307027145)))
+    )
+    tail = series * bell
+    below = jnp.where(u < 0.0, tail, 1.0 - tail)
+    return u * below, below + u * (bell * (1.0 / math.sqrt(2.0 * math.pi)))
+
+
+def assemble(source, first, blocks, target):
+    per_z, size = source.shape[1] // 2, 24
+
+    def one(i, carry):
+        z, pair = lax.div(i, per_z), lax.rem(i, per_z)
+        left = source[z, 2 * pair].astype(jnp.float32)
+        right = source[z, 2 * pair + 1].astype(jnp.float32)
+        for b in range(blocks):
+            rows = slice(first + b * size, first + (b + 1) * size)
+            both = jnp.concatenate([left[rows], right[rows]], axis=0)
+            target[b, aligned(i, 2 * size), :] = both.astype(target.dtype)
+        return carry
+
+    lax.fori_loop(0, source.shape[0] * per_z, one, 0)
+
+
+def sum_slabs(source, first):
+    def one(i, total):
+        per_z = source.shape[1]
+        slab = source[lax.div(i, per_z), lax.rem(i, per_z)].astype(jnp.float32)
+        return total + slab[first : first + 8]
+
+    count = source.shape[0] * source.shape[1]
+    return lax.fori_loop(0, count, one, jnp.zeros((8, source.shape[-1]), jnp.float32))
+
+
+def normalize(row_data):
+    center = row_data - jnp.mean(row_data, axis=-1, keepdims=True)
+    spread = jnp.mean(center * center, axis=-1, keepdims=True)
+    scale = lax.rsqrt(spread + EPS)
+    return center * scale, scale
+
+
+def weights_forward(queries, keys_all, live):
+    scores = jnp.where(live, times_turned(queries, keys_all), -1e30)
+    exponent = jnp.exp(scores - jnp.max(scores, axis=-1, keepdims=True))
+    return (exponent * (1.0 / jnp.sum(exponent, axis=-1, keepdims=True))).astype(jnp.bfloat16)
+
+
+def forward_kernel(
+    limits, slab0, slab1, slab2, slab3, short_tok, long_tok, short_cot, long_cot, short_pool, pool,
+    out_down, out_wq, out_wu, out_rows, out_cot, out_qkv, out_short_probs, out_long_probs, out_mixed,
+    out_first, out_hat, out_scale, out_low, out_acted, out_slope, vectors, share,
+    whole0, whole1, whole2, wq, wu, rows_in, qkv, short_probs, long_probs, mixed,
+    first, hat, scale, low, acted, slope, pool_in,
+    send, recv, here,
+):
+    place = Place()
+    x, other = place.x, 1 - place.x
+    short_rows, half = short_tok.shape[0], long_tok.shape[1]
+    total_rows, width = rows_in.shape
+    long_rows = 2 * half
+    cap = short_probs.shape[-1]
+    count = short_rows // cap
+    mine = pl.ds(pl.multiple_of(short_rows + x * half, half), half)
+    theirs = pl.ds(pl.multiple_of(short_rows + other * half, half), half)
+    slabs = (slab0, slab1, slab2, slab3)
+    wholes = (whole0, whole1, whole2, out_down)
+    local = []
+
+    def move(src, dst):
+        copy = pltpu.make_async_copy(src, dst, here.at[len(local)])
+        copy.start()
+        local.append(copy)
+        return copy
+
+    for k in range(4):
+        move(slabs[k], wholes[k].at[place.z, place.slot()])
+    for src, dst in (
+        (short_tok, rows_in.at[pl.ds(0, short_rows)]),
+        (long_tok.at[x], rows_in.at[mine]),
+        (pool.at[x], pool_in.at[x]),
+        (short_cot, out_cot.at[pl.ds(0, short_rows)]),
+        (long_cot.at[x], out_cot.at[mine]),
+    ):
+        move(src, dst)
+    arrived = len(local)
+    place.greet()
+    wires = Wires(send, recv)
+    net = Gather(wires, place, slabs, wholes)
+    net.start(0)
+    tok = wires.put(long_tok.at[other], rows_in.at[mine], place.at_x())
+    pooled = wires.put(pool.at[other], pool_in.at[x], place.at_x())
+    net.start(1)
+    net.relay_z(0)
+    net.start(2)
+    net.relay_plane(0)
+    net.relay_corner(0)
+    net.relay_z(1)
+    net.relay_plane(1)
+    net.relay_corner(1)
+    net.start(3)
+    for copy in local:
+        copy.wait()
+    net.finish(0)
+    assemble(whole0, 0, 3, wq)
+    vectors[0:8, :] = sum_slabs(whole0, 72)
+    wires.landed(tok, rows_in.at[theirs])
+    net.relay_z(2)
+
+    head_dim = width // HEADS
+    score_scale = 1.0 / math.sqrt(head_dim)
+
+    def project(i, carry):
+        rows = aligned(i, 256)
+        data = rows_in[rows, :]
+        queries = times(data, wq[0]) + vectors[0:1, :]
+        qkv[0, rows, :] = (queries.astype(jnp.bfloat16).astype(jnp.float32) * score_scale).astype(jnp.bfloat16)
+        qkv[1, rows, :] = times(data, wq[1]).astype(jnp.bfloat16)
+        qkv[2, rows, :] = (times(data, wq[2]) + vectors[1:2, :]).astype(jnp.bfloat16)
+        return carry
+
+    lax.fori_loop(0, total_rows // 256, project, 0)
+    move(qkv, out_qkv)
+    move(rows_in, out_rows)
+
+    wires.landed(pooled, pool_in.at[other])
+    place_in_block = lax.broadcasted_iota(jnp.int32, (1, cap), 1)
+    chosen = []
+    for block in range(total_rows // cap):
+        if block < count:
+            mask, start = short_pool[block : block + 1, :], 0
+        else:
+            step = block - count
+            per_half = half // cap
+            mask, start = pool_in[step // per_half, step % per_half : step % per_half + 1, :], step * cap
+        live = place_in_block < limits[block]
+        keep = live & ((mask > 0) | (place_in_block + start == 0))
+        chosen.append(jnp.where(keep, 1.0, 0.0))
+    for block in range(count):
+        share[block : block + 1, :] = chosen[block] / jnp.sum(chosen[block], axis=-1, keepdims=True)
+    long_total = sum(jnp.sum(row, axis=-1, keepdims=True) for row in chosen[count:])
+    for block in range(count, total_rows // cap):
+        share[block : block + 1, :] = chosen[block] / long_total
+    masks = head_masks(2 * head_dim, head_dim)
+    keep_first = lax.broadcasted_iota(jnp.int32, (1, 2 * head_dim), 1) < head_dim
+    short_live = [place_in_block < limits[i] for i in range(count)]
+    long_live = lax.broadcasted_iota(jnp.int32, (1, long_rows), 1) < limits[count]
+
+    def attend(pair, carry):
+        lanes = aligned(pair, 2 * head_dim)
+        for i in range(count):
+            rows = pl.ds(i * cap, cap)
+            queries, keys_all, values = qkv[0, rows, lanes], qkv[1, rows, lanes], qkv[2, rows, lanes]
+            parts = []
+            for h in range(2):
+                probs = weights_forward(queries * masks[h], keys_all, short_live[i])
+                short_probs[i, 2 * pair + h] = probs
+                parts.append(times(probs, values))
+            mixed[rows, lanes] = jnp.where(keep_first, parts[0], parts[1]).astype(jnp.bfloat16)
+        rows = pl.ds(short_rows, long_rows)
+        keys_all, values = qkv[1, rows, lanes], qkv[2, rows, lanes]
+        for block in range(long_rows // 256):
+            inner = pl.ds(block * 256, 256)
+            rows = pl.ds(short_rows + block * 256, 256)
+            queries = qkv[0, rows, lanes]
+            parts = []
+            for h in range(2):
+                probs = weights_forward(queries * masks[h], keys_all, long_live)
+                long_probs[2 * pair + h, inner, :] = probs
+                parts.append(times(probs, values))
+            mixed[rows, lanes] = jnp.where(keep_first, parts[0], parts[1]).astype(jnp.bfloat16)
+        return carry
+
+    pairs = width // (2 * head_dim)
+    lax.fori_loop(0, pairs // 3, attend, 0)
+    net.relay_plane(2)
+    lax.fori_loop(pairs // 3, 2 * pairs // 3, attend, 0)
+    net.relay_corner(2)
+    net.relay_z(3)
+    cot = wires.put(long_cot.at[other], out_cot.at[mine], place.at_x())
+    lax.fori_loop(2 * pairs // 3, pairs, attend, 0)
+    move(short_probs, out_short_probs)
+    move(long_probs, out_long_probs)
+    move(mixed, out_mixed)
+    net.finish(1)
+    assemble(whole1, 0, 1, wq.at[pl.ds(3, 1)])
+    vectors[8:16, :] = sum_slabs(whole1, 24)
+    move(wq, out_wq)
+    net.relay_plane(3)
+
+    def attach(i, carry):
+        rows = aligned(i, 256)
+        first_in = rows_in[rows, :].astype(jnp.float32) + (times(mixed[rows, :], wq[3]) + vectors[2:3, :])
+        normal, factor = normalize(first_in)
+        out = normal * vectors[4:5, :] + vectors[6:7, :]
+        first[rows, :] = out
+        low[rows, :] = out.astype(jnp.bfloat16)
+        hat[rows, :] = normal.astype(jnp.bfloat16)
+        scale[rows, :] = jnp.broadcast_to(factor, (256, scale.shape[1]))
+        return carry
+
+    lax.fori_loop(0, total_rows // 256, attach, 0)
+    move(first, out_first)
+    move(low, out_low)
+    move(hat, out_hat)
+    move(scale, out_scale)
+    net.finish(2)
+    assemble(whole2, 0, 4, wu)
+    move(wu, out_wu)
+
+    def expand(i, carry):
+        j, rows = lax.div(i, 4), aligned(lax.rem(i, 4), 256)
+        inner = times(low[rows, :], wu[j]) + vectors[pl.ds(8 + j, 1), :]
+        value, grad = gelu_and_slope(inner)
+        acted[j, rows, :] = value.astype(jnp.bfloat16)
+        slope[j, rows, :] = grad.astype(jnp.bfloat16)
+        return carry
+
+    lax.fori_loop(0, 8, expand, 0)
+    net.relay_corner(3)
+    lax.fori_loop(8, 16, expand, 0)
+    move(acted, out_acted)
+    move(slope, out_slope)
+    net.finish(3)
+    wires.landed(cot, out_cot.at[theirs])
+    wires.close()
+    for copy in local[arrived:]:
+        copy.wait()
+
+
+def forward(limits, slabs, short_tok, long_tok, short_cot, long_cot, short_pool, pool, groups):
+    short_rows, width = short_tok.shape
+    half = long_tok.shape[1]
+    long_rows = 2 * half
+    rows = short_rows + long_rows
+    count, cap = short_pool.shape
+    inner = 4 * width
+    copies = 4 * ((groups - 1) + 4 * groups + 4 * groups) + 3
+    low = jnp.bfloat16
+    shape = jax.ShapeDtypeStruct
+    outs = (
+        shape((groups, 8, SIZES[3], width), low),
+        shape((4, width, width), low),
+        shape((4, width, width), low),
+        shape((rows, width), low),
+        shape((rows, width), low),
+        shape((3, rows, width), low),
+        shape((count, HEADS, cap, cap), low),
+        shape((HEADS, long_rows, long_rows), low),
+        shape((rows, width), low),
+        shape((rows, width), jnp.float32),
+        shape((rows, width), low),
+        shape((rows, 128), jnp.float32),
+        shape((rows, width), low),
+        shape((inner // width, rows, width), low),
+        shape((inner // width, rows, width), low),
+        shape((16, width), jnp.float32),
+        shape((rows // cap, cap), jnp.float32),
+    )
+    anywhere, near = pl.BlockSpec(memory_space=pl.ANY), pl.BlockSpec(memory_space=pltpu.VMEM)
+    kept = [pltpu.VMEM(out.shape, out.dtype) for out in (outs[1:4] + outs[5:15])]
+    return pl.pallas_call(
+        forward_kernel,
+        name="forward",
+        out_shape=outs,
+        in_specs=[pl.BlockSpec(memory_space=pltpu.SMEM)] + [anywhere] * 8 + [near] + [anywhere],
+        out_specs=[anywhere] * 15 + [near] * 2,
+        scratch_shapes=[pltpu.VMEM((groups, 8, SIZES[k], width), low) for k in range(3)]
+        + kept
+        + [
+            pltpu.VMEM(pool.shape, pool.dtype),
+            pltpu.SemaphoreType.DMA((copies,)),
+            pltpu.SemaphoreType.DMA((copies,)),
+            pltpu.SemaphoreType.DMA((24,)),
+        ],
+        compiler_params=pltpu.CompilerParams(
+            collective_id=0, has_side_effects=True, vmem_limit_bytes=60 * 1024 * 1024
+        ),
+    )(limits, *slabs, short_tok, long_tok, short_cot, long_cot, short_pool, pool)
+
+
+def backward_kernel(
+    limits, vectors, share, short_pool_cot, long_pool_cot,
+    in_down, in_wq, in_wu, in_rows, in_cot, in_qkv, in_short_probs, in_long_probs, in_mixed,
+    in_first, in_hat, in_scale, in_low, in_acted, in_slope,
+    short_out, long_out, short_grad, long_grad, short_pooled, long_pooled,
+    grad_qkv, grad_out, grad_up, grad_down, grad_vectors, grad_up_vector,
+    wide, pair, w_up, w_far, hat, sums, branch, low, scale, halves, probs_short,
+    vector_sums, pool_cots, pooled_rows, pooled_own, pooled_far,
+    grads0, grads1, grads2, grads3, core0, core1, core2, core3,
+    x0, x1, x2, x3, y0, y1, y2, y3, lx0, lx1, lx2, lx3, ly0, ly1, ly2, ly3, z0, z1, z2, z3,
+    send, recv, here, blocks, fetch,
+):
+    place = Place()
+    x, other = place.x, 1 - place.x
+    total_rows, width = sums.shape
+    short_rows = short_out.shape[0]
+    count, cap = probs_short.shape[1], probs_short.shape[-1]
+    long_rows = total_rows - short_rows
+    half = long_rows // 2
+    head_dim = width // HEADS
+    steps = total_rows // 256
+    low_type = jnp.bfloat16
+    local = []
+
+    def move(src, dst):
+        copy = pltpu.make_async_copy(src, dst, here.at[len(local)])
+        copy.start()
+        local.append(copy)
+        return copy
+
+    load_down = [move(in_down.at[j], w_far.at[j]) for j in range(4)]
+
+    def block_copies(i):
+        rows = aligned(i, 256)
+        return (
+            pltpu.make_async_copy(in_acted.at[:, rows], wide.at[:, rows], blocks.at[0, i]),
+            pltpu.make_async_copy(in_first.at[rows], sums.at[rows], blocks.at[1, i]),
+            pltpu.make_async_copy(in_cot.at[rows], branch.at[rows], blocks.at[2, i]),
+        )
+
+    for i in range(steps):
+        for copy in block_copies(i):
+            copy.start()
+    load_slope = [move(in_slope.at[0], pair.at[0])]
+    load_low = move(in_low, low)
+    load_up = move(in_wu, w_up)
+    load_hat, load_scale = move(in_hat, hat), move(in_scale, scale)
+    vector_sums[...] = jnp.zeros_like(vector_sums)
+    pool_cots[0:count, :] = short_pool_cot[...]
+    pool_cots[count : 2 * count, :] = jnp.broadcast_to(long_pool_cot[pl.ds(x, 1), :], (count, width))
+    place.greet()
+    wires = Wires(send, recv)
+    net = Scatter(
+        wires, place, (grads0, grads1, grads2, grads3), (core0, core1, core2, core3),
+        (x0, x1, x2, x3), (y0, y1, y2, y3), (lx0, lx1, lx2, lx3), (ly0, ly1, ly2, ly3), (z0, z1, z2, z3),
+    )
+    for copy in load_down:
+        copy.wait()
+    tall = lax.broadcasted_iota(jnp.int32, (256, 1), 0)
+    diagonal = lax.broadcasted_iota(jnp.int32, (cap, cap), 0) == lax.broadcasted_iota(jnp.int32, (cap, cap), 1)
+
+    def add_vector(row, rows):
+        vector_sums[row : row + 1, :] += jnp.sum(rows, axis=0, keepdims=True)
+
+    def second(i, carry):
+        rows = aligned(i, 256)
+        for copy in block_copies(i):
+            copy.wait()
+        product = times(wide[0, rows, :], w_far[0])
+        for j in range(1, 4):
+            product += times(wide[j, rows, :], w_far[j])
+        normal, factor = normalize(sums[rows, :] + (product + vectors[3:4, :]))
+        live = tall < jnp.where(tall < cap, limits[2 * i], limits[2 * i + 1] + cap)
+        final = jnp.where(live, normal * vectors[5:6, :] + vectors[7:8, :], 0.0)
+        pair[1, rows, :] = final.astype(low_type)
+        spread = []
+        for part in range(2):
+            share_row = share[pl.ds(2 * i + part, 1), :]
+            column = jnp.sum(jnp.where(diagonal, share_row, 0.0), axis=1, keepdims=True)
+            piece = final[part * cap : (part + 1) * cap]
+            pooled_rows[pl.ds(2 * i + part, 1), :] = jnp.sum(piece * column, axis=0, keepdims=True)
+            spread.append(column * pool_cots[pl.ds(2 * i + part, 1), :])
+        grad_final = jnp.where(live, branch[rows, :].astype(jnp.float32), 0.0) + jnp.concatenate(spread, axis=0)
+        add_vector(5, grad_final * normal)
+        add_vector(7, grad_final)
+        scaled = grad_final * vectors[5:6, :]
+        mean_one = jnp.mean(scaled, axis=-1, keepdims=True)
+        mean_two = jnp.mean(scaled * normal, axis=-1, keepdims=True)
+        grad_second = factor * (scaled - mean_one - normal * mean_two)
+        sums[rows, :] = grad_second
+        grad_branch = grad_second.astype(low_type)
+        branch[rows, :] = grad_branch
+        add_vector(3, grad_branch.astype(jnp.float32))
+        return carry
+
+    lax.fori_loop(0, steps, second, 0)
+    short_pooled[...] = pooled_rows[0:count, :]
+    own_pooled = jnp.sum(pooled_rows[count : 2 * count, :], axis=0, keepdims=True)
+    pooled_own[...] = jnp.broadcast_to(own_pooled, pooled_own.shape)
+    long_pooled[pl.ds(x, 1), :] = own_pooled
+    mine = pl.ds(pl.multiple_of(short_rows + x * half, half), half)
+    theirs = pl.ds(pl.multiple_of(short_rows + other * half, half), half)
+    out_copies = [
+        move(pair.at[1, pl.ds(0, short_rows)], short_out),
+        move(pair.at[1, mine], long_out.at[x]),
+    ]
+
+    def down_step(i, carry):
+        j, part = lax.div(i, 2), lax.rem(i, 2)
+        product = turned_times(wide[j, :, aligned(part, width // 2)], branch[...])
+        grads3[j, aligned(part, 4)] = product.reshape(4, SIZES[3], width).astype(low_type)
+        return carry
+
+    lax.fori_loop(0, 8, down_step, 0)
+    net.send_core(3)
+    swap_out = wires.put(pair.at[1, theirs], long_out.at[x], place.at_x())
+    swap_pooled = wires.put(pooled_own, pooled_far, place.at_x())
+
+    def inner_block(j):
+        def inner(i, carry):
+            rows = aligned(i, 256)
+            product = times_turned(branch[rows, :], w_far[j]) * pair[j % 2, rows, :].astype(jnp.float32)
+            grad_inner = product.astype(low_type)
+            wide[j, rows, :] = grad_inner
+            add_vector(8 + j, grad_inner.astype(jnp.float32))
+            return carry
+
+        lax.fori_loop(0, steps, inner, 0)
+
+    load_slope[0].wait()
+    inner_block(0)
+    for copy in out_copies:
+        copy.wait()
+    wires.has_left(swap_out)
+    load_slope.append(move(in_slope.at[1], pair.at[1]))
+    load_slope.append(move(in_slope.at[2], pair.at[0]))
+    load_slope[1].wait()
+    inner_block(1)
+    load_slope.append(move(in_slope.at[3], pair.at[1]))
+    net.after_core(3)
+    load_slope[2].wait()
+    inner_block(2)
+    load_mixed = move(in_mixed, pair.at[0])
+    load_slope[3].wait()
+    inner_block(3)
+    load_wq = move(in_wq, w_far)
+
+    def pack(target, first, r, tail):
+        def one(i, carry):
+            rows = pl.ds(pl.multiple_of(i * 24, 8), 24)
+            pieces = [halves[0, rows, :], halves[1, rows, :]] if tail is None else [halves[0, rows, :], tail]
+            data = jnp.concatenate(pieces, axis=0).astype(low_type)
+            target[2 * r + lax.div(i, 8), lax.rem(i, 8), first : first + data.shape[0], :] = data
+            return carry
+
+        lax.fori_loop(0, 16, one, 0)
+
+    def up_step(i, carry):
+        r, both = lax.div(i, 2), lax.rem(i, 2)
+        data = low[:, aligned(r, width // 2)]
+        halves[0] = turned_times(data, wide[2 * both])
+        halves[1] = turned_times(data, wide[2 * both + 1])
+
+        def one(k, carry):
+            rows = pl.ds(pl.multiple_of(k * 24, 8), 24)
+            data = jnp.concatenate([halves[0, rows, :], halves[1, rows, :]], axis=0)
+            grads2[2 * r + lax.div(k, 8), lax.rem(k, 8), aligned(both, 48), :] = data.astype(low_type)
+            return carry
+
+        return lax.fori_loop(0, 16, one, carry)
+
+    load_low.wait()
+    lax.fori_loop(0, 4, up_step, 0)
+    net.send_core(2)
+
+    load_up.wait()
+    load_hat.wait()
+    load_scale.wait()
+
+    def first_back(i, carry):
+        rows = aligned(i, 256)
+        grad_first = sums[rows, :]
+        for j in range(4):
+            grad_first += times_turned(wide[j, rows, :], w_up[j])
+        normal = hat[rows, :].astype(jnp.float32)
+        add_vector(4, grad_first * normal)
+        add_vector(6, grad_first)
+        scaled = grad_first * vectors[4:5, :]
+        mean_one = jnp.mean(scaled, axis=-1, keepdims=True)
+        mean_two = jnp.mean(scaled * normal, axis=-1, keepdims=True)
+        grad_in = scale[rows, 0:1] * (scaled - mean_one - normal * mean_two)
+        sums[rows, :] = grad_in
+        grad_attn = grad_in.astype(low_type)
+        branch[rows, :] = grad_attn
+        add_vector(2, grad_attn.astype(jnp.float32))
+        return carry
+
+    lax.fori_loop(0, steps, first_back, 0)
+    load_qkv = move(in_qkv, wide.at[pl.ds(0, 3)])
+    load_rows = move(in_rows, wide.at[3])
+    net.after_core(2)
+    net.after_first(3)
+
+    load_mixed.wait()
+    load_wq.wait()
+    for r in range(2):
+        halves[0] = turned_times(pair[0, :, r * (width // 2) : (r + 1) * (width // 2)], branch[...])
+        pack(grads1, 0, r, vector_sums[8:16, :])
+    net.send_core(1)
+
+    def mixed_back(i, carry):
+        rows = aligned(i, 256)
+        pair[1, rows, :] = times_turned(branch[rows, :], w_far[3]).astype(low_type)
+        return carry
+
+    lax.fori_loop(0, steps, mixed_back, 0)
+
+    def probs_copies(p, slot):
+        lanes = pl.ds(2 * p, 2)
+        return (
+            pltpu.make_async_copy(in_short_probs.at[:, lanes], probs_short.at[slot], fetch.at[0, slot]),
+            pltpu.make_async_copy(
+                in_long_probs.at[lanes],
+                w_up.at[pl.ds(2 * slot, 2), pl.ds(0, long_rows), pl.ds(0, long_rows)],
+                fetch.at[1, slot],
+            ),
+        )
+
+    for copy in probs_copies(0, 0):
+        copy.start()
+    load_qkv.wait()
+    score_scale = 1.0 / math.sqrt(head_dim)
+    masks = head_masks(2 * head_dim, head_dim)
+    pairs = width // (2 * head_dim)
+
+    def attend_back(rows, lanes, queries_rows, probs_of, keys_all, values, carry_k, carry_v):
+        queries, grad_mixed = wide[0, queries_rows, lanes], pair[1, queries_rows, lanes]
+        overlap = grad_mixed.astype(jnp.float32) * pair[0, queries_rows, lanes].astype(jnp.float32)
+        grad_queries = None
+        for h in range(2):
+            center = jnp.sum(overlap * masks[h].astype(jnp.float32), axis=-1, keepdims=True)
+            grad_head = grad_mixed * masks[h]
+            probs = probs_of(h)
+            grad_probs = times_turned(grad_head, values)
+            grad_scores = (probs.astype(jnp.float32) * (grad_probs - center)).astype(low_type)
+            part = times(grad_scores, keys_all * masks[h])
+            grad_queries = part if grad_queries is None else grad_queries + part
+            part = turned_times(grad_scores, queries * masks[h])
+            carry_k = part if carry_k is None else carry_k + part
+            part = turned_times(probs, grad_head)
+            carry_v = part if carry_v is None else carry_v + part
+        wide[0, queries_rows, lanes] = (grad_queries * score_scale).astype(low_type)
+        return carry_k, carry_v
+
+    def attention_back(p, carry):
+        slot = lax.rem(p, 2)
+        for copy in probs_copies(p, slot):
+            copy.wait()
+
+        @pl.when(p + 1 < pairs)
+        def _():
+            for copy in probs_copies(p + 1, 1 - slot):
+                copy.start()
+
+        lanes = aligned(p, 2 * head_dim)
+        for i in range(count):
+            rows = pl.ds(i * cap, cap)
+            grad_k, grad_v = attend_back(
+                rows, lanes, rows, lambda h, i=i: probs_short[slot, i, h],
+                wide[1, rows, lanes], wide[2, rows, lanes], None, None,
+            )
+            wide[1, rows, lanes] = grad_k.astype(low_type)
+            wide[2, rows, lanes] = grad_v.astype(low_type)
+        rows = pl.ds(short_rows, long_rows)
+        keys_all, values = wide[1, rows, lanes], wide[2, rows, lanes]
+        grad_k, grad_v = None, None
+        for block in range(long_rows // 256):
+            inner = pl.ds(block * 256, 256)
+            grad_k, grad_v = attend_back(
+                rows, lanes, pl.ds(short_rows + block * 256, 256),
+                lambda h, inner=inner: w_up[2 * slot + h, inner, 0:long_rows],
+                keys_all, values, grad_k, grad_v,
+            )
+        wide[1, rows, lanes] = grad_k.astype(low_type)
+        wide[2, rows, lanes] = grad_v.astype(low_type)
+        return carry
+
+    lax.fori_loop(0, pairs // 3, attention_back, 0)
+    net.after_second(3)
+    net.after_core(1)
+    lax.fori_loop(pairs // 3, 2 * pairs // 3, attention_back, 0)
+    net.after_first(2)
+    lax.fori_loop(2 * pairs // 3, pairs, attention_back, 0)
+    net.after_first(1)
+    net.after_second(2)
+
+    def bias_sums(i, carry):
+        rows = aligned(i, 256)
+        add_vector(0, wide[0, rows, :].astype(jnp.float32))
+        add_vector(1, wide[2, rows, :].astype(jnp.float32))
+        return carry
+
+    lax.fori_loop(0, steps, bias_sums, 0)
+    load_rows.wait()
+    for r in range(2):
+        data = wide[3, :, r * (width // 2) : (r + 1) * (width // 2)]
+        halves[0] = turned_times(data, wide[0])
+        halves[1] = turned_times(data, wide[1])
+        pack(grads0, 0, r, None)
+        halves[0] = turned_times(data, wide[2])
+        pack(grads0, 48, r, vector_sums[0:8, :])
+    net.send_core(0)
+    net.after_second(1)
+
+    def tokens_back(rows):
+        grad_in = sums[rows, :]
+        for b in range(3):
+            grad_in += times_turned(wide[b, rows, :], w_far[b])
+        return grad_in
+
+    far_low, far_in = low.at[pl.ds(0, half)], low.at[pl.ds(half, half)]
+    far_low[...] = tokens_back(theirs).astype(low_type)
+    swap_grad = wires.put(far_low, far_in, place.at_x())
+    net.after_core(0)
+
+    def tokens_step(i, carry):
+        rows = pl.ds(pl.multiple_of(jnp.where(i < 2, i * 256, short_rows + x * half), 256), 256)
+        sums[rows, :] = tokens_back(rows)
+        return carry
+
+    lax.fori_loop(0, 3, tokens_step, 0)
+    move(sums.at[pl.ds(0, short_rows)], short_grad)
+    move(sums.at[mine], long_grad.at[x])
+    net.after_first(0)
+    grad_down[...] = net.finish(3)
+    total = net.finish(2)
+    for j in range(4):
+        grad_up[:, j * width : (j + 1) * width] = total[24 * j : 24 * j + 24]
+    total = net.finish(1)
+    grad_out[...] = total[0:24]
+    grad_up_vector[...] = total[24:32]
+    wires.landed(swap_pooled, pooled_far)
+    long_pooled[pl.ds(other, 1), :] = pooled_far[0:1, :]
+    wires.landed(swap_grad, far_in)
+    sums[theirs, :] = far_in[...].astype(jnp.float32)
+    move(sums.at[theirs], long_grad.at[other])
+    wires.landed(swap_out, long_out.at[other])
+    net.after_second(0)
+    total = net.finish(0)
+    for b in range(3):
+        grad_qkv[:, b * width : (b + 1) * width] = total[24 * b : 24 * b + 24]
+    grad_vectors[...] = total[72:80]
+    wires.close()
+    for copy in local[-3:]:
+        copy.wait()
+
+
+def backward(limits, vectors, share, short_pool_cot, long_pool_cot, arrays, groups):
+    width = vectors.shape[1]
+    rows = arrays[3].shape[0]
+    count, _, cap, _ = arrays[6].shape
+    short_rows = count * cap
+    half = (rows - short_rows) // 2
+    low, wide_type = jnp.bfloat16, jnp.float32
+    shape = jax.ShapeDtypeStruct
+    rows24 = 24
+    outs = (
+        shape((short_rows, width), low),
+        shape((2, half, width), low),
+        shape((short_rows, width), wide_type),
+        shape((2, half, width), wide_type),
+        shape((count, width), wide_type),
+        shape((2, width), wide_type),
+        shape((rows24, 3 * width), wide_type),
+        shape((rows24, width), wide_type),
+        shape((rows24, 4 * width), wide_type),
+        shape((4 * rows24, width), wide_type),
+        shape((8, width), wide_type),
+        shape((8, width), wide_type),
+    )
+    anywhere, near = pl.BlockSpec(memory_space=pl.ANY), pl.BlockSpec(memory_space=pltpu.VMEM)
+    copies = 4 * (4 + 6 + (groups - 1)) + 3
+
+    def chunks(parts, sizes):
+        return [pltpu.VMEM(parts + (size, width), low) for size in sizes]
+
+    rest = tuple(size - some for size, some in zip(SIZES, SCATTER_X))
+    scratch = [
+        pltpu.VMEM((4, rows, width), low),
+        pltpu.VMEM((2, rows, width), low),
+        pltpu.VMEM((4, width, width), low),
+        pltpu.VMEM((4, width, width), low),
+        pltpu.VMEM((rows, width), low),
+        pltpu.VMEM((rows, width), wide_type),
+        pltpu.VMEM((rows, width), low),
+        pltpu.VMEM((rows, width), low),
+        pltpu.VMEM((rows, 128), wide_type),
+        pltpu.VMEM((2, width // 2, width), wide_type),
+        pltpu.VMEM((2, count, 2, cap, cap), low),
+        pltpu.VMEM((16, width), wide_type),
+        pltpu.VMEM((2 * count, width), wide_type),
+        pltpu.VMEM((2 * count, width), wide_type),
+        pltpu.VMEM((8, width), wide_type),
+        pltpu.VMEM((8, width), wide_type),
+        *chunks((groups, 8), SIZES),
+        *chunks((4, groups), SIZES),
+        *chunks((2, groups), SCATTER_X),
+        *chunks((2, groups), rest),
+        *chunks((groups,), rest),
+        *chunks((groups,), SCATTER_X),
+        *chunks((groups - 1,), SIZES),
+        pltpu.SemaphoreType.DMA((copies,)),
+        pltpu.SemaphoreType.DMA((copies,)),
+        pltpu.SemaphoreType.DMA((24,)),
+        pltpu.SemaphoreType.DMA((3, rows // 256)),
+        pltpu.SemaphoreType.DMA((2, 2)),
+    ]
+    return pl.pallas_call(
+        backward_kernel,
+        name="backward",
+        out_shape=outs,
+        in_specs=[pl.BlockSpec(memory_space=pltpu.SMEM)] + [near] * 4 + [anywhere] * 15,
+        out_specs=[anywhere] * 4 + [near] * 8,
+        scratch_shapes=scratch,
+        compiler_params=pltpu.CompilerParams(
+            collective_id=1, has_side_effects=True, vmem_limit_bytes=63 * 1024 * 1024
+        ),
+    )(limits, vectors, share, short_pool_cot, long_pool_cot, *arrays)
 
 
 def layer_norm(row_data, gain_vec, shift_vec):
@@ -89,7 +1082,7 @@
     )
 
 
-def shards(
+def general_shards(
     short_tokens,
     long_tokens,
     short_len,
@@ -329,43 +1322,88 @@
     )
 
 
+def fast_shards(
+    short_tokens, long_tokens, short_len, long_len, short_pool, long_pool, short_cot, long_cot,
+    short_pool_cot, long_pool_cot, w_qkv, w_out, w_up, w_down, qv_bias, out_bias, up_bias,
+    norm_gain, norm_shift,
+):
+    groups = lax.axis_size("dp") // 4
+    rows, width = w_out.shape
+    seq = lax.axis_index("seq")
+    device = lax.axis_index("dp") * 2 + seq
+    count, cap, _ = short_tokens.shape
+    half = long_tokens.shape[1]
+    short_rows = count * cap
+
+    pairs = jnp.concatenate([member.T for member in (qv_bias, out_bias, norm_gain, norm_shift)], axis=0)
+    empty = jnp.zeros((8, width), w_out.dtype)
+    lane = lax.rem(device, 8) * (4 * rows)
+    pairs = lax.dynamic_update_slice(empty, pairs, (0, device * rows))
+    ups = lax.dynamic_update_slice(empty, up_bias[None, :], (lax.div(device, 8), lane))
+    slabs = (
+        jnp.concatenate([w_qkv[:, i * width : (i + 1) * width] for i in range(3)] + [pairs], axis=0),
+        jnp.concatenate([w_out, ups], axis=0),
+        jnp.concatenate([w_up[:, i * width : (i + 1) * width] for i in range(4)], axis=0),
+        w_down,
+    )
+    passage_len = lax.dynamic_slice_in_dim(long_len, seq, 1)
+    limits = jnp.concatenate([short_len, passage_len - cap * jnp.arange(2 * half // cap, dtype=jnp.int32)])
+    pool = jnp.pad(long_pool.reshape(2, half // cap, cap), ((0, 0), (0, 8 - half // cap), (0, 0)))
+    (down, *kept, vectors, share) = forward(
+        limits,
+        slabs,
+        short_tokens.reshape(short_rows, width),
+        long_tokens,
+        short_cot.reshape(short_rows, width),
+        long_cot,
+        short_pool,
+        pool,
+        groups,
+    )
+    (
+        short_out, long_out, short_grad, long_grad, short_pooled, long_pooled,
+        grad_qkv, grad_out, grad_up, grad_down, grad_vectors, grad_ups,
+    ) = backward(
+        limits, vectors, share, short_pool_cot, long_pool_cot, (down.reshape(4, width, width), *kept), groups
+    )
+    small = lax.dynamic_slice(grad_vectors, (0, device * rows), (8, rows))
+    return (
+        short_out.reshape(short_tokens.shape),
+        long_out,
+        short_pooled,
+        long_pooled,
+        short_grad.reshape(short_tokens.shape),
+        long_grad,
+        grad_qkv,
+        grad_out,
+        grad_up,
+        grad_down,
+        small[0:2].T,
+        small[2:4].T,
+        lax.dynamic_slice(grad_ups, (lax.div(device, 8), lane), (1, 4 * rows))[0],
+        small[4:6].T,
+        small[6:8].T,
+    )
+
+
 def solution(mesh):
+    short_spec, long_spec, spread = P(("dp", "seq"), None, None), P("dp", "seq", None), P(("dp", "seq"), None)
+    vector, parameters = P(("dp", "seq")), [P(("dp", "seq"), None)] * 6
     in_specs = (
-        P(("dp", "seq"), None, None),
-        P("dp", "seq", None),
-        P(("dp", "seq")),
-        P("dp"),
-        P(("dp", "seq"), None),
-        P("dp", "seq"),
-        P(("dp", "seq"), None, None),
-        P("dp", "seq", None),
-        P(("dp", "seq"), None),
-        P("dp", None),
-        P(("dp", "seq"), None),
-        P(("dp", "seq"), None),
-        P(("dp", "seq"), None),
-        P(("dp", "seq"), None),
-        P(("dp", "seq"), None),
-        P(("dp", "seq"), None),
-        P(("dp", "seq")),
-        P(("dp", "seq"), None),
-        P(("dp", "seq"), None),
+        short_spec, long_spec, vector, P("dp"), spread, P("dp", "seq"), short_spec, long_spec,
+        spread, P("dp", None), *parameters, vector, spread, spread,
     )
     out_specs = (
-        P(("dp", "seq"), None, None),
-        P("dp", "seq", None),
-        P(("dp", "seq"), None),
-        P("dp", None),
-        P(("dp", "seq"), None, None),
-        P("dp", "seq", None),
-        P(("dp", "seq"), None),
-        P(("dp", "seq"), None),
-        P(("dp", "seq"), None),
-        P(("dp", "seq"), None),
-        P(("dp", "seq"), None),
-        P(("dp", "seq"), None),
-        P(("dp", "seq")),
-        P(("dp", "seq"), None),
-        P(("dp", "seq"), None),
-    )
-    return jax.shard_map(shards, mesh=mesh, in_specs=in_specs, out_specs=out_specs, check_vma=False)
+        short_spec, long_spec, spread, P("dp", None), short_spec, long_spec, *parameters, vector,
+        spread, spread,
+    )
+    dp, seq = mesh.shape["dp"], mesh.shape["seq"]
+
+    def run(*arrays):
+        width = arrays[11].shape[1]
+        passages = arrays[1].shape[0] // dp
+        regular = dp == 16 and seq == 2 and passages == 2 and width == 24 * dp * seq
+        body = fast_shards if regular else general_shards
+        return jax.shard_map(body, mesh=mesh, in_specs=in_specs, out_specs=out_specs, check_vma=False)(*arrays)
+
+    return run

time: 1120 us -> 259 us (0.23)
  waiting for transfers between devices: 487 us -> 0 us
  blocking collectives: 340 us -> 0 us
  Pallas kernels: 0 us -> 235 us
  matrix products: 179 us -> 0 us
  local copies, waits for them, and re-layouts: 60.9 us -> 17.9 us
  other arithmetic: 32.8 us -> 5.33 us
  between operations: 15.5 us -> 0.74 us
    reduce_scatter x6 -> x0, waiting for transfers between devices: 418 us -> none  [the longest x1 142 us: shards(): lax.psum_scatter(grad_up, ('dp', 'seq'), scatter_dimension=0, tiled=True)]
    all_gather x4 -> x0, blocking collectives: 260 us -> none  [the longest x1 65.8 us: shards(): lax.all_gather(qv_bias, ('dp', 'seq'), axis=0, tiled=True)]
    pallas_call x0 -> x2, Pallas kernels: none -> 235 us  [the longest x1 127 us: backward(): pl.pallas_call(backward_kernel, name='backward', out_shape=outs, in_specs...]
    dot_general x24 -> x0, matrix products: 179 us -> none  [the longest x4 41.5 us: outer_sum(): lax.dot_general(left_rows, right_rows, (((0,), (0,)), ((), ())), preferre...]
    unnamed x2 -> x0, blocking collectives: 75.4 us -> none
    all_gather x6 -> x0, waiting for transfers between devices: 65.9 us -> none  [the longest x1 65.9 us: shards(): lax.all_gather(w_qkv, ('dp', 'seq'), axis=0, tiled=True)]
    reduce_sum x17 -> x0, other arithmetic: 18.5 us -> none  [the longest x4 5.74 us: layer_norm(): return center * lax.rsqrt(spread + EPS) * gain_vec + shift_vec]
    slice x12 -> x2, local copies, waits for them, and re-layouts: 13.9 us -> 1.65 us  [the longest x1 0.83 us: fast_shards(): w_up[:, i * width:(i + 1) * width]]
  transfers between devices with their start and end apart: 12 -> 0, of which waited for: 5 -> 0; matrix products, arithmetic and copies ran while one was open for 16% -> 0% of each run, Pallas kernels for 0% -> 0%
where the time goes in v2:
time: 259 us
  Pallas kernels  235 us (91%)
  local copies, waits for them, and re-layouts  17.9 us (7%)
  other arithmetic  5.33 us (2%)
    pallas_call x1, Pallas kernels, backward(): pl.pallas_call(backward_kernel, name='backward', out_shape=outs, in_specs...  127 us
    pallas_call x1, Pallas kernels, forward(): pl.pallas_call(forward_kernel, name='forward', out_shape=outs, in_specs=[...  108 us
    unnamed x28, local copies, waits for them, and re-layouts  10.2 us

profile of v2, /device:TPU:0, one launch (start us, length us, event | category | flops | bytes accessed | tf_op | source)
XLA Modules:
  0.0 258.7 jit_solution(15782485878784071897)
XLA Ops:
  0.7 1.2 dynamic_slice.9
  1.9 0.6 multiply_subtract_fusion
  2.6 1.2 pad_add_fusion.limits
  3.8 0.7 reshape.50
  4.5 0.7 pad_maximum_fusion.3
  5.2 0.6 pad.4.pool
  5.8 0.1 dynamic_update_slice.6
  5.9 0.8 dynamic_update_slice.7
  6.7 1.4 pad_maximum_fusion.2.slab1
  8.1 0.8 fusion.1
  8.9 0.7 pad_maximum_fusion.1.slab0
  9.6 0.8 fusion
  10.4 0.7 pad_maximum_fusion.slab2
  11.1 108.2 %forward.1 = (bf16[4,8,96,768]{3,2,1,0:T(8,128)(2,1)}, bf16[4,768,768]{2,1,0:T(8,128)(2,1)}, bf16[4,768,768]{2,1,0:T(8,128)(2,1)}, bf16[1024,768]{1,0:T(8,128)(2...) custom-call(s32[8]{0:T(128)} %pad_add_fusion.limits, ...), custom_call_target="tpu_custom_call" | custom-call | tf_op jit(solution)/shard_map/forward/pallas_call | solution.py:557
  119.3 126.6 %backward.1 = (bf16[512,768]{1,0:T(8,128)(2,1)}, bf16[2,256,768]{2,1,0:T(8,128)(2,1)}, f32[512,768]{1,0:T(8,128)}, f32[2,256,768]{2,1,0:T(8,128)}, f32[4,768]{1,...) custom-call(s32[8]{0:T(128)} %pad_add_fusion.limits, ...), custom_call_target="tpu_custom_call" | custom-call | tf_op jit(solution)/shard_map/backward/pallas_call | solution.py:994
  245.9 0.0 copy-start.2
  245.9 1.4 dynamic-slice_bitcast_fusion
  247.2 0.8 constant_dynamic-slice_fusion
  248.0 0.6 slice_bitcast_fusion
  248.6 2.2 copy.46
  250.8 0.9 copy.47
  251.6 0.6 copy.48
  252.2 0.6 copy.49
  252.8 1.1 copy.50
  254.0 0.8 copy-done
  254.8 1.1 copy.51
  256.0 0.0 copy-done.5
  256.0 0.7 copy.52
  256.7 0.0 copy-done.6
  256.7 0.6 copy.53
  257.3 0.7 copy.54
  258.0 0.7 copy.55
  (16 shorter events, 0.0 us)
Async XLA Ops:
  245.9 4.9 %copy-start.2 = (bf16[2,256,768]{2,1,0:T(8,128)(2,1)S(1)}, bf16[2,256,768]{2,1,0:T(8,128)(2,1)}, u32[]{:S(2)}) copy-start(bf16[2,256,768]{2,1,0:T(8,128)(2,1)} %get-tuple-element.100) | copy-start | bytes 2359300
  248.6 3.1 %copy-start.7 = (f32[4,768]{1,0:T(4,128)S(1)}, f32[4,768]{1,0:T(4,128)}, u32[]{:S(2)}) copy-start(f32[4,768]{1,0:T(4,128)} %get-tuple-element.101) | copy-start | bytes 36868
  248.6 3.7 %copy-start.8 = (f32[2,768]{1,0:T(2,128)S(1)}, f32[2,768]{1,0:T(2,128)}, u32[]{:S(2)}) copy-start(f32[2,768]{1,0:T(2,128)} %get-tuple-element.102) | copy-start | bytes 18436
  248.6 4.3 %copy-start.1 = (f32[512,768]{1,0:T(8,128)S(1)}, f32[512,768]{1,0:T(8,128)}, u32[]{:S(2)}) copy-start(f32[512,768]{1,0:T(8,128)} %get-tuple-element.65) | copy-start | bytes 4718596
  252.8 2.0 copy-start
  254.8 1.2 copy-start.5
  254.8 1.8 copy-start.6
  254.8 2.5 copy-start.4
  254.8 3.2 %copy-start.3 = (f32[96,768]{1,0:T(8,128)S(1)}, f32[96,768]{1,0:T(8,128)}, u32[]{:S(2)}) copy-start(f32[96,768]{1,0:T(8,128)} %get-tuple-element.108) | copy-start | bytes 884740

commit v3 on v2

--- a/solution.py
+++ b/solution.py
@@ -13,8 +13,9 @@
 MESH = pl.DeviceIdType.MESH
 
 SIZES = (80, 32, 96, 96)
-GATHER_X = (48, 16, 64, 64)
-SCATTER_X = (32, 16, 32, 32)
+GATHER_X = (48, 16, 48, 48)
+SUMS = (80, 80, 80, 32, 96, 96)
+SUMS_X = (32, 32, 32, 16, 32, 32)
 
 
 FLIPS = ((0, 0), (0, 1), (1, 0), (1, 1))
@@ -59,12 +60,14 @@
             self.at_core(),
         ]
 
-    def greet(self):
-        barrier = pltpu.get_barrier_semaphore()
-        partners = self.partners()
-        for partner in partners:
-            pl.semaphore_signal(barrier, inc=1, device_id=partner, device_id_type=MESH)
-        pl.semaphore_wait(barrier, len(partners))
+    def greet_start(self):
+        for partner in self.partners():
+            pl.semaphore_signal(
+                pltpu.get_barrier_semaphore(), inc=1, device_id=partner, device_id_type=MESH
+            )
+
+    def greet_wait(self):
+        pl.semaphore_wait(pltpu.get_barrier_semaphore(), len(self.partners()))
 
 
 class Wires:
@@ -107,8 +110,8 @@
 
 
 class Gather:
-    def __init__(self, wires, place, slabs, wholes):
-        self.wires, self.place, self.slabs, self.wholes = wires, place, slabs, wholes
+    def __init__(self, wires, place, wholes, last):
+        self.wires, self.place, self.wholes, self.last = wires, place, wholes, last
         self.steps = place.groups
         self.along_z, self.along_x, self.along_y = {}, {}, {}
         self.by_x, self.by_y, self.core = {}, {}, {}
@@ -119,10 +122,15 @@
 
     def start(self, k):
         place, wires = self.place, self.wires
-        src = self.slabs[k]
         dst = self.wholes[k].at[place.z, place.slot()]
+        src = self.last if k == 3 else dst
         for step in range(1, self.steps):
             self.along_z[k, step] = wires.put(src, dst, place.at_z(step))
+
+    def start_plane(self, k):
+        place, wires = self.place, self.wires
+        dst = self.wholes[k].at[place.z, place.slot()]
+        src = self.last if k == 3 else dst
         self.along_x[k, 0] = wires.put(src, dst, place.at_x())
         self.along_y[k, 0] = wires.put(src, dst, place.at_y())
         self.core[k, 0, 0] = wires.put(src, dst, place.at_core())
@@ -183,8 +191,8 @@
         self.core, self.first, self.second, self.third = {}, {}, {}, {}
 
     def halves(self, k):
-        some = SCATTER_X[k]
-        return pl.ds(0, some), pl.ds(some, SIZES[k] - some)
+        some = SUMS_X[k]
+        return pl.ds(0, some), pl.ds(some, SUMS[k] - some)
 
     def own(self, k, part, rows):
         flip_y, flip_x = FLIPS[part]
@@ -209,7 +217,7 @@
 
     def after_core(self, k):
         upper, lower = self.halves(k)
-        whole = pl.ds(0, SIZES[k])
+        whole = pl.ds(0, SUMS[k])
         wires, place = self.wires, self.place
         for part in (3, 1, 2, 0):
             wires.landed(self.core[k, part], self.from_core[k].at[part])
@@ -341,25 +349,37 @@
     return (exponent * (1.0 / jnp.sum(exponent, axis=-1, keepdims=True))).astype(jnp.bfloat16)
 
 
+def as_column(row):
+    size = row.shape[1]
+    down = lax.broadcasted_iota(jnp.int32, (size, size), 0)
+    across = lax.broadcasted_iota(jnp.int32, (size, size), 1)
+    return jnp.sum(jnp.where(down == across, row, 0.0), axis=1, keepdims=True)
+
+
+def put_at(row, start, width):
+    size = row.shape[1]
+    down = lax.broadcasted_iota(jnp.int32, (size, width), 0)
+    across = lax.broadcasted_iota(jnp.int32, (size, width), 1)
+    return jnp.sum(jnp.where(across == down + start, as_column(row), 0.0), axis=0, keepdims=True)
+
+
 def forward_kernel(
-    limits, slab0, slab1, slab2, slab3, short_tok, long_tok, short_cot, long_cot, short_pool, pool,
-    out_down, out_wq, out_wu, out_rows, out_cot, out_qkv, out_short_probs, out_long_probs, out_mixed,
+    short_len, long_len, w_qkv, w_out, w_up, w_down, qv_bias, out_bias, gains, shifts, up_bias,
+    short_pool, long_pool, short_tok, long_tok,
+    out_down, out_wq, out_wu, out_rows, out_qkv, out_short_probs, out_long_probs, out_mixed,
     out_first, out_hat, out_scale, out_low, out_acted, out_slope, vectors, share,
     whole0, whole1, whole2, wq, wu, rows_in, qkv, short_probs, long_probs, mixed,
-    first, hat, scale, low, acted, slope, pool_in,
-    send, recv, here,
+    first, hat, scale, low, acted, slope, far_pool,
+    send, recv, here, leave,
 ):
     place = Place()
     x, other = place.x, 1 - place.x
     short_rows, half = short_tok.shape[0], long_tok.shape[1]
     total_rows, width = rows_in.shape
     long_rows = 2 * half
-    cap = short_probs.shape[-1]
-    count = short_rows // cap
+    count, cap = short_pool.shape
     mine = pl.ds(pl.multiple_of(short_rows + x * half, half), half)
     theirs = pl.ds(pl.multiple_of(short_rows + other * half, half), half)
-    slabs = (slab0, slab1, slab2, slab3)
-    wholes = (whole0, whole1, whole2, out_down)
     local = []
 
     def move(src, dst):
@@ -368,39 +388,52 @@
         local.append(copy)
         return copy
 
-    for k in range(4):
-        move(slabs[k], wholes[k].at[place.z, place.slot()])
-    for src, dst in (
-        (short_tok, rows_in.at[pl.ds(0, short_rows)]),
-        (long_tok.at[x], rows_in.at[mine]),
-        (pool.at[x], pool_in.at[x]),
-        (short_cot, out_cot.at[pl.ds(0, short_rows)]),
-        (long_cot.at[x], out_cot.at[mine]),
-    ):
-        move(src, dst)
-    arrived = len(local)
-    place.greet()
+    move(w_down, out_down.at[place.z, place.slot()])
+    loads = [
+        move(short_tok, rows_in.at[pl.ds(0, short_rows)]),
+        move(long_tok.at[x], rows_in.at[mine]),
+    ]
+    place.greet_start()
+
+    device = place.dp * 2 + x
+    size = w_out.shape[0]
+
+    def blocks(matrix):
+        data = matrix[...].astype(jnp.float32)
+        return [data[:, i * width : (i + 1) * width] for i in range(data.shape[1] // width)]
+
+    pairs = [
+        put_at(member[i : i + 1, :].astype(jnp.float32), device * size, width)
+        for member in (qv_bias, out_bias, gains, shifts)
+        for i in range(2)
+    ]
+    ups = put_at(up_bias[...].astype(jnp.float32), lax.rem(device, 8) * (4 * size), width)
+    ups = jnp.where(lax.broadcasted_iota(jnp.int32, (8, 1), 0) == lax.div(device, 8), ups, 0.0)
+    z, slot = place.z, place.slot()
+    whole0[z, slot] = jnp.concatenate(blocks(w_qkv) + pairs, axis=0).astype(jnp.bfloat16)
+    whole1[z, slot] = jnp.concatenate(blocks(w_out) + [ups], axis=0).astype(jnp.bfloat16)
+    whole2[z, slot] = jnp.concatenate(blocks(w_up), axis=0).astype(jnp.bfloat16)
+
+    place.greet_wait()
     wires = Wires(send, recv)
-    net = Gather(wires, place, slabs, wholes)
+    net = Gather(wires, place, (whole0, whole1, whole2, out_down), w_down)
     net.start(0)
+    net.start(1)
+    net.start_plane(2)
+    net.start(2)
+    net.start_plane(1)
+    net.start_plane(0)
+    pooled = wires.put(long_pool, far_pool, place.at_x())
+    net.relay_z(0)
+    net.relay_plane(0)
     tok = wires.put(long_tok.at[other], rows_in.at[mine], place.at_x())
-    pooled = wires.put(pool.at[other], pool_in.at[x], place.at_x())
-    net.start(1)
-    net.relay_z(0)
-    net.start(2)
-    net.relay_plane(0)
+    net.relay_z(1)
     net.relay_corner(0)
-    net.relay_z(1)
-    net.relay_plane(1)
-    net.relay_corner(1)
-    net.start(3)
-    for copy in local:
+    for copy in loads:
         copy.wait()
     net.finish(0)
     assemble(whole0, 0, 3, wq)
     vectors[0:8, :] = sum_slabs(whole0, 72)
-    wires.landed(tok, rows_in.at[theirs])
-    net.relay_z(2)
 
     head_dim = width // HEADS
     score_scale = 1.0 / math.sqrt(head_dim)
@@ -414,44 +447,71 @@
         qkv[2, rows, :] = (times(data, wq[2]) + vectors[1:2, :]).astype(jnp.bfloat16)
         return carry
 
-    lax.fori_loop(0, total_rows // 256, project, 0)
+    lax.fori_loop(0, short_rows // 256, project, 0)
+
+    masks = head_masks(2 * head_dim, head_dim)
+    keep_first = lax.broadcasted_iota(jnp.int32, (1, 2 * head_dim), 1) < head_dim
+    place_in_block = lax.broadcasted_iota(jnp.int32, (1, cap), 1)
+    short_live = [place_in_block < short_len[i] for i in range(count)]
+    passage_len = long_len[x]
+    long_live = lax.broadcasted_iota(jnp.int32, (1, long_rows), 1) < passage_len
+    pairs = width // (2 * head_dim)
+
+    def attend_short(pair, carry):
+        lanes = aligned(pair, 2 * head_dim)
+        blocks_of = [pl.ds(i * cap, cap) for i in range(count)]
+        queries, keys_all, values = [[qkv[b, rows, lanes] for rows in blocks_of] for b in range(3)]
+        units = [(i, h) for i in range(count) for h in range(2)]
+        scores = [times_turned(queries[i] * masks[h], keys_all[i]) for i, h in units]
+        scores = [jnp.where(short_live[i], part, -1e30) for (i, h), part in zip(units, scores)]
+        tops = [jnp.max(part, axis=-1, keepdims=True) for part in scores]
+        exponents = [jnp.exp(part - top) for part, top in zip(scores, tops)]
+        totals = [jnp.sum(part, axis=-1, keepdims=True) for part in exponents]
+        probs = [(part * (1.0 / total)).astype(jnp.bfloat16) for part, total in zip(exponents, totals)]
+        parts = [times(part, values[i]) for (i, h), part in zip(units, probs)]
+        for (i, h), part in zip(units, probs):
+            short_probs[i, 2 * pair + h] = part
+        for i in range(count):
+            mixed[blocks_of[i], lanes] = jnp.where(keep_first, parts[2 * i], parts[2 * i + 1]).astype(jnp.bfloat16)
+        return carry
+
+    lax.fori_loop(0, pairs // 2, attend_short, 0)
+    net.relay_z(2)
+    lax.fori_loop(pairs // 2, pairs - 1, attend_short, 0)
+    net.start(3)
+    net.relay_plane(1)
+    lax.fori_loop(pairs - 1, pairs, attend_short, 0)
+    net.start_plane(3)
+    move(short_probs, out_short_probs)
+    wires.landed(tok, rows_in.at[theirs])
+    lax.fori_loop(short_rows // 256, total_rows // 256, project, 0)
     move(qkv, out_qkv)
     move(rows_in, out_rows)
 
-    wires.landed(pooled, pool_in.at[other])
-    place_in_block = lax.broadcasted_iota(jnp.int32, (1, cap), 1)
+    wires.landed(pooled, far_pool)
     chosen = []
     for block in range(total_rows // cap):
         if block < count:
             mask, start = short_pool[block : block + 1, :], 0
+            limit = short_len[block]
         else:
             step = block - count
-            per_half = half // cap
-            mask, start = pool_in[step // per_half, step % per_half : step % per_half + 1, :], step * cap
-        live = place_in_block < limits[block]
-        keep = live & ((mask > 0) | (place_in_block + start == 0))
+            in_half, start = step % (half // cap) * cap, step * cap
+            at = slice(in_half, in_half + cap)
+            own = jnp.where(x == 0, long_pool[0:1, at], long_pool[1:2, at])
+            far = jnp.where(x == 0, far_pool[0:1, at], far_pool[1:2, at])
+            mask = jnp.where(x == step // (half // cap), own, far)
+            limit = passage_len - start
+        keep = (place_in_block < limit) & ((mask > 0) | (place_in_block + start == 0))
         chosen.append(jnp.where(keep, 1.0, 0.0))
     for block in range(count):
         share[block : block + 1, :] = chosen[block] / jnp.sum(chosen[block], axis=-1, keepdims=True)
     long_total = sum(jnp.sum(row, axis=-1, keepdims=True) for row in chosen[count:])
     for block in range(count, total_rows // cap):
         share[block : block + 1, :] = chosen[block] / long_total
-    masks = head_masks(2 * head_dim, head_dim)
-    keep_first = lax.broadcasted_iota(jnp.int32, (1, 2 * head_dim), 1) < head_dim
-    short_live = [place_in_block < limits[i] for i in range(count)]
-    long_live = lax.broadcasted_iota(jnp.int32, (1, long_rows), 1) < limits[count]
-
-    def attend(pair, carry):
+
+    def attend_long(pair, carry):
         lanes = aligned(pair, 2 * head_dim)
-        for i in range(count):
-            rows = pl.ds(i * cap, cap)
-            queries, keys_all, values = qkv[0, rows, lanes], qkv[1, rows, lanes], qkv[2, rows, lanes]
-            parts = []
-            for h in range(2):
-                probs = weights_forward(queries * masks[h], keys_all, short_live[i])
-                short_probs[i, 2 * pair + h] = probs
-                parts.append(times(probs, values))
-            mixed[rows, lanes] = jnp.where(keep_first, parts[0], parts[1]).astype(jnp.bfloat16)
         rows = pl.ds(short_rows, long_rows)
         keys_all, values = qkv[1, rows, lanes], qkv[2, rows, lanes]
         for block in range(long_rows // 256):
@@ -466,22 +526,18 @@
             mixed[rows, lanes] = jnp.where(keep_first, parts[0], parts[1]).astype(jnp.bfloat16)
         return carry
 
-    pairs = width // (2 * head_dim)
-    lax.fori_loop(0, pairs // 3, attend, 0)
+    lax.fori_loop(0, pairs - 2, attend_long, 0)
     net.relay_plane(2)
-    lax.fori_loop(pairs // 3, 2 * pairs // 3, attend, 0)
-    net.relay_corner(2)
+    net.relay_corner(1)
+    lax.fori_loop(pairs - 2, pairs - 1, attend_long, 0)
     net.relay_z(3)
-    cot = wires.put(long_cot.at[other], out_cot.at[mine], place.at_x())
-    lax.fori_loop(2 * pairs // 3, pairs, attend, 0)
-    move(short_probs, out_short_probs)
+    lax.fori_loop(pairs - 1, pairs, attend_long, 0)
     move(long_probs, out_long_probs)
     move(mixed, out_mixed)
     net.finish(1)
     assemble(whole1, 0, 1, wq.at[pl.ds(3, 1)])
     vectors[8:16, :] = sum_slabs(whole1, 24)
     move(wq, out_wq)
-    net.relay_plane(3)
 
     def attach(i, carry):
         rows = aligned(i, 256)
@@ -499,9 +555,17 @@
     move(low, out_low)
     move(hat, out_hat)
     move(scale, out_scale)
+    net.relay_corner(2)
     net.finish(2)
     assemble(whole2, 0, 4, wu)
     move(wu, out_wu)
+
+    def leaving(i):
+        j, rows = lax.div(i, 4), aligned(lax.rem(i, 4), 256)
+        return (
+            pltpu.make_async_copy(acted.at[j, rows], out_acted.at[j, rows], leave.at[0, i]),
+            pltpu.make_async_copy(slope.at[j, rows], out_slope.at[j, rows], leave.at[1, i]),
+        )
 
     def expand(i, carry):
         j, rows = lax.div(i, 4), aligned(lax.rem(i, 4), 256)
@@ -509,35 +573,41 @@
         value, grad = gelu_and_slope(inner)
         acted[j, rows, :] = value.astype(jnp.bfloat16)
         slope[j, rows, :] = grad.astype(jnp.bfloat16)
+        for copy in leaving(i):
+            copy.start()
         return carry
 
-    lax.fori_loop(0, 8, expand, 0)
+    def left(i, carry):
+        for copy in leaving(i):
+            copy.wait()
+        return carry
+
+    lax.fori_loop(0, 7, expand, 0)
+    net.relay_plane(3)
+    lax.fori_loop(7, 14, expand, 0)
     net.relay_corner(3)
-    lax.fori_loop(8, 16, expand, 0)
-    move(acted, out_acted)
-    move(slope, out_slope)
+    lax.fori_loop(14, 16, expand, 0)
     net.finish(3)
-    wires.landed(cot, out_cot.at[theirs])
     wires.close()
-    for copy in local[arrived:]:
+    lax.fori_loop(0, 16, left, 0)
+    for copy in [local[0]] + local[3:]:
         copy.wait()
 
 
-def forward(limits, slabs, short_tok, long_tok, short_cot, long_cot, short_pool, pool, groups):
+def forward(lengths, parameters, pools, short_tok, long_tok, groups):
     short_rows, width = short_tok.shape
     half = long_tok.shape[1]
     long_rows = 2 * half
     rows = short_rows + long_rows
-    count, cap = short_pool.shape
+    count, cap = pools[0].shape
     inner = 4 * width
-    copies = 4 * ((groups - 1) + 4 * groups + 4 * groups) + 3
+    copies = 4 * ((groups - 1) + 4 * groups + 4 * groups) + 2
     low = jnp.bfloat16
     shape = jax.ShapeDtypeStruct
     outs = (
         shape((groups, 8, SIZES[3], width), low),
         shape((4, width, width), low),
         shape((4, width, width), low),
-        shape((rows, width), low),
         shape((rows, width), low),
         shape((3, rows, width), low),
         shape((count, HEADS, cap, cap), low),
@@ -553,41 +623,44 @@
         shape((rows // cap, cap), jnp.float32),
     )
     anywhere, near = pl.BlockSpec(memory_space=pl.ANY), pl.BlockSpec(memory_space=pltpu.VMEM)
-    kept = [pltpu.VMEM(out.shape, out.dtype) for out in (outs[1:4] + outs[5:15])]
+    scalars = pl.BlockSpec(memory_space=pltpu.SMEM)
+    kept = [pltpu.VMEM(out.shape, out.dtype) for out in outs[1:14]]
     return pl.pallas_call(
         forward_kernel,
         name="forward",
         out_shape=outs,
-        in_specs=[pl.BlockSpec(memory_space=pltpu.SMEM)] + [anywhere] * 8 + [near] + [anywhere],
-        out_specs=[anywhere] * 15 + [near] * 2,
+        in_specs=[scalars] * 2 + [near] * 11 + [anywhere] * 2,
+        out_specs=[anywhere] * 14 + [near] * 2,
         scratch_shapes=[pltpu.VMEM((groups, 8, SIZES[k], width), low) for k in range(3)]
         + kept
         + [
-            pltpu.VMEM(pool.shape, pool.dtype),
+            pltpu.VMEM(pools[1].shape, pools[1].dtype),
             pltpu.SemaphoreType.DMA((copies,)),
             pltpu.SemaphoreType.DMA((copies,)),
             pltpu.SemaphoreType.DMA((24,)),
+            pltpu.SemaphoreType.DMA((2, 16)),
         ],
         compiler_params=pltpu.CompilerParams(
             collective_id=0, has_side_effects=True, vmem_limit_bytes=60 * 1024 * 1024
         ),
-    )(limits, *slabs, short_tok, long_tok, short_cot, long_cot, short_pool, pool)
+    )(*lengths, *parameters, *pools, short_tok, long_tok)
 
 
 def backward_kernel(
-    limits, vectors, share, short_pool_cot, long_pool_cot,
-    in_down, in_wq, in_wu, in_rows, in_cot, in_qkv, in_short_probs, in_long_probs, in_mixed,
+    short_len, long_len, vectors, share, short_pool_cot, long_pool_cot, short_cot, long_cot,
+    in_down, in_wq, in_wu, in_rows, in_qkv, in_short_probs, in_long_probs, in_mixed,
     in_first, in_hat, in_scale, in_low, in_acted, in_slope,
     short_out, long_out, short_grad, long_grad, short_pooled, long_pooled,
     grad_qkv, grad_out, grad_up, grad_down, grad_vectors, grad_up_vector,
     wide, pair, w_up, w_far, hat, sums, branch, low, scale, halves, probs_short,
     vector_sums, pool_cots, pooled_rows, pooled_own, pooled_far,
-    grads0, grads1, grads2, grads3, core0, core1, core2, core3,
-    x0, x1, x2, x3, y0, y1, y2, y3, lx0, lx1, lx2, lx3, ly0, ly1, ly2, ly3, z0, z1, z2, z3,
-    send, recv, here, blocks, fetch,
+    *more,
 ):
     place = Place()
     x, other = place.x, 1 - place.x
+    *chunks, send, recv, here, blocks, fetch = more
+    parts = len(SUMS)
+    grads, *received = [chunks[i * parts : (i + 1) * parts] for i in range(7)]
     total_rows, width = sums.shape
     short_rows = short_out.shape[0]
     count, cap = probs_short.shape[1], probs_short.shape[-1]
@@ -604,32 +677,33 @@
         local.append(copy)
         return copy
 
+    mine = pl.ds(pl.multiple_of(short_rows + x * half, half), half)
+    theirs = pl.ds(pl.multiple_of(short_rows + other * half, half), half)
+    place.greet_start()
     load_down = [move(in_down.at[j], w_far.at[j]) for j in range(4)]
+    load_down += [
+        move(short_cot, branch.at[pl.ds(0, short_rows)]),
+        move(long_cot.at[x], branch.at[mine]),
+    ]
+    passage_len = long_len[x]
 
     def block_copies(i):
         rows = aligned(i, 256)
         return (
             pltpu.make_async_copy(in_acted.at[:, rows], wide.at[:, rows], blocks.at[0, i]),
             pltpu.make_async_copy(in_first.at[rows], sums.at[rows], blocks.at[1, i]),
-            pltpu.make_async_copy(in_cot.at[rows], branch.at[rows], blocks.at[2, i]),
         )
 
     for i in range(steps):
         for copy in block_copies(i):
             copy.start()
-    load_slope = [move(in_slope.at[0], pair.at[0])]
-    load_low = move(in_low, low)
-    load_up = move(in_wu, w_up)
-    load_hat, load_scale = move(in_hat, hat), move(in_scale, scale)
     vector_sums[...] = jnp.zeros_like(vector_sums)
     pool_cots[0:count, :] = short_pool_cot[...]
     pool_cots[count : 2 * count, :] = jnp.broadcast_to(long_pool_cot[pl.ds(x, 1), :], (count, width))
-    place.greet()
+    place.greet_wait()
     wires = Wires(send, recv)
-    net = Scatter(
-        wires, place, (grads0, grads1, grads2, grads3), (core0, core1, core2, core3),
-        (x0, x1, x2, x3), (y0, y1, y2, y3), (lx0, lx1, lx2, lx3), (ly0, ly1, ly2, ly3), (z0, z1, z2, z3),
-    )
+    swap_cot = wires.put(long_cot.at[other], branch.at[mine], place.at_x())
+    net = Scatter(wires, place, grads, *received)
     for copy in load_down:
         copy.wait()
     tall = lax.broadcasted_iota(jnp.int32, (256, 1), 0)
@@ -638,7 +712,13 @@
     def add_vector(row, rows):
         vector_sums[row : row + 1, :] += jnp.sum(rows, axis=0, keepdims=True)
 
-    def second(i, carry):
+    def second(step, carry):
+        i = jnp.where(step < 2, step, 2 + lax.rem(step + x, 2))
+
+        @pl.when(step == steps - 1)
+        def _():
+            wires.landed(swap_cot, branch.at[theirs])
+
         rows = aligned(i, 256)
         for copy in block_copies(i):
             copy.wait()
@@ -646,9 +726,13 @@
         for j in range(1, 4):
             product += times(wide[j, rows, :], w_far[j])
         normal, factor = normalize(sums[rows, :] + (product + vectors[3:4, :]))
-        live = tall < jnp.where(tall < cap, limits[2 * i], limits[2 * i + 1] + cap)
+        lens = [
+            jnp.where(2 * i + part < count, short_len[lax.rem(2 * i + part, count)], passage_len - (2 * i + part - count) * cap)
+            for part in range(2)
+        ]
+        live = tall < jnp.where(tall < cap, lens[0], lens[1] + cap)
         final = jnp.where(live, normal * vectors[5:6, :] + vectors[7:8, :], 0.0)
-        pair[1, rows, :] = final.astype(low_type)
+        low[rows, :] = final.astype(low_type)
         spread = []
         for part in range(2):
             share_row = share[pl.ds(2 * i + part, 1), :]
@@ -674,22 +758,23 @@
     own_pooled = jnp.sum(pooled_rows[count : 2 * count, :], axis=0, keepdims=True)
     pooled_own[...] = jnp.broadcast_to(own_pooled, pooled_own.shape)
     long_pooled[pl.ds(x, 1), :] = own_pooled
-    mine = pl.ds(pl.multiple_of(short_rows + x * half, half), half)
-    theirs = pl.ds(pl.multiple_of(short_rows + other * half, half), half)
     out_copies = [
-        move(pair.at[1, pl.ds(0, short_rows)], short_out),
-        move(pair.at[1, mine], long_out.at[x]),
+        move(low.at[pl.ds(0, short_rows)], short_out),
+        move(low.at[mine], long_out.at[x]),
     ]
+    load_slope = [move(in_slope.at[0], pair.at[0]), move(in_slope.at[1], pair.at[1])]
+    load_up = move(in_wu, w_up)
+    load_hat, load_scale = move(in_hat, hat), move(in_scale, scale)
 
     def down_step(i, carry):
         j, part = lax.div(i, 2), lax.rem(i, 2)
         product = turned_times(wide[j, :, aligned(part, width // 2)], branch[...])
-        grads3[j, aligned(part, 4)] = product.reshape(4, SIZES[3], width).astype(low_type)
+        grads[5][j, aligned(part, 4)] = product.reshape(4, SUMS[5], width).astype(low_type)
         return carry
 
-    lax.fori_loop(0, 8, down_step, 0)
-    net.send_core(3)
-    swap_out = wires.put(pair.at[1, theirs], long_out.at[x], place.at_x())
+    lax.fori_loop(0, 8, down_step, 0, unroll=2)
+    net.send_core(5)
+    swap_out = wires.put(low.at[theirs], long_out.at[x], place.at_x())
     swap_pooled = wires.put(pooled_own, pooled_far, place.at_x())
 
     def inner_block(j):
@@ -701,19 +786,19 @@
             add_vector(8 + j, grad_inner.astype(jnp.float32))
             return carry
 
-        lax.fori_loop(0, steps, inner, 0)
+        lax.fori_loop(0, steps, inner, 0, unroll=2)
 
     load_slope[0].wait()
     inner_block(0)
-    for copy in out_copies:
-        copy.wait()
-    wires.has_left(swap_out)
-    load_slope.append(move(in_slope.at[1], pair.at[1]))
     load_slope.append(move(in_slope.at[2], pair.at[0]))
     load_slope[1].wait()
     inner_block(1)
     load_slope.append(move(in_slope.at[3], pair.at[1]))
-    net.after_core(3)
+    for copy in out_copies:
+        copy.wait()
+    wires.has_left(swap_out)
+    load_low = move(in_low, low)
+    net.after_core(5)
     load_slope[2].wait()
     inner_block(2)
     load_mixed = move(in_mixed, pair.at[0])
@@ -721,16 +806,6 @@
     inner_block(3)
     load_wq = move(in_wq, w_far)
 
-    def pack(target, first, r, tail):
-        def one(i, carry):
-            rows = pl.ds(pl.multiple_of(i * 24, 8), 24)
-            pieces = [halves[0, rows, :], halves[1, rows, :]] if tail is None else [halves[0, rows, :], tail]
-            data = jnp.concatenate(pieces, axis=0).astype(low_type)
-            target[2 * r + lax.div(i, 8), lax.rem(i, 8), first : first + data.shape[0], :] = data
-            return carry
-
-        lax.fori_loop(0, 16, one, 0)
-
     def up_step(i, carry):
         r, both = lax.div(i, 2), lax.rem(i, 2)
         data = low[:, aligned(r, width // 2)]
@@ -740,14 +815,14 @@
         def one(k, carry):
             rows = pl.ds(pl.multiple_of(k * 24, 8), 24)
             data = jnp.concatenate([halves[0, rows, :], halves[1, rows, :]], axis=0)
-            grads2[2 * r + lax.div(k, 8), lax.rem(k, 8), aligned(both, 48), :] = data.astype(low_type)
+            grads[4][2 * r + lax.div(k, 8), lax.rem(k, 8), aligned(both, 48), :] = data.astype(low_type)
             return carry
 
         return lax.fori_loop(0, 16, one, carry)
 
     load_low.wait()
     lax.fori_loop(0, 4, up_step, 0)
-    net.send_core(2)
+    net.send_core(4)
 
     load_up.wait()
     load_hat.wait()
@@ -771,18 +846,28 @@
         add_vector(2, grad_attn.astype(jnp.float32))
         return carry
 
-    lax.fori_loop(0, steps, first_back, 0)
+    lax.fori_loop(0, steps // 2, first_back, 0)
+    net.after_first(5)
+    lax.fori_loop(steps // 2, steps, first_back, 0)
     load_qkv = move(in_qkv, wide.at[pl.ds(0, 3)])
     load_rows = move(in_rows, wide.at[3])
-    net.after_core(2)
-    net.after_first(3)
+    net.after_core(4)
 
     load_mixed.wait()
     load_wq.wait()
-    for r in range(2):
-        halves[0] = turned_times(pair[0, :, r * (width // 2) : (r + 1) * (width // 2)], branch[...])
-        pack(grads1, 0, r, vector_sums[8:16, :])
-    net.send_core(1)
+    def out_step(r, carry):
+        halves[0] = turned_times(pair[0, :, aligned(r, width // 2)], branch[...])
+
+        def one(k, carry):
+            rows = pl.ds(pl.multiple_of(k * 24, 8), 24)
+            data = jnp.concatenate([halves[0, rows, :], vector_sums[8:16, :]], axis=0)
+            grads[3][2 * r + lax.div(k, 8), lax.rem(k, 8)] = data.astype(low_type)
+            return carry
+
+        return lax.fori_loop(0, 16, one, carry)
+
+    lax.fori_loop(0, 2, out_step, 0)
+    net.send_core(3)
 
     def mixed_back(i, carry):
         rows = aligned(i, 256)
@@ -809,24 +894,33 @@
     masks = head_masks(2 * head_dim, head_dim)
     pairs = width // (2 * head_dim)
 
-    def attend_back(rows, lanes, queries_rows, probs_of, keys_all, values, carry_k, carry_v):
-        queries, grad_mixed = wide[0, queries_rows, lanes], pair[1, queries_rows, lanes]
-        overlap = grad_mixed.astype(jnp.float32) * pair[0, queries_rows, lanes].astype(jnp.float32)
-        grad_queries = None
-        for h in range(2):
-            center = jnp.sum(overlap * masks[h].astype(jnp.float32), axis=-1, keepdims=True)
-            grad_head = grad_mixed * masks[h]
-            probs = probs_of(h)
-            grad_probs = times_turned(grad_head, values)
-            grad_scores = (probs.astype(jnp.float32) * (grad_probs - center)).astype(low_type)
-            part = times(grad_scores, keys_all * masks[h])
-            grad_queries = part if grad_queries is None else grad_queries + part
-            part = turned_times(grad_scores, queries * masks[h])
-            carry_k = part if carry_k is None else carry_k + part
-            part = turned_times(probs, grad_head)
-            carry_v = part if carry_v is None else carry_v + part
-        wide[0, queries_rows, lanes] = (grad_queries * score_scale).astype(low_type)
-        return carry_k, carry_v
+    def attend_back(lanes, units):
+        heads = [(u, h) for u in range(len(units)) for h in range(2)]
+        queries = [wide[0, rows, lanes] for rows, _, _, _ in units]
+        grads_mixed = [pair[1, rows, lanes] for rows, _, _, _ in units]
+        overlaps = [
+            grad.astype(jnp.float32) * pair[0, rows, lanes].astype(jnp.float32)
+            for grad, (rows, _, _, _) in zip(grads_mixed, units)
+        ]
+        centers = [
+            jnp.sum(overlaps[u] * masks[h].astype(jnp.float32), axis=-1, keepdims=True) for u, h in heads
+        ]
+        grads_head = [grads_mixed[u] * masks[h] for u, h in heads]
+        probs = [units[u][1](h) for u, h in heads]
+        grads_probs = [times_turned(grad, units[u][3]) for grad, (u, h) in zip(grads_head, heads)]
+        scores = [
+            (part.astype(jnp.float32) * (grad - center)).astype(low_type)
+            for part, grad, center in zip(probs, grads_probs, centers)
+        ]
+        grads_q = [times(part, units[u][2] * masks[h]) for part, (u, h) in zip(scores, heads)]
+        grads_k = [turned_times(part, queries[u] * masks[h]) for part, (u, h) in zip(scores, heads)]
+        grads_v = [turned_times(part, grad) for part, grad in zip(probs, grads_head)]
+        for u, (rows, _, _, _) in enumerate(units):
+            total = grads_q[2 * u] + grads_q[2 * u + 1]
+            wide[0, rows, lanes] = (total * score_scale).astype(low_type)
+        return [
+            [grads[2 * u] + grads[2 * u + 1] for u in range(len(units))] for grads in (grads_k, grads_v)
+        ]
 
     def attention_back(p, carry):
         slot = lax.rem(p, 2)
@@ -839,54 +933,80 @@
                 copy.start()
 
         lanes = aligned(p, 2 * head_dim)
-        for i in range(count):
-            rows = pl.ds(i * cap, cap)
-            grad_k, grad_v = attend_back(
-                rows, lanes, rows, lambda h, i=i: probs_short[slot, i, h],
-                wide[1, rows, lanes], wide[2, rows, lanes], None, None,
-            )
+        blocks_of = [pl.ds(i * cap, cap) for i in range(count)]
+        units = [
+            (rows, lambda h, i=i: probs_short[slot, i, h], wide[1, rows, lanes], wide[2, rows, lanes])
+            for i, rows in enumerate(blocks_of)
+        ]
+        grads_k, grads_v = attend_back(lanes, units)
+        for rows, grad_k, grad_v in zip(blocks_of, grads_k, grads_v):
             wide[1, rows, lanes] = grad_k.astype(low_type)
             wide[2, rows, lanes] = grad_v.astype(low_type)
         rows = pl.ds(short_rows, long_rows)
         keys_all, values = wide[1, rows, lanes], wide[2, rows, lanes]
-        grad_k, grad_v = None, None
+        total_k, total_v = None, None
         for block in range(long_rows // 256):
             inner = pl.ds(block * 256, 256)
-            grad_k, grad_v = attend_back(
-                rows, lanes, pl.ds(short_rows + block * 256, 256),
+            unit = (
+                pl.ds(short_rows + block * 256, 256),
                 lambda h, inner=inner: w_up[2 * slot + h, inner, 0:long_rows],
-                keys_all, values, grad_k, grad_v,
+                keys_all,
+                values,
             )
-        wide[1, rows, lanes] = grad_k.astype(low_type)
-        wide[2, rows, lanes] = grad_v.astype(low_type)
+            (grad_k,), (grad_v,) = attend_back(lanes, [unit])
+            total_k = grad_k if total_k is None else total_k + grad_k
+            total_v = grad_v if total_v is None else total_v + grad_v
+        wide[1, rows, lanes] = total_k.astype(low_type)
+        wide[2, rows, lanes] = total_v.astype(low_type)
         return carry
 
+    third = width // 3
+
+    def qkv_step(group):
+        lanes = pl.ds(group * third, third)
+
+        def bias(i, carry):
+            rows = aligned(i, 256)
+            for row, b in ((0, 0), (1, 2)):
+                piece = wide[b, rows, lanes].astype(jnp.float32)
+                vector_sums[row : row + 1, lanes] += jnp.sum(piece, axis=0, keepdims=True)
+            return carry
+
+        lax.fori_loop(0, steps, bias, 0)
+
+        def step(r, carry):
+            data = wide[3, :, aligned(r, width // 2)]
+            for b in range(3):
+                halves[0, :, b * third : (b + 1) * third] = turned_times(data, wide[b, :, lanes])
+
+            def one(k, carry):
+                rows = pl.ds(pl.multiple_of(k * 24, 8), 24)
+                pieces = [halves[0, rows, b * third : (b + 1) * third] for b in range(3)]
+                data = jnp.concatenate(pieces + [vector_sums[0:8, lanes]], axis=0)
+                grads[group][2 * r + lax.div(k, 8), lax.rem(k, 8)] = data.astype(low_type)
+                return carry
+
+            return lax.fori_loop(0, 16, one, carry)
+
+        lax.fori_loop(0, 2, step, 0)
+        net.send_core(group)
+
     lax.fori_loop(0, pairs // 3, attention_back, 0)
+    load_rows.wait()
+    qkv_step(0)
+    net.after_core(3)
+    net.after_second(5)
+    net.after_first(4)
+    lax.fori_loop(pairs // 3, 2 * pairs // 3, attention_back, 0)
+    qkv_step(1)
+    net.after_core(0)
+    net.after_first(3)
+    net.after_second(4)
+    lax.fori_loop(2 * pairs // 3, pairs, attention_back, 0)
+    qkv_step(2)
+    net.after_core(1)
+    net.after_first(0)
     net.after_second(3)
-    net.after_core(1)
-    lax.fori_loop(pairs // 3, 2 * pairs // 3, attention_back, 0)
-    net.after_first(2)
-    lax.fori_loop(2 * pairs // 3, pairs, attention_back, 0)
-    net.after_first(1)
-    net.after_second(2)
-
-    def bias_sums(i, carry):
-        rows = aligned(i, 256)
-        add_vector(0, wide[0, rows, :].astype(jnp.float32))
-        add_vector(1, wide[2, rows, :].astype(jnp.float32))
-        return carry
-
-    lax.fori_loop(0, steps, bias_sums, 0)
-    load_rows.wait()
-    for r in range(2):
-        data = wide[3, :, r * (width // 2) : (r + 1) * (width // 2)]
-        halves[0] = turned_times(data, wide[0])
-        halves[1] = turned_times(data, wide[1])
-        pack(grads0, 0, r, None)
-        halves[0] = turned_times(data, wide[2])
-        pack(grads0, 48, r, vector_sums[0:8, :])
-    net.send_core(0)
-    net.after_second(1)
 
     def tokens_back(rows):
         grad_in = sums[rows, :]
@@ -897,7 +1017,9 @@
     far_low, far_in = low.at[pl.ds(0, half)], low.at[pl.ds(half, half)]
     far_low[...] = tokens_back(theirs).astype(low_type)
     swap_grad = wires.put(far_low, far_in, place.at_x())
-    net.after_core(0)
+    net.after_core(2)
+    net.after_first(1)
+    net.after_second(0)
 
     def tokens_step(i, carry):
         rows = pl.ds(pl.multiple_of(jnp.where(i < 2, i * 256, short_rows + x * half), 256), 256)
@@ -907,12 +1029,13 @@
     lax.fori_loop(0, 3, tokens_step, 0)
     move(sums.at[pl.ds(0, short_rows)], short_grad)
     move(sums.at[mine], long_grad.at[x])
-    net.after_first(0)
-    grad_down[...] = net.finish(3)
-    total = net.finish(2)
+    net.after_first(2)
+    net.after_second(1)
+    grad_down[...] = net.finish(5)
+    total = net.finish(4)
     for j in range(4):
         grad_up[:, j * width : (j + 1) * width] = total[24 * j : 24 * j + 24]
-    total = net.finish(1)
+    total = net.finish(3)
     grad_out[...] = total[0:24]
     grad_up_vector[...] = total[24:32]
     wires.landed(swap_pooled, pooled_far)
@@ -921,20 +1044,22 @@
     sums[theirs, :] = far_in[...].astype(jnp.float32)
     move(sums.at[theirs], long_grad.at[other])
     wires.landed(swap_out, long_out.at[other])
-    net.after_second(0)
-    total = net.finish(0)
-    for b in range(3):
-        grad_qkv[:, b * width : (b + 1) * width] = total[24 * b : 24 * b + 24]
-    grad_vectors[...] = total[72:80]
+    net.after_second(2)
+    for group in range(3):
+        total = net.finish(group)
+        for b in range(3):
+            columns = slice(b * width + group * third, b * width + (group + 1) * third)
+            grad_qkv[:, columns] = total[24 * b : 24 * b + 24]
+        grad_vectors[:, group * third : (group + 1) * third] = total[72:80]
     wires.close()
     for copy in local[-3:]:
         copy.wait()
 
 
-def backward(limits, vectors, share, short_pool_cot, long_pool_cot, arrays, groups):
+def backward(lengths, vectors, share, pool_cots, cots, arrays, groups):
     width = vectors.shape[1]
     rows = arrays[3].shape[0]
-    count, _, cap, _ = arrays[6].shape
+    count, _, cap, _ = arrays[5].shape
     short_rows = count * cap
     half = (rows - short_rows) // 2
     low, wide_type = jnp.bfloat16, jnp.float32
@@ -955,12 +1080,14 @@
         shape((8, width), wide_type),
     )
     anywhere, near = pl.BlockSpec(memory_space=pl.ANY), pl.BlockSpec(memory_space=pltpu.VMEM)
-    copies = 4 * (4 + 6 + (groups - 1)) + 3
+    copies = len(SUMS) * (4 + 6 + (groups - 1)) + 4
+
+    widths = (width // 3,) * 3 + (width,) * 3
 
     def chunks(parts, sizes):
-        return [pltpu.VMEM(parts + (size, width), low) for size in sizes]
-
-    rest = tuple(size - some for size, some in zip(SIZES, SCATTER_X))
+        return [pltpu.VMEM(parts + (size, columns), low) for size, columns in zip(sizes, widths)]
+
+    rest = tuple(size - some for size, some in zip(SUMS, SUMS_X))
     scratch = [
         pltpu.VMEM((4, rows, width), low),
         pltpu.VMEM((2, rows, width), low),
@@ -978,30 +1105,77 @@
         pltpu.VMEM((2 * count, width), wide_type),
         pltpu.VMEM((8, width), wide_type),
         pltpu.VMEM((8, width), wide_type),
-        *chunks((groups, 8), SIZES),
-        *chunks((4, groups), SIZES),
-        *chunks((2, groups), SCATTER_X),
+        *chunks((groups, 8), SUMS),
+        *chunks((4, groups), SUMS),
+        *chunks((2, groups), SUMS_X),
         *chunks((2, groups), rest),
         *chunks((groups,), rest),
-        *chunks((groups,), SCATTER_X),
-        *chunks((groups - 1,), SIZES),
+        *chunks((groups,), SUMS_X),
+        *chunks((groups - 1,), SUMS),
         pltpu.SemaphoreType.DMA((copies,)),
         pltpu.SemaphoreType.DMA((copies,)),
         pltpu.SemaphoreType.DMA((24,)),
-        pltpu.SemaphoreType.DMA((3, rows // 256)),
+        pltpu.SemaphoreType.DMA((2, rows // 256)),
         pltpu.SemaphoreType.DMA((2, 2)),
     ]
     return pl.pallas_call(
         backward_kernel,
         name="backward",
         out_shape=outs,
-        in_specs=[pl.BlockSpec(memory_space=pltpu.SMEM)] + [near] * 4 + [anywhere] * 15,
+        in_specs=[pl.BlockSpec(memory_space=pltpu.SMEM)] * 2 + [near] * 4 + [anywhere] * 16,
         out_specs=[anywhere] * 4 + [near] * 8,
         scratch_shapes=scratch,
         compiler_params=pltpu.CompilerParams(
             collective_id=1, has_side_effects=True, vmem_limit_bytes=63 * 1024 * 1024
         ),
-    )(limits, vectors, share, short_pool_cot, long_pool_cot, *arrays)
+    )(*lengths, vectors, share, *pool_cots, *cots, *arrays)
+
+
+def results_kernel(
+    in_0, in_1, in_2, in_3, in_4, in_5, in_6, in_7, in_8, in_9, grad_vectors, grad_ups,
+    out_0, out_1, out_2, out_3, out_4, out_5, out_6, out_7, out_8, out_9, pair_0, pair_1, ups, pair_2, pair_3,
+    *more,
+):
+    *held, come, leave = more
+    sources = (in_0, in_1, in_2, in_3, in_4, in_5, in_6, in_7, in_8, in_9)
+    places = (out_0, out_1, out_4, out_5, out_2, out_3, out_6, out_7, out_8, out_9)
+    ins = [pltpu.make_async_copy(sources[i], held[i], come.at[i]) for i in range(10)]
+    outs = [pltpu.make_async_copy(held[i], places[i], leave.at[i]) for i in range(10)]
+    for copy in ins:
+        copy.start()
+    device = lax.axis_index("dp") * 2 + lax.axis_index("seq")
+    size, width = in_7.shape
+    rows = pltpu.roll(grad_vectors[...], lax.rem(width - device * size, width), 1)
+    for i, ref in enumerate((pair_0, pair_1, pair_2, pair_3)):
+        ref[...] = rows[2 * i : 2 * i + 2, 0:size]
+    start = lax.rem(device, 8) * (4 * size)
+    row = grad_ups[pl.ds(lax.div(device, 8), 1), :]
+    row = pltpu.roll(jnp.broadcast_to(row, (8, width)), lax.rem(width - start, width), 1)
+    ups[...] = row[0:1, 0 : 4 * size]
+    for i in range(10):
+        ins[i].wait()
+        outs[i].start()
+    for copy in outs:
+        copy.wait()
+
+
+def results(arrays):
+    size = arrays[7].shape[0]
+    order = (0, 1, 4, 5, 2, 3, 6, 7, 8, 9)
+    shape = jax.ShapeDtypeStruct
+    pair = shape((2, size), jnp.float32)
+    outs = tuple(shape(arrays[i].shape, arrays[i].dtype) for i in order)
+    anywhere, near = pl.BlockSpec(memory_space=pl.ANY), pl.BlockSpec(memory_space=pltpu.VMEM)
+    return pl.pallas_call(
+        results_kernel,
+        name="results",
+        out_shape=outs + (pair, pair, shape((1, 4 * size), jnp.float32), pair, pair),
+        in_specs=[anywhere] * 10 + [near] * 2,
+        out_specs=[anywhere] * 10 + [near] * 5,
+        scratch_shapes=[pltpu.VMEM(array.shape, array.dtype) for array in arrays[:10]]
+        + [pltpu.SemaphoreType.DMA((10,)), pltpu.SemaphoreType.DMA((10,))],
+        compiler_params=pltpu.CompilerParams(vmem_limit_bytes=56 * 1024 * 1024),
+    )(*arrays)
 
 
 def layer_norm(row_data, gain_vec, shift_vec):
@@ -1328,61 +1502,38 @@
     norm_gain, norm_shift,
 ):
     groups = lax.axis_size("dp") // 4
-    rows, width = w_out.shape
-    seq = lax.axis_index("seq")
-    device = lax.axis_index("dp") * 2 + seq
+    width = w_out.shape[1]
     count, cap, _ = short_tokens.shape
-    half = long_tokens.shape[1]
     short_rows = count * cap
-
-    pairs = jnp.concatenate([member.T for member in (qv_bias, out_bias, norm_gain, norm_shift)], axis=0)
-    empty = jnp.zeros((8, width), w_out.dtype)
-    lane = lax.rem(device, 8) * (4 * rows)
-    pairs = lax.dynamic_update_slice(empty, pairs, (0, device * rows))
-    ups = lax.dynamic_update_slice(empty, up_bias[None, :], (lax.div(device, 8), lane))
-    slabs = (
-        jnp.concatenate([w_qkv[:, i * width : (i + 1) * width] for i in range(3)] + [pairs], axis=0),
-        jnp.concatenate([w_out, ups], axis=0),
-        jnp.concatenate([w_up[:, i * width : (i + 1) * width] for i in range(4)], axis=0),
-        w_down,
-    )
-    passage_len = lax.dynamic_slice_in_dim(long_len, seq, 1)
-    limits = jnp.concatenate([short_len, passage_len - cap * jnp.arange(2 * half // cap, dtype=jnp.int32)])
-    pool = jnp.pad(long_pool.reshape(2, half // cap, cap), ((0, 0), (0, 8 - half // cap), (0, 0)))
+    lengths = (short_len, long_len)
+    parameters = (
+        w_qkv, w_out, w_up, w_down, qv_bias.T, out_bias.T, norm_gain.T, norm_shift.T, up_bias[None, :],
+    )
     (down, *kept, vectors, share) = forward(
-        limits,
-        slabs,
+        lengths,
+        parameters,
+        (short_pool, long_pool),
         short_tokens.reshape(short_rows, width),
         long_tokens,
-        short_cot.reshape(short_rows, width),
-        long_cot,
-        short_pool,
-        pool,
         groups,
     )
+    arrays = backward(
+        lengths,
+        vectors,
+        share,
+        (short_pool_cot, long_pool_cot),
+        (short_cot.reshape(short_rows, width), long_cot),
+        (down.reshape(4, width, width), *kept),
+        groups,
+    )
     (
-        short_out, long_out, short_grad, long_grad, short_pooled, long_pooled,
-        grad_qkv, grad_out, grad_up, grad_down, grad_vectors, grad_ups,
-    ) = backward(
-        limits, vectors, share, short_pool_cot, long_pool_cot, (down.reshape(4, width, width), *kept), groups
-    )
-    small = lax.dynamic_slice(grad_vectors, (0, device * rows), (8, rows))
+        short_out, long_out, short_pooled, long_pooled, short_grad, long_grad,
+        grad_qkv, grad_out, grad_up, grad_down, qv, out, ups, gain, shift,
+    ) = results(arrays)
     return (
-        short_out.reshape(short_tokens.shape),
-        long_out,
-        short_pooled,
-        long_pooled,
-        short_grad.reshape(short_tokens.shape),
-        long_grad,
-        grad_qkv,
-        grad_out,
-        grad_up,
-        grad_down,
-        small[0:2].T,
-        small[2:4].T,
-        lax.dynamic_slice(grad_ups, (lax.div(device, 8), lane), (1, 4 * rows))[0],
-        small[4:6].T,
-        small[6:8].T,
+        short_out.reshape(short_tokens.shape), long_out, short_pooled, long_pooled,
+        short_grad.reshape(short_tokens.shape), long_grad, grad_qkv, grad_out, grad_up, grad_down,
+        qv.T, out.T, ups[0], gain.T, shift.T,
     )
 
 

time: 259 us -> 211 us (0.81)
  Pallas kernels: 235 us -> 210 us
  local copies, waits for them, and re-layouts: 17.9 us -> 0 us
  other arithmetic: 5.33 us -> 0 us
    pallas_call x1, Pallas kernels: 108 us -> 83.8 us  [forward(): pl.pallas_call(forward_kernel, name='forward', out_shape=outs, in_specs=[...]
    unnamed x28 -> x0, local copies, waits for them, and re-layouts: 10.2 us -> none
    pallas_call x1, Pallas kernels: 127 us -> 120 us  [backward(): pl.pallas_call(backward_kernel, name='backward', out_shape=outs, in_specs...]
    pallas_call x0 -> x1, Pallas kernels: none -> 5.97 us  [results(): pl.pallas_call(results_kernel, name='results', out_shape=outs + (pair, pa...]
    concatenate x5 -> x0, other arithmetic: 4.68 us -> none  [the longest x1 1.39 us: fast_shards(): jnp.concatenate([w_out, ups], axis=0)]
where the time goes in v3:
time: 211 us
  Pallas kernels  210 us (100%)
    pallas_call x1, Pallas kernels, backward(): pl.pallas_call(backward_kernel, name='backward', out_shape=outs, in_specs...  120 us
    pallas_call x1, Pallas kernels, forward(): pl.pallas_call(forward_kernel, name='forward', out_shape=outs, in_specs=[...  83.8 us
    pallas_call x1, Pallas kernels, results(): pl.pallas_call(results_kernel, name='results', out_shape=outs + (pair, pa...  5.97 us

profile of v3, /device:TPU:0, one launch (start us, length us, event | category | flops | bytes accessed | tf_op | source)
XLA Modules:
  0.0 210.6 jit_solution(8118863689760672126)
XLA Ops:
  0.7 83.8 %forward.1 = (bf16[4,8,96,768]{3,2,1,0:T(8,128)(2,1)}, bf16[4,768,768]{2,1,0:T(8,128)(2,1)}, bf16[4,768,768]{2,1,0:T(8,128)(2,1)}, bf16[1024,768]{1,0:T(8,128)(2...) custom-call(s32[4]{0:T(128)} %short_len.3, ...), custom_call_target="tpu_custom_call" | custom-call | tf_op jit(solution)/shard_map/forward/pallas_call | solution.py:628
  84.4 120.0 %backward.1 = (bf16[512,768]{1,0:T(8,128)(2,1)}, bf16[2,256,768]{2,1,0:T(8,128)(2,1)}, f32[512,768]{1,0:T(8,128)}, f32[2,256,768]{2,1,0:T(8,128)}, f32[4,768]{1,...) custom-call(s32[4]{0:T(128)} %short_len.3, ...), custom_call_target="tpu_custom_call" | custom-call | tf_op jit(solution)/shard_map/backward/pallas_call | solution.py:1121
  204.5 6.0 %results.1 = (bf16[512,768]{1,0:T(8,128)(2,1)}, bf16[2,256,768]{2,1,0:T(8,128)(2,1)}, f32[4,768]{1,0:T(4,128)}, f32[2,768]{1,0:T(2,128)}, f32[512,768]{1,0:T(8,1...) custom-call(bf16[512,768]{1,0:T(8,128)(2,1)} %get-tuple-element.74.i, ...), custom_call_target="tpu_custom_call" | custom-call | tf_op jit(solution)/shard_map/results/pallas_call | solution.py:1169
